TPU v7x, 32 devices: a whole 2x2x4 slice. The times are simulated.
32 devices in a mesh: expert: 16 (over z, y, core), shard: 2 (over x).
Axes of the slice: x: 2, y: 2, z: 4, core: 2. Of those that a mesh axis runs over, the one named last changes fastest.
Arguments:
- tokens: bfloat16 [96, 197, 512], P(('expert', 'shard')), may hold values from -6 to 6
- cotangent: bfloat16 [96, 197, 512], P(('expert', 'shard')), may hold values from -6 to 6
- routes: int32 [96, 197, 2], P(('expert', 'shard')), may hold values from 0 to 31, all different within a row; in each aligned block of 591 rows (0 to 590, 591 to 1181, ..., all dimensions but the last counted through in order) at most 40 rows name the same one
- counts: int32 [32], P(('expert', 'shard')), may hold values from 1 to 3, as said below
- aux_weight: float32 [], replicated, may hold values from 605184 to 1210368
- attn_qkv1: bfloat16 [3, 512, 512], P(None, 'shard'), may hold values from -0.25 to 0.25
- attn_out1: bfloat16 [512, 512], P('shard'), may hold values from -3 to 3
- mlp_in: bfloat16 [512, 2048], P('shard'), may hold values from -0.25 to 0.25
- mlp_out: bfloat16 [2048, 512], P('shard'), may hold values from -0.125 to 0.125
- gains1: bfloat16 [2, 512], P(None, 'shard'), may hold values from 0.5 to 1.5
- attn_qkv2: bfloat16 [3, 512, 512], P(None, 'shard'), may hold values from -0.25 to 0.25
- attn_out2: bfloat16 [512, 512], P('shard'), may hold values from -3 to 3
- router: bfloat16 [512, 32], P('shard'), may hold values from -0.25 to 0.25
- gains2: bfloat16 [2, 512], P(None, 'shard'), may hold values from 0.5 to 1.5
- expert_in: bfloat16 [32, 512, 2048], P('expert'), may hold values from -0.25 to 0.25
- expert_out: bfloat16 [32, 2048, 512], P('expert'), as said below
Outputs:
- output: bfloat16 [96, 197, 512], P(('expert', 'shard'))
- balance_loss: float32 [], replicated
- grad_tokens: float32 [96, 197, 512], P(('expert', 'shard'))
- grad_attn_qkv1: float32 [3, 512, 512], P(None, 'shard')
- grad_attn_out1: float32 [512, 512], P('shard')
- grad_mlp_in: float32 [512, 2048], P('shard')
- grad_mlp_out: float32 [2048, 512], P('shard')
- grad_gains1: float32 [2, 512], P(None, 'shard')
- grad_attn_qkv2: float32 [3, 512, 512], P(None, 'shard')
- grad_attn_out2: float32 [512, 512], P('shard')
- grad_router: float32 [512, 32], P('shard')
- grad_gains2: float32 [2, 512], P(None, 'shard')
- grad_expert_in: float32 [32, 512, 2048], P('expert')
- grad_expert_out: float32 [32, 2048, 512], P('expert')
Inputs may be any that keep to these rules, and one draw needn't show every extreme that they name: `counts`: each device holds its images in its first slots, the further slots are padding; some device holds 3 images in every draw. `routes`: each token names two different experts. Among the 591 tokens of one device's slots no expert is named more than 40 times, a bound that some block reaches. `expert_out`: independent entries of mean 0 and standard deviation 40 / sqrt(2048).
All inputs are finite; a program needn't handle non-finite values.
Results may differ from a plain program's by a relative error of at most 0.023.
Values may be sent and summed in bfloat16 or wider, within the bound.
A program may use at most 256 MiB of HBM per device.

v0:
```python
import jax
import jax.numpy as jnp
from jax import lax
from jax.sharding import PartitionSpec as P

HEADS = 8
CAP = 40


EPS = 1e-06


def layer_norm(values, norm_gain):
    average = jnp.mean(values, axis=-1, keepdims=True)
    centered = values - average
    variance = jnp.mean(centered * centered, axis=-1, keepdims=True)
    return centered * lax.rsqrt(variance + EPS) * norm_gain


def gelu_exact(values):
    return jax.nn.gelu(values, approximate=False)


def attend_forward(normed, qkv_weight, out_weight, images):
    row_count, model_width = normed.shape
    score_scale = (model_width // HEADS) ** (-0.5)
    projected = jnp.einsum(
        "nd,cde->cne", normed, qkv_weight, preferred_element_type=jnp.float32
    ).astype(jnp.bfloat16)
    head_vals = projected.reshape(3, images, row_count // images, HEADS, model_width // HEADS)
    scores = (
        jnp.einsum(
            "bqhd,bkhd->bhqk", head_vals[0], head_vals[1], preferred_element_type=jnp.float32
        )
        * score_scale
    )
    peak = jnp.max(scores, axis=-1, keepdims=True)
    raised = jnp.exp(scores - peak)
    row_total = jnp.sum(raised, axis=-1, keepdims=True)
    attn_probs = (raised / row_total).astype(jnp.bfloat16)
    logsum = peak + jnp.log(row_total)
    mixture = jnp.einsum(
        "bhqk,bkhd->bqhd", attn_probs, head_vals[2], preferred_element_type=jnp.float32
    )
    mixture = mixture.astype(jnp.bfloat16).reshape(row_count, model_width)
    branch = jnp.dot(mixture, out_weight, preferred_element_type=jnp.float32)
    return (branch, (head_vals, logsum, mixture))


def attend_backward(grad_branch, normed, qkv_weight, out_weight, saved_state):
    head_vals, logsum, mixture = saved_state
    row_count, model_width = normed.shape
    score_scale = (model_width // HEADS) ** (-0.5)
    grad_low = grad_branch.astype(jnp.bfloat16)
    grad_out_w = jnp.einsum("nd,ne->de", mixture, grad_low, preferred_element_type=jnp.float32)
    grad_mixture = jnp.einsum("ne,de->nd", grad_low, out_weight, preferred_element_type=jnp.float32)
    grad_mixture = grad_mixture.astype(jnp.bfloat16).reshape(head_vals.shape[1:])
    scores = (
        jnp.einsum(
            "bqhd,bkhd->bhqk", head_vals[0], head_vals[1], preferred_element_type=jnp.float32
        )
        * score_scale
    )
    attn_probs = jnp.exp(scores - logsum)
    grad_probs = jnp.einsum(
        "bqhd,bkhd->bhqk", grad_mixture, head_vals[2], preferred_element_type=jnp.float32
    )
    grad_value = jnp.einsum(
        "bhqk,bqhd->bkhd",
        attn_probs.astype(jnp.bfloat16),
        grad_mixture,
        preferred_element_type=jnp.float32,
    )
    grad_scores = attn_probs * (
        grad_probs - jnp.sum(attn_probs * grad_probs, axis=-1, keepdims=True)
    )
    grad_scores = grad_scores.astype(jnp.bfloat16)
    grad_query = (
        jnp.einsum("bhqk,bkhd->bqhd", grad_scores, head_vals[1], preferred_element_type=jnp.float32)
        * score_scale
    )
    grad_key = (
        jnp.einsum("bhqk,bqhd->bkhd", grad_scores, head_vals[0], preferred_element_type=jnp.float32)
        * score_scale
    )
    grad_proj = (
        jnp.stack([grad_query, grad_key, grad_value])
        .astype(jnp.bfloat16)
        .reshape(3, row_count, model_width)
    )
    grad_qkv = jnp.einsum("nd,cne->cde", normed, grad_proj, preferred_element_type=jnp.float32)
    grad_normed = jnp.einsum(
        "cne,cde->nd", grad_proj, qkv_weight, preferred_element_type=jnp.float32
    )
    return (grad_normed, grad_qkv, grad_out_w)


def serve_rows(received, expert_in, expert_out):
    preact = jnp.einsum("slcd,ldf->slcf", received, expert_in, preferred_element_type=jnp.float32)
    activation = gelu_exact(preact).astype(jnp.bfloat16)
    result = jnp.einsum(
        "slcf,lfd->slcd", activation, expert_out, preferred_element_type=jnp.float32
    ).astype(jnp.bfloat16)
    returned = lax.all_to_all(result, "expert", split_axis=0, concat_axis=0, tiled=True)
    return (returned, received, preact)


def per_device(
    tokens,
    cotangent,
    routes,
    counts,
    aux_weight,
    attn_qkv1,
    attn_out1,
    mlp_in,
    mlp_out,
    gains1,
    attn_qkv2,
    attn_out2,
    router,
    gains2,
    expert_in,
    expert_out,
):
    slot_count, seq_len, model_width = tokens.shape
    row_count = slot_count * seq_len
    experts = router.shape[1]
    local_experts = expert_in.shape[0]
    owners = experts // local_experts
    capacity = CAP
    qkv_one, out_one, w_up, w_down, gain_one, qkv_two, out_two, route_w, gain_two = (
        lax.all_gather(attn_qkv1, "shard", axis=1, tiled=True),
        lax.all_gather(attn_out1, "shard", axis=0, tiled=True),
        lax.all_gather(mlp_in, "shard", axis=0, tiled=True),
        lax.all_gather(mlp_out, "shard", axis=0, tiled=True),
        lax.all_gather(gains1, "shard", axis=1, tiled=True),
        lax.all_gather(attn_qkv2, "shard", axis=1, tiled=True),
        lax.all_gather(attn_out2, "shard", axis=0, tiled=True),
        lax.all_gather(router, "shard", axis=0, tiled=True),
        lax.all_gather(gains2, "shard", axis=1, tiled=True),
    )
    live_images = jnp.arange(slot_count, dtype=jnp.int32) < counts[0]
    live_rows = jnp.repeat(live_images.astype(jnp.float32), seq_len)
    live_pairs = jnp.repeat(live_images, seq_len * 2)
    inputs = tokens.astype(jnp.float32).reshape(row_count, model_width)
    normed_one, pull_one = jax.vjp(layer_norm, inputs, gain_one[0].astype(jnp.float32))
    normed_one = normed_one.astype(jnp.bfloat16)
    branch_one, saved_one = attend_forward(normed_one, qkv_one, out_one, slot_count)
    hidden = inputs + branch_one
    normed_two, pull_two = jax.vjp(layer_norm, hidden, gain_one[1].astype(jnp.float32))
    normed_two = normed_two.astype(jnp.bfloat16)
    mlp_pre = jnp.dot(normed_two, w_up, preferred_element_type=jnp.float32)
    mlp_act = gelu_exact(mlp_pre).astype(jnp.bfloat16)
    block_out = hidden + jnp.dot(mlp_act, w_down, preferred_element_type=jnp.float32)
    normed_three, pull_three = jax.vjp(layer_norm, block_out, gain_two[0].astype(jnp.float32))
    normed_three = normed_three.astype(jnp.bfloat16)
    branch_three, saved_three = attend_forward(normed_three, qkv_two, out_two, slot_count)
    hidden_two = block_out + branch_three
    normed_four, pull_four = jax.vjp(layer_norm, hidden_two, gain_two[1].astype(jnp.float32))
    normed_four = normed_four.astype(jnp.bfloat16)
    logits = jnp.dot(normed_four, route_w, preferred_element_type=jnp.float32)
    router_probs = jax.nn.softmax(logits, axis=-1)
    chosen = routes.reshape(row_count * 2)
    onehot = (
        (chosen[:, None] == jnp.arange(experts, dtype=jnp.int32)[None, :]) & live_pairs[:, None]
    ).astype(jnp.int32)
    position = jnp.sum((jnp.cumsum(onehot, axis=0) - onehot) * onehot, axis=1)
    slot_index = jnp.where(live_pairs, chosen * capacity + position, experts * capacity)
    safe_slot = jnp.minimum(slot_index, experts * capacity - 1)
    onehot_f = onehot.astype(jnp.float32)
    gate_value = jnp.sum(jnp.repeat(router_probs, 2, axis=0) * onehot_f, axis=1)
    outgoing = jnp.zeros((experts * capacity, model_width), jnp.bfloat16)
    outgoing = outgoing.at[slot_index].set(jnp.repeat(normed_four, 2, axis=0), mode="drop")
    outgoing = outgoing.reshape(owners, local_experts, capacity, model_width)
    returned, received, expert_pre = serve_rows(
        lax.all_to_all(outgoing, "expert", split_axis=0, concat_axis=0, tiled=True),
        expert_in=expert_in,
        expert_out=expert_out,
    )
    expert_rows = returned.reshape(experts * capacity, model_width)[safe_slot]
    weighted = gate_value[:, None] * expert_rows.astype(jnp.float32)
    mixture = jnp.sum(weighted.reshape(row_count, 2, model_width), axis=1)
    output = (hidden_two + mixture) * live_rows[:, None]
    load_local = jnp.sum(onehot_f, axis=0)
    prob_local = jnp.sum(router_probs * live_rows[:, None], axis=0)
    token_local = jnp.sum(live_rows)
    load_total, prob_total, token_total = lax.psum(
        (load_local, prob_local, token_local), ("expert", "shard")
    )
    fraction = load_total / (2.0 * token_total)
    balance_loss = experts * jnp.sum(fraction * prob_total / token_total)
    grad_out = cotangent.astype(jnp.float32).reshape(row_count, model_width) * live_rows[:, None]
    grad_pairs = jnp.repeat(grad_out, 2, axis=0)
    grad_gate = jnp.sum(grad_pairs * expert_rows.astype(jnp.float32), axis=1)
    grad_result = (gate_value[:, None] * grad_pairs).astype(jnp.bfloat16)
    grad_send = jnp.zeros((experts * capacity, model_width), jnp.bfloat16)
    grad_send = (
        grad_send.at[slot_index]
        .set(grad_result, mode="drop")
        .reshape(owners, local_experts, capacity, model_width)
    )
    grad_recv = lax.all_to_all(grad_send, "expert", split_axis=0, concat_axis=0, tiled=True)
    expert_act, gelu_pull = jax.vjp(gelu_exact, expert_pre)
    expert_act = expert_act.astype(jnp.bfloat16)
    grad_eout = jnp.einsum(
        "slcf,slcd->lfd", expert_act, grad_recv, preferred_element_type=jnp.float32
    )
    grad_act = jnp.einsum(
        "slcd,lfd->slcf", grad_recv, expert_out, preferred_element_type=jnp.float32
    )
    grad_pre = gelu_pull(grad_act)[0].astype(jnp.bfloat16)
    grad_ein = jnp.einsum("slcd,slcf->ldf", received, grad_pre, preferred_element_type=jnp.float32)
    grad_sent = jnp.einsum(
        "slcf,ldf->slcd", grad_pre, expert_in, preferred_element_type=jnp.float32
    ).astype(jnp.bfloat16)
    grad_return = lax.all_to_all(grad_sent, "expert", split_axis=0, concat_axis=0, tiled=True)
    grad_e_in, grad_e_out = (
        lax.psum(grad_ein.astype(jnp.bfloat16), "shard").astype(jnp.float32),
        lax.psum(grad_eout.astype(jnp.bfloat16), "shard").astype(jnp.float32),
    )
    back_rows = grad_return.reshape(experts * capacity, model_width)[safe_slot].astype(jnp.float32)
    back_rows = jnp.where(live_pairs[:, None], back_rows, 0.0)
    grad_from_experts = jnp.sum(back_rows.reshape(row_count, 2, model_width), axis=1)
    grad_probs = jnp.sum((grad_gate[:, None] * onehot_f).reshape(row_count, 2, experts), axis=1)
    grad_probs = (
        grad_probs + aux_weight * experts * fraction[None, :] * live_rows[:, None] / token_total
    )
    grad_logits = router_probs * (
        grad_probs - jnp.sum(router_probs * grad_probs, axis=-1, keepdims=True)
    )
    grad_logits = grad_logits.astype(jnp.bfloat16)
    grad_route = jnp.einsum(
        "nd,ne->de", normed_four, grad_logits, preferred_element_type=jnp.float32
    )
    grad_norm_four = (
        jnp.einsum("ne,de->nd", grad_logits, route_w, preferred_element_type=jnp.float32)
        + grad_from_experts
    )
    back_four = pull_four(grad_norm_four)
    grad_hidden_two = grad_out + back_four[0]
    grad_norm_three, grad_qkv_two, grad_out_two = attend_backward(
        grad_hidden_two, normed_three, qkv_two, out_two, saved_three
    )
    back_three = pull_three(grad_norm_three)
    grad_block = grad_hidden_two + back_three[0]
    grad_gain_two = jnp.stack([back_three[1], back_four[1]])
    late_qkv, late_out, late_route, late_gain = (
        lax.psum_scatter(
            grad_qkv_two.astype(jnp.bfloat16), "shard", scatter_dimension=1, tiled=True
        ).astype(jnp.float32),
        lax.psum_scatter(
            grad_out_two.astype(jnp.bfloat16), "shard", scatter_dimension=0, tiled=True
        ).astype(jnp.float32),
        lax.psum_scatter(
            grad_route.astype(jnp.bfloat16), "shard", scatter_dimension=0, tiled=True
        ).astype(jnp.float32),
        lax.psum_scatter(
            grad_gain_two.astype(jnp.bfloat16), "shard", scatter_dimension=1, tiled=True
        ).astype(jnp.float32),
    )
    late_qkv, late_out, late_route, late_gain = (
        lax.psum(late_qkv.astype(jnp.bfloat16), "expert").astype(jnp.float32),
        lax.psum(late_out.astype(jnp.bfloat16), "expert").astype(jnp.float32),
        lax.psum(late_route.astype(jnp.bfloat16), "expert").astype(jnp.float32),
        lax.psum(late_gain.astype(jnp.bfloat16), "expert").astype(jnp.float32),
    )
    grad_down_low = grad_block.astype(jnp.bfloat16)
    grad_w_down = jnp.einsum(
        "nf,nd->fd", mlp_act, grad_down_low, preferred_element_type=jnp.float32
    )
    grad_mlp_act = jnp.einsum(
        "nd,fd->nf", grad_down_low, w_down, preferred_element_type=jnp.float32
    )
    mlp_pull = jax.vjp(gelu_exact, mlp_pre)[1]
    grad_mlp_pre = mlp_pull(grad_mlp_act)[0].astype(jnp.bfloat16)
    grad_w_up = jnp.einsum(
        "nd,nf->df", normed_two, grad_mlp_pre, preferred_element_type=jnp.float32
    )
    grad_norm_two = jnp.einsum("nf,df->nd", grad_mlp_pre, w_up, preferred_element_type=jnp.float32)
    back_two = pull_two(grad_norm_two)
    grad_hidden = grad_block + back_two[0]
    grad_norm_one, grad_qkv_one, grad_out_one = attend_backward(
        grad_hidden, normed_one, qkv_one, out_one, saved_one
    )
    back_one = pull_one(grad_norm_one)
    grad_inputs = grad_hidden + back_one[0]
    grad_gain_one = jnp.stack([back_one[1], back_two[1]])
    early_qkv, early_out, early_up, early_down, early_gain = (
        lax.psum_scatter(
            grad_qkv_one.astype(jnp.bfloat16), "shard", scatter_dimension=1, tiled=True
        ).astype(jnp.float32),
        lax.psum_scatter(
            grad_out_one.astype(jnp.bfloat16), "shard", scatter_dimension=0, tiled=True
        ).astype(jnp.float32),
        lax.psum_scatter(
            grad_w_up.astype(jnp.bfloat16), "shard", scatter_dimension=0, tiled=True
        ).astype(jnp.float32),
        lax.psum_scatter(
            grad_w_down.astype(jnp.bfloat16), "shard", scatter_dimension=0, tiled=True
        ).astype(jnp.float32),
        lax.psum_scatter(
            grad_gain_one.astype(jnp.bfloat16), "shard", scatter_dimension=1, tiled=True
        ).astype(jnp.float32),
    )
    early_qkv, early_out, early_up, early_down, early_gain = (
        lax.psum(early_qkv.astype(jnp.bfloat16), "expert").astype(jnp.float32),
        lax.psum(early_out.astype(jnp.bfloat16), "expert").astype(jnp.float32),
        lax.psum(early_up.astype(jnp.bfloat16), "expert").astype(jnp.float32),
        lax.psum(early_down.astype(jnp.bfloat16), "expert").astype(jnp.float32),
        lax.psum(early_gain.astype(jnp.bfloat16), "expert").astype(jnp.float32),
    )
    return (
        output.astype(jnp.bfloat16).reshape(slot_count, seq_len, model_width),
        balance_loss,
        grad_inputs.reshape(slot_count, seq_len, model_width),
        early_qkv,
        early_out,
        early_up,
        early_down,
        early_gain,
        late_qkv,
        late_out,
        late_route,
        late_gain,
        grad_e_in,
        grad_e_out,
    )


def solution(mesh):
    return jax.shard_map(
        per_device,
        mesh=mesh,
        in_specs=(
            P(("expert", "shard"), None, None),
            P(("expert", "shard"), None, None),
            P(("expert", "shard"), None, None),
            P(("expert", "shard")),
            P(),
            P(None, "shard", None),
            P("shard", None),
            P("shard", None),
            P("shard", None),
            P(None, "shard"),
            P(None, "shard", None),
            P("shard", None),
            P("shard", None),
            P(None, "shard"),
            P("expert", None, None),
            P("expert", None, None),
        ),
        out_specs=(
            P(("expert", "shard"), None, None),
            P(),
            P(("expert", "shard"), None, None),
            P(None, "shard", None),
            P("shard", None),
            P("shard", None),
            P("shard", None),
            P(None, "shard"),
            P(None, "shard", None),
            P("shard", None),
            P("shard", None),
            P(None, "shard"),
            P("expert", None, None),
            P("expert", None, None),
        ),
        check_vma=False,
    )
```

profile of v0, /device:TPU:0, one launch (start us, length us, event | category | flops | bytes accessed | tf_op | source)
XLA Modules:
  0.0 1019.1 jit_solution(17279745648350581504)
XLA Ops:
  12.6 5.1 all_gather.27
  17.8 13.5 %all_gather.29 = bf16[512,512]{1,0:T(8,128)(2,1)} all-gather(bf16[256,512]{1,0:T(8,128)(2,1)S(1)} %copy-done.55), channel_id=1, replica_groups=mesh['expert'=16,'shard'=2] {'shard'}, dimensions={0}, use_global_device_ids=true | all-gather | bytes 786432 | tf_op jit(solution)/shard_map/all_gather | solution.py:134
  31.3 4.8 all_gather.32
  36.1 12.2 %all_gather.34 = bf16[512,512]{1,0:T(8,128)(2,1)} all-gather(bf16[256,512]{1,0:T(8,128)(2,1)S(1)} %copy-done.56), channel_id=1, replica_groups=mesh['expert'=16,'shard'=2] {'shard'}, dimensions={0}, use_global_device_ids=true | all-gather | bytes 786432 | tf_op jit(solution)/shard_map/all_gather | solution.py:139
  48.6 9.1 reduce-window.6
  83.6 15.7 %multiply_convert_fusion.2 = (bf16[591,2048]{1,0:T(8,128)(2,1)}, f32[591,2048]{1,0:T(8,128)}, f32[591,2048]{1,0:T(8,128)}) fusion(bf16[512,2048]{1,0:T(8,128)(2,1)} %all-gather.7.cloned.1.call-done, f32[591,512]{1,0:T(8,128)S(1)} %get-tuple-element.125, f32[512]{0:T(512)S(1)} %bitcast.269, f32[591]{0:T(1024)S(1)} %fusion.119, ...), kind=kOutput, calls=%fused_computation.52 | convolution fusion | flops 1319301120 | bytes 15417976 | tf_op jit(solution)/shard_map/dot_general | solution.py:153
  99.4 19.0 %all-gather.9.cloned.1.call-done = bf16[2048,512]{1,0:T(8,128)(2,1)} async-done(((bf16[1024,512]{1,0:T(8,128)(2,1)}), bf16[2048,512]{1,0:T(8,128)(2,1)}) %all-gather.9.cloned.1.call-update) | async-done | bytes 2097168 | tf_op jit(solution)/shard_map/all_gather | solution.py:136
  123.2 23.8 %all-gather.11.cloned.1.call-done = bf16[3,512,512]{2,1,0:T(8,128)(2,1)} async-done(((bf16[3,256,512]{2,1,0:T(8,128)(2,1)}), bf16[3,512,512]{2,1,0:T(8,128)(2,1)}) %all-gather.11.cloned.1.call-update) | async-done | bytes 1572880 | tf_op jit(solution)/shard_map/all_gather | solution.py:138
  170.3 8.4 scatter_custom_fusion
  178.7 36.9 %all_to_all.20 = bf16[16,2,40,512]{3,2,1,0:T(8,128)(2,1)S(1)} all-to-all(bf16[16,2,40,512]{3,2,1,0:T(8,128)(2,1)S(1)} %bitcast.253), channel_id=1, replica_groups=mesh['expert'=16,'shard'=2] {'expert'}, dimensions={0} | all-to-all | bytes 2621440 | tf_op jit(solution)/shard_map/all_to_all | solution.py:177
  215.7 28.4 %fusion.9 = (bf16[16,2,40,2048]{3,2,0,1:T(8,128)(2,1)S(1)}, f32[16,2,40,2048]{3,2,0,1:T(8,128)}, f32[2,16,40,2048]{3,2,1,0:T(8,128)}) fusion(bf16[2,512,2048]{2,1,0:T(8,128)(2,1)} %param.30, bf16[16,2,40,512]{3,2,1,0:T(8,128)(2,1)S(1)} %all_to_all.20), kind=kOutput, calls=%fused_computation.21 | convolution fusion | flops 2854748160 | bytes 31719424 | tf_op jit(solution)/shard_map/slcd,ldf->slcf/dot_general | solution.py:99
  265.2 14.4 %all-to-all-done.1 = bf16[16,2,40,512]{3,2,1,0:T(8,128)(2,1)S(1)} async-done(((bf16[16,2,40,512]{3,2,1,0:T(8,128)(2,1)}), bf16[16,2,40,512]{3,2,1,0:T(8,128)(2,1)S(1)}, u32[]{:S(2)}, u32[]{:S(2)}) %all-to-all-start.1) | async-done | bytes 1310752 | tf_op jit(solution)/shard_map/all_to_all | solution.py:104
  279.6 5.1 gather_fusion
  288.0 10.7 %scatter_custom_fusion.1 = bf16[1280,512]{1,0:T(8,128)(2,1)} fusion(s32[1182]{0:T(1024)S(1)} %get-tuple-element.83, f32[1182,512]{1,0:T(8,128)S(1)} %copy-done.4, f32[1182]{0:T(1024)S(1)} %mul.530, bf16[]{:T(256)} %constant.77.clone.1), kind=kCustom, calls=%fused_computation.136 | custom fusion | flops 1210368 | bytes 3743746 | tf_op jit(solution)/shard_map/scatter | solution.py:200
  298.7 39.5 %all_to_all.21 = bf16[16,2,40,512]{3,2,1,0:T(8,128)(2,1)S(1)} all-to-all(bf16[16,2,40,512]{3,2,1,0:T(8,128)(2,1)} %bitcast.252), channel_id=1, replica_groups=mesh['expert'=16,'shard'=2] {'expert'}, dimensions={0} | all-to-all | bytes 2621440 | tf_op jit(solution)/shard_map/all_to_all | solution.py:203
  338.3 13.1 %fusion.6 = bf16[16,2,40,2048]{3,2,0,1:T(8,128)(2,1)} fusion(f32[16,2,40,2048]{3,2,0,1:T(8,128)} %get-tuple-element.108, f32[2,16,40,2048]{3,2,1,0:T(8,128)} %get-tuple-element.133, bf16[2,2048,512]{2,1,0:T(8,128)(2,1)} %param.31, bf16[16,2,40,512]{3,2,1,0:T(8,128)(2,1)S(1)} %all_to_all.21), kind=kOutput, calls=%fused_computation.13 | convolution fusion | flops 2721054720 | bytes 31719424 | tf_op jit(solution)/shard_map/slcd,lfd->slcf/dot_general | solution.py:209
  351.3 5.4 fusion.64
  362.9 50.7 %all-reduce.1 = (f32[]{:T(128)}, f32[32]{0:T(128)S(1)}) all-reduce(f32[]{:T(128)} %broadcast_reduce_fusion, f32[32]{0:T(128)S(1)} %fusion.111), channel_id=1, replica_groups=mesh['expert'=16,'shard'=2] {'expert','shard'}, use_global_device_ids=true, to_apply=%region_23.24 | all-reduce | flops 33 | bytes 264 | tf_op jit(solution)/shard_map/psum | solution.py:188
  419.9 6.0 multiply_reduce_fusion.5
  425.9 4.7 gather_fusion.1
  526.8 5.0 convolution_convert_fusion.1
  532.1 5.2 convolution_convert_fusion
  545.2 7.7 bitcast_convert_fusion.1
  552.9 8.4 bitcast_convert_fusion
  561.5 14.2 %reduce-scatter.14.cloned.1.call-done = bf16[3,256,512]{1,2,0:T(8,128)(2,1)} async-done(((bf16[3,512,512]{1,2,0:T(8,128)(2,1)}), bf16[3,256,512]{1,2,0:T(8,128)(2,1)}) %reduce-scatter.14.cloned.1.call-update) | async-done | bytes 786448 | tf_op jit(solution)/shard_map/reduce_scatter | solution.py:290
  575.7 34.7 %reduce-scatter.18.cloned.1.call-done = bf16[256,2048]{1,0:T(8,128)(2,1)} async-done(((bf16[512,2048]{1,0:T(8,128)(2,1)}), bf16[256,2048]{1,0:T(8,128)(2,1)}) %reduce-scatter.18.cloned.1.call-update) | async-done | bytes 1048592 | tf_op jit(solution)/shard_map/reduce_scatter | solution.py:296
  610.4 34.6 %reduce-scatter.20.cloned.1.call-done = bf16[1024,512]{1,0:T(8,128)(2,1)} async-done(((bf16[2048,512]{1,0:T(8,128)(2,1)}), bf16[1024,512]{1,0:T(8,128)(2,1)}) %reduce-scatter.20.cloned.1.call-update) | async-done | bytes 1048592 | tf_op jit(solution)/shard_map/reduce_scatter | solution.py:299
  645.1 39.4 %psum.100 = f32[32]{0:T(128)S(1)} all-reduce(f32[32]{0:T(128)S(1)} %copy-done.118), channel_id=1, replica_groups=mesh['expert'=16,'shard'=2] {'expert','shard'}, use_global_device_ids=true, to_apply=%region_25.26 | all-reduce | flops 32 | bytes 256 | tf_op jit(solution)/shard_map/psum | solution.py:188
  692.4 60.1 %all-reduce.2 = (bf16[2,256]{1,0:T(2,128)(2,1)S(1)}, bf16[256,32]{0,1:T(8,128)(2,1)S(1)}, bf16[2,256]{1,0:T(2,128)(2,1)S(1)}) all-reduce(bf16[2,256]{1,0:T(2,128)(2,1)S(1)} %copy.257, bf16[256,32]{0,1:T(8,128)(2,1)} %reduce-scatter.26.cloned.1.call-done, bf16[2,256]{1,0:T(2,128)(2,1)S(1)} %copy.259), channel_id=1, replica_groups=mesh['expert'=16,'shard'=2] {'expert'}, use_global_device_ids=true, to_apply=%region_53.54 | all-reduce | flops 9216 | bytes 36864 | tf_op jit(solution)/shard_map/psum | solution.py:311
  754.4 129.8 %all-reduce.10.cloned.1.call-done = (bf16[2,512,2048]{2,1,0:T(8,128)(2,1)}, bf16[2,2048,512]{2,1,0:T(8,128)(2,1)}) async-done(((bf16[2,512,2048]{2,1,0:T(8,128)(2,1)}, bf16[2,2048,512]{2,1,0:T(8,128)(2,1)}), (bf16[2,512,2048]{2,1,0:T(8,128)(2,1)}, bf16[2,2048,512]{2,1,0:T(8,128)(2,1)})) %all-reduce.10.cloned.1.call-update) | async-done | bytes 8388624 | tf_op jit(solution)/shard_map/psum | solution.py:219
  884.2 6.8 convert_element_type.308
  895.6 106.5 %all-reduce.8.cloned.1.call-done = (bf16[3,256,512]{1,2,0:T(8,128)(2,1)}, bf16[3,256,512]{1,2,0:T(8,128)(2,1)}, bf16[256,512]{1,0:T(8,128)(2,1)}, bf16[256,2048]...) async-done(((bf16[3,256,512]{1,2,0:T(8,128)(2,1)}, bf16[3,256,512]{1,2,0:T(8,128)(2,1)}, bf16[256,512]{1,0:T(8,128)(2,1)}, ...) | async-done | bytes 4194320 | tf_op jit(solution)/shard_map/psum | solution.py:307
  (506 shorter events, 220.2 us)
Async XLA Ops:
  7.2 52.2 %all-gather.5.cloned.1.call-start = ((), (), s32[]{:S(2)}) async-start(), calls=%async_computation.13 | async-start | bytes 2359296 | tf_op jit(solution)/shard_map/all_gather | solution.py:133
  7.9 75.7 %all-gather.7.cloned.1.call-start = ((), (), s32[]{:S(2)}) async-start(), calls=%async_computation.14 | async-start | bytes 3145728 | tf_op jit(solution)/shard_map/all_gather | solution.py:135
  8.7 109.7 %all-gather.9.cloned.1.call-start = ((), (), s32[]{:S(2)}) async-start(), calls=%async_computation.15 | async-start | bytes 3145728 | tf_op jit(solution)/shard_map/all_gather | solution.py:136
  9.5 137.6 %all-gather.11.cloned.1.call-start = ((), (), s32[]{:S(2)}) async-start(), calls=%async_computation.16 | async-start | bytes 2359296 | tf_op jit(solution)/shard_map/all_gather | solution.py:138
  10.4 69.3 %copy-start.7 = (f32[591,512]{1,0:T(8,128)}, f32[591,512]{1,0:T(8,128)S(1)}, u32[]{:S(2)}) copy-start(f32[591,512]{1,0:T(8,128)S(1)} %reshape.414) | copy-start | bytes 3631108
  10.9 48.5 %copy-start.94 = (f32[591]{0:T(1024)}, f32[591]{0:T(1024)S(1)}, u32[]{:S(2)}) copy-start(f32[591]{0:T(1024)S(1)} %div.117) | copy-start | bytes 7096
  12.6 46.8 %copy-start.96 = (f32[591]{0:T(1024)}, f32[591]{0:T(1024)S(1)}, u32[]{:S(2)}) copy-start(f32[591]{0:T(1024)S(1)} %rsqrt.40) | copy-start | bytes 7096
  17.8 65.9 %copy-start.105 = (f32[1,512]{1,0:T(1,128)}, f32[1,512]{1,0:T(1,128)S(1)}, u32[]{:S(2)}) copy-start(f32[1,512]{1,0:T(1,128)S(1)} %get-tuple-element.120) | copy-start | bytes 6148
  36.1 111.0 %copy-start.108 = (f32[1,512]{1,0:T(1,128)}, f32[1,512]{1,0:T(1,128)S(1)}, u32[]{:S(2)}) copy-start(f32[1,512]{1,0:T(1,128)S(1)} %get-tuple-element.119) | copy-start | bytes 6148
  36.1 132.8 %copy-start.92 = (f32[1,512]{1,0:T(1,128)}, f32[1,512]{1,0:T(1,128)S(1)}, u32[]{:S(2)}) copy-start(f32[1,512]{1,0:T(1,128)S(1)} %get-tuple-element.118) | copy-start | bytes 6148
  169.2 95.6 %copy-start.29 = (bf16[591,512]{1,0:T(8,128)(2,1)}, bf16[591,512]{1,0:T(8,128)(2,1)S(1)}, u32[]{:S(2)}) copy-start(bf16[591,512]{1,0:T(8,128)(2,1)S(1)} %multiply_convert_fusion.10) | copy-start | bytes 1815556
  248.3 31.4 %all-to-all-start.1 = ((bf16[16,2,40,512]{3,2,1,0:T(8,128)(2,1)}), bf16[16,2,40,512]{3,2,1,0:T(8,128)(2,1)S(1)}, u32[]{:S(2)}, u32[]{:S(2)}) async-start(bf16[16,2,40,512]{3,2,1,0:T(8,128)(2,1)} %copy.200), calls=%async_computation.1 | async-start | bytes 2621440 | tf_op jit(solution)/shard_map/all_to_all | solution.py:104
  265.2 172.3 %copy-start.44 = (f32[591,32]{0,1:T(8,128)}, f32[591,32]{0,1:T(8,128)S(1)}, u32[]{:S(2)}) copy-start(f32[591,32]{0,1:T(8,128)S(1)} %get-tuple-element.135) | copy-start | bytes 226948
  287.6 149.8 %copy-start.53 = (f32[591,32]{0,1:T(8,128)}, f32[591,32]{0,1:T(8,128)S(1)}, u32[]{:S(2)}) copy-start(f32[591,32]{0,1:T(8,128)S(1)} %get-tuple-element.80) | copy-start | bytes 226948
  356.8 58.7 %copy-start.62 = (f32[3,8,197]{2,1,0:T(8,128)S(1)}, f32[3,8,197]{2,1,0:T(8,128)}, u32[]{:S(2)}) copy-start(f32[3,8,197]{2,1,0:T(8,128)} %copy-done.61) | copy-start | bytes 56740
  356.8 58.7 %copy-start.72 = (f32[3,8,197]{2,1,0:T(8,128)S(1)}, f32[3,8,197]{2,1,0:T(8,128)}, u32[]{:S(2)}) copy-start(f32[3,8,197]{2,1,0:T(8,128)} %copy-done.71) | copy-start | bytes 56740
  356.8 58.7 %copy-start.16 = (bf16[1182,512]{1,0:T(8,128)(2,1)S(1)}, bf16[1182,512]{1,0:T(8,128)(2,1)}, u32[]{:S(2)}) copy-start(bf16[1182,512]{1,0:T(8,128)(2,1)} %gather_fusion) | copy-start | bytes 3631108
  358.0 67.9 %all-to-all-start.3 = ((bf16[16,2,40,512]{3,2,1,0:T(8,128)(2,1)}), bf16[16,2,40,512]{3,2,1,0:T(8,128)(2,1)S(1)}, u32[]{:S(2)}, u32[]{:S(2)}) async-start(bf16[16,2,40,512]{3,2,1,0:T(8,128)(2,1)} %copy.204), calls=%async_computation.3 | async-start | bytes 2621440 | tf_op jit(solution)/shard_map/all_to_all | solution.py:217
  362.0 199.5 %reduce-scatter.16.cloned.1.call-start = ((), (), s32[]{:S(2)}) async-start(), calls=%async_computation.18 | async-start | bytes 786432 | tf_op jit(solution)/shard_map/reduce_scatter | solution.py:293
  484.8 76.6 %reduce-scatter.24.cloned.1.call-start = ((), (), s32[]{:S(2)}) async-start(), calls=%async_computation.22 | async-start | bytes 786432 | tf_op jit(solution)/shard_map/reduce_scatter | solution.py:252
  486.3 75.2 %reduce-scatter.22.cloned.1.call-start = ((), (), s32[]{:S(2)}) async-start(), calls=%async_computation.21 | async-start | bytes 2359296 | tf_op jit(solution)/shard_map/reduce_scatter | solution.py:249
  491.0 84.8 %reduce-scatter.14.cloned.1.call-start = ((), (), s32[]{:S(2)}) async-start(), calls=%async_computation.17 | async-start | bytes 2359296 | tf_op jit(solution)/shard_map/reduce_scatter | solution.py:290
  526.7 83.7 %reduce-scatter.18.cloned.1.call-start = ((), (), s32[]{:S(2)}) async-start(), calls=%async_computation.19 | async-start | bytes 3145728 | tf_op jit(solution)/shard_map/reduce_scatter | solution.py:296
  531.8 113.2 %reduce-scatter.20.cloned.1.call-start = ((), (), s32[]{:S(2)}) async-start(), calls=%async_computation.20 | async-start | bytes 3145728 | tf_op jit(solution)/shard_map/reduce_scatter | solution.py:299
  537.3 153.3 %reduce-scatter.30.cloned.1.call-start = ((), (), s32[]{:S(2)}) async-start(), calls=%async_computation.25 | async-start | bytes 196608
  542.6 148.9 %reduce-scatter.28.cloned.1.call-start = ((), (), s32[]{:S(2)}) async-start(), calls=%async_computation.24 | async-start | bytes 196608
  543.5 148.9 %reduce-scatter.26.cloned.1.call-start = ((), (), s32[]{:S(2)}) async-start(), calls=%async_computation.23 | async-start | bytes 49152 | tf_op jit(solution)/shard_map/reduce_scatter | solution.py:255
  545.2 339.0 %all-reduce.10.cloned.1.call-start = ((), (), s32[]{:S(2)}) async-start(), calls=%async_computation.27 | async-start | bytes 16777216 | tf_op jit(solution)/shard_map/psum | solution.py:219
  561.4 83.7 %copy-start.118 = (f32[32]{0:T(128)S(1)}, f32[32]{0:T(128)}, u32[]{:S(2)}) copy-start(f32[32]{0:T(128)} %get-tuple-element.79) | copy-start | bytes 388
  561.4 123.1 %copy-start.113 = (f32[32]{0:T(128)S(1)}, f32[32]{0:T(128)}, u32[]{:S(2)}) copy-start(f32[32]{0:T(128)} %get-tuple-element.106) | copy-start | bytes 388
  561.4 125.0 %copy-start.88 = (f32[591]{0:T(1024)S(1)}, f32[591]{0:T(1024)}, u32[]{:S(2)}) copy-start(f32[591]{0:T(1024)} %copy-done.87) | copy-start | bytes 7096
  561.4 440.7 %all-reduce.8.cloned.1.call-start = ((), (), s32[]{:S(2)}) async-start(), calls=%async_computation.26 | async-start | bytes 8388608 | tf_op jit(solution)/shard_map/psum | solution.py:307
  (122 other events, 953.9 us)
Sparse Core Ops, SparseCore 0:
  9.6 37.9 all-gather.4
  49.1 34.4 all-gather.6
  85.2 33.1 all-gather.8
  119.8 27.1 all-gather.10
  485.0 15.4 reduce-scatter.15
  503.2 14.5 reduce-scatter.23
  520.6 26.0 reduce-scatter.21
  549.6 26.0 reduce-scatter.13
  578.6 31.8 reduce-scatter.17
  613.2 31.8 reduce-scatter.19
  647.3 10.2 reduce-scatter.29
  659.6 10.3 reduce-scatter.27
  672.7 9.8 reduce-scatter.25
  685.5 198.5 all-reduce.9
  888.4 113.6 all-reduce.7
where the time goes:
time: 1030 us; the launch traced here: 1020 us
  waiting for transfers between devices  382 us (37%)
  blocking collectives  267 us (26%)
  matrix products  157 us (15%)
  local copies, waits for them, and re-layouts  117 us (11%)
  other arithmetic  68.4 us (7%)
  between operations  20.1 us (2%)
    psum x1, waiting for transfers between devices, per_device(): lax.psum(grad_ein.astype(jnp.bfloat16), 'shard').astype(jnp.float32)  130 us
    psum x1, waiting for transfers between devices, per_device(): lax.psum(early_qkv.astype(jnp.bfloat16), 'expert').astype(jnp.float32)  107 us
    psum x2, blocking collectives, per_device(): lax.psum((load_local, prob_local, token_local), ('expert', 'shard'))  90.1 us
    psum x1, blocking collectives, per_device(): lax.psum(early_gain.astype(jnp.bfloat16), 'expert').astype(jnp.float32)  60.1 us
    all_to_all x1, blocking collectives, per_device(): lax.all_to_all(grad_send, 'expert', split_axis=0, concat_axis=0, tiled=True)  39.5 us
    all_to_all x1, blocking collectives, per_device(): lax.all_to_all(outgoing, 'expert', split_axis=0, concat_axis=0, tiled=True)  36.9 us
    reduce_scatter x1, waiting for transfers between devices, per_device(): lax.psum_scatter(grad_w_up.astype(jnp.bfloat16), 'shard', scatter_dimensi...  34.7 us
    reduce_scatter x1, waiting for transfers between devices, per_device(): lax.psum_scatter(grad_w_down.astype(jnp.bfloat16), 'shard', scatter_dimen...  34.6 us
  transfers between devices with their start and end apart: 17, of which 9 were waited for; matrix products, arithmetic and copies ran while one was open for 17% of the time, Pallas kernels for 0%

commit v1 on v0

v1 whole, which is shorter than its diff:
```python
import functools

import jax
import jax.numpy as jnp
from jax import lax
from jax.experimental import pallas as pl
from jax.experimental.pallas import tpu as pltpu
from jax.sharding import PartitionSpec as P

HEADS = 8
CAP = 40
EPS = 1e-06
NEG = -1e30
LANES = 128
f32 = jnp.float32
bf16 = jnp.bfloat16
ANY = pl.BlockSpec(memory_space=pl.ANY)
VM = pl.BlockSpec(memory_space=pltpu.VMEM)
VMEM_BYTES = 58 << 20


def nn(a, b):
    return lax.dot_general(a, b, (((1,), (0,)), ((), ())), preferred_element_type=f32)


def nt(a, b):
    return lax.dot_general(a, b, (((1,), (1,)), ((), ())), preferred_element_type=f32)


def tn(a, b):
    return lax.dot_general(a, b, (((0,), (0,)), ((), ())), preferred_element_type=f32)


def sds(shape, dtype):
    return jax.ShapeDtypeStruct(shape, dtype)


def padded(seq):
    return -(-seq // 16) * 16


def norm(x):
    xc = x - jnp.mean(x, axis=-1, keepdims=True)
    rs = lax.rsqrt(jnp.mean(xc * xc, axis=-1, keepdims=True) + EPS)
    return xc * rs, rs


def norm_back(dyn, xn, rs, gain):
    dgain = jnp.sum(dyn * xn, axis=0, keepdims=True)
    dxn = dyn * gain
    dv = dxn - jnp.mean(dxn, axis=-1, keepdims=True)
    dv = (dv - xn * jnp.mean(dxn * xn, axis=-1, keepdims=True)) * rs
    return dv, dgain


def gelu_pair(z):
    a = jnp.abs(z)
    t = 1.0 / (1.0 + (0.3275911 * 0.7071067811865476) * a)
    e = jnp.exp(-0.5 * (z * z))
    q = t * (0.127414796 + t * (-0.142248368 + t * (0.7107068705 + t * (-0.7265760135 + t * 0.5307027145))))
    q = q * e
    phi = jnp.where(z >= 0.0, 1.0 - q, q)
    return z * phi, phi + z * (e * 0.3989422804014327)


class Split:
    def __init__(self, shards):
        self.pair = shards == 2
        self.shards = shards

    def gather(self, owns):
        if not self.pair:
            whole = [lax.all_gather(o, "shard", axis=1, tiled=True) for o in owns]
            return whole
        core = lax.axis_index("expert") % 2
        owners = lax.axis_size("expert")
        half = owns[0].shape[1] // 2
        send = jnp.concatenate([lax.dynamic_slice_in_dim(o, core * half, half, 1) for o in owns], axis=0)
        far = lax.ppermute(send, "shard", [(0, 1), (1, 0)])
        near = lax.ppermute(far, "expert", [(i, i ^ 1) for i in range(owners)])
        return list(owns) + [far, near]

    def count(self, owns):
        return owns + 2 if self.pair else owns

    def copies(self, refs, full, sems):
        out = []
        if not self.pair:
            at = 0
            for i, r in enumerate(refs):
                n = r.shape[0]
                out.append(pltpu.make_async_copy(r, full.at[at:at + n], sems.at[i]))
                at += n
            return out
        me = lax.axis_index("shard")
        core = lax.axis_index("expert") % 2
        rows = refs[0].shape[1]
        half = rows // 2
        at = 0
        for i, r in enumerate(refs[:-2]):
            n = r.shape[0]
            out.append(pltpu.make_async_copy(r, full.at[at:at + n, pl.ds(me * rows, rows), :], sems.at[i]))
            at += n
        base = (1 - me) * rows
        k = len(refs) - 2
        out.append(pltpu.make_async_copy(refs[k], full.at[:, pl.ds(base + core * half, half), :], sems.at[k]))
        out.append(pltpu.make_async_copy(refs[k + 1], full.at[:, pl.ds(base + (1 - core) * half, half), :], sems.at[k + 1]))
        return out


def start(copies):
    for c in copies:
        c.start()


def finish(copies):
    for c in copies:
        c.wait()


def call(body, outs, ins, scratch=(), specs=None, flops=0, nbytes=0, **kw):
    return pl.pallas_call(
        body,
        out_shape=outs,
        in_specs=specs or [VM] * len(ins),
        out_specs=[VM] * len(outs),
        scratch_shapes=list(scratch),
        compiler_params=pltpu.CompilerParams(vmem_limit_bytes=VMEM_BYTES),
        cost_estimate=pl.CostEstimate(flops=int(flops), bytes_accessed=int(nbytes), transcendentals=0),
        **kw,
    )(*ins)


def pad_store(ref, block, images, seq, step):
    ref[...] = jnp.zeros(ref.shape, ref.dtype)
    for i in range(images):
        ref[i * step:i * step + seq, :] = block(i).astype(ref.dtype)


def slot_start(expert, local, block):
    owner = jnp.floor((expert.astype(f32) + 0.5) * (1.0 / local))
    return owner * block + (expert.astype(f32) - owner * local) * CAP


def route_body(images, seq, local, block, r_ref, rt_ref, live_ref, cot_ref, dy_ref, dyd_ref, disp_ref, back_ref):
    rows = r_ref.shape[0]
    slots = disp_ref.shape[0]
    step = rows // images
    pad_store(dy_ref, lambda i: cot_ref[i], images, seq, step)
    dy_ref[...] = (dy_ref[...].astype(f32) * live_ref[...]).astype(bf16)
    lane = lax.broadcasted_iota(jnp.int32, (rows, LANES), 1)
    hit = (r_ref[:, 0:1] == lane) | (r_ref[:, 1:2] == lane)
    ti = lax.broadcasted_iota(jnp.int32, (rows, rows), 0)
    tj = lax.broadcasted_iota(jnp.int32, (rows, rows), 1)
    place = nn((ti > tj).astype(f32).astype(bf16), hit.astype(f32).astype(bf16))
    place = jnp.where(hit, place, -1.0).astype(bf16)
    off = lax.broadcasted_iota(jnp.int32, (LANES, slots), 1).astype(f32) - slot_start(
        lax.broadcasted_iota(jnp.int32, (LANES, slots), 0), local, block)
    spread = ((off >= 0) & (off < CAP)).astype(f32)
    within = jnp.sum(spread * off, axis=0, keepdims=True)
    within = jnp.where(jnp.sum(spread, axis=0, keepdims=True) > 0, within, -2.0)
    back_ref[...] = (nn(place, spread.astype(bf16)) == within).astype(f32).astype(bf16)
    sub = lax.broadcasted_iota(jnp.int32, (LANES, rows), 0)
    hit_t = (rt_ref[0:1, :] == sub) | (rt_ref[1:2, :] == sub)
    place_t = nn(hit_t.astype(f32).astype(bf16), (ti < tj).astype(f32).astype(bf16))
    place_t = jnp.where(hit_t, place_t, -1.0).astype(bf16)
    off = lax.broadcasted_iota(jnp.int32, (slots, LANES), 0).astype(f32) - slot_start(
        lax.broadcasted_iota(jnp.int32, (slots, LANES), 1), local, block)
    spread_t = ((off >= 0) & (off < CAP)).astype(f32)
    within_t = jnp.sum(spread_t * off, axis=1, keepdims=True)
    within_t = jnp.where(jnp.sum(spread_t, axis=1, keepdims=True) > 0, within_t, -2.0)
    disp_ref[...] = (nn(spread_t.astype(bf16), place_t) == within_t).astype(f32).astype(bf16)
    dyd_ref[...] = nn(disp_ref[...], dy_ref[...]).astype(bf16)


def attend_forward(step, seq, images, x, gain, wq, wo, qkv_ref, mix_ref):
    width = x.shape[1]
    head = width // HEADS
    scale = head ** -0.5
    xn, _ = norm(x)
    a = (xn * gain).astype(bf16)
    for c in range(3):
        qkv_ref[:, c * width:(c + 1) * width] = nn(a, wq[c][...]).astype(bf16)
    lane = lax.broadcasted_iota(jnp.int32, (1, LANES), 1)
    col = lax.broadcasted_iota(jnp.int32, (1, step), 1)
    per = LANES // head

    def image(i, _):
        at = pl.ds(pl.multiple_of(i * step, step), step)
        for hp in range(width // LANES):
            q = qkv_ref[at, hp * LANES:(hp + 1) * LANES]
            k = qkv_ref[at, width + hp * LANES:width + (hp + 1) * LANES]
            v = qkv_ref[at, 2 * width + hp * LANES:2 * width + (hp + 1) * LANES]
            got = None
            for h in range(per):
                mine = (lane >= h * head) & (lane < (h + 1) * head)
                qm = q * jnp.where(mine, scale, 0.0).astype(bf16)
                s = jnp.where(col < seq, nt(qm, k), NEG)
                e = jnp.exp(s - jnp.max(s, axis=-1, keepdims=True))
                p = (e * (1.0 / jnp.sum(e, axis=-1, keepdims=True))).astype(bf16)
                o = nn(p, v)
                got = o if got is None else jnp.where(mine, o, got)
            mix_ref[at, hp * LANES:(hp + 1) * LANES] = got.astype(bf16)
        return 0

    lax.fori_loop(0, images, image, 0)
    return x + nn(mix_ref[...], wo[...])


def attend_backward(step, seq, images, grad, x, gain, wq, wo, qkv_ref, mix_ref, dmix_ref, dqkv_ref, pack_ref, base):
    width = x.shape[1]
    head = width // HEADS
    scale = head ** -0.5
    shards = pack_ref.shape[0]
    part = width // shards
    low = grad.astype(bf16)
    dwo = tn(mix_ref[...], low).astype(bf16)
    for s in range(shards):
        pack_ref[s, base + 3 * part:base + 4 * part, :] = dwo[s * part:(s + 1) * part]
    dmix_ref[...] = nt(low, wo[...]).astype(bf16)
    lane = lax.broadcasted_iota(jnp.int32, (1, LANES), 1)
    key = lax.broadcasted_iota(jnp.int32, (step, 1), 0)
    per = LANES // head

    def image(i, _):
        at = pl.ds(pl.multiple_of(i * step, step), step)
        for hp in range(width // LANES):
            q = qkv_ref[at, hp * LANES:(hp + 1) * LANES]
            k = qkv_ref[at, width + hp * LANES:width + (hp + 1) * LANES]
            v = qkv_ref[at, 2 * width + hp * LANES:2 * width + (hp + 1) * LANES]
            do = dmix_ref[at, hp * LANES:(hp + 1) * LANES]
            dq = dk = dv = None
            for h in range(per):
                mine = (lane >= h * head) & (lane < (h + 1) * head)
                scaled = jnp.where(mine, scale, 0.0).astype(bf16)
                km = k * scaled
                s = jnp.where(key < seq, nt(km, q), NEG)
                e = jnp.exp(s - jnp.max(s, axis=0, keepdims=True))
                p = e * (1.0 / jnp.sum(e, axis=0, keepdims=True))
                dom = do * jnp.where(mine, 1.0, 0.0).astype(bf16)
                dp = nt(v, dom)
                ds = (p * (dp - jnp.sum(p * dp, axis=0, keepdims=True))).astype(bf16)
                hv = nn(p.astype(bf16), dom)
                hk = nn(ds, q * scaled)
                hq = tn(ds, km)
                dq, dk, dv = (hq, hk, hv) if dq is None else (dq + hq, dk + hk, dv + hv)
            dqkv_ref[at, hp * LANES:(hp + 1) * LANES] = dq.astype(bf16)
            dqkv_ref[at, width + hp * LANES:width + (hp + 1) * LANES] = dk.astype(bf16)
            dqkv_ref[at, 2 * width + hp * LANES:2 * width + (hp + 1) * LANES] = dv.astype(bf16)
        return 0

    lax.fori_loop(0, images, image, 0)
    xn, rs = norm(x)
    a = (xn * gain).astype(bf16)
    da = None
    for c in range(3):
        d = dqkv_ref[:, c * width:(c + 1) * width]
        dw = tn(a, d).astype(bf16)
        for s in range(shards):
            pack_ref[s, base + c * part:base + (c + 1) * part, :] = dw[s * part:(s + 1) * part]
        one = nt(d, wq[c][...])
        da = one if da is None else da + one
    return norm_back(da, xn, rs, gain)


def block1_body(split, images, seq, x_ref, gain_ref, *refs):
    n = split.count(2)
    pieces, (hidden_ref, qkv_ref, mix_ref, w, sems) = refs[:n], refs[n:]
    copies = split.copies(pieces, w, sems)
    start(copies)
    step = hidden_ref.shape[0] // images
    pad_store(hidden_ref, lambda i: x_ref[i], images, seq, step)
    finish(copies)
    hidden_ref[...] = attend_forward(
        step, seq, images, hidden_ref[...], gain_ref[0:1, :], [w.at[c] for c in range(3)], w.at[3], qkv_ref, mix_ref
    )


def mlp_body(split, blocks, hidden_ref, gain_ref, *refs):
    n = 2 * split.count(1)
    pieces, (out_ref, act_ref, slope_ref, w1, w2, sems) = refs[:n], refs[n:]
    half = n // 2
    copies = split.copies(pieces[:half], w1, sems.at[0]) + split.copies(pieces[half:], w2, sems.at[1])
    start(copies)
    hidden = hidden_ref[...]
    xn, _ = norm(hidden)
    u = (xn * gain_ref[1:2, :]).astype(bf16)
    out_ref[...] = hidden
    finish(copies)
    ff = act_ref.shape[1]
    wide = ff // blocks
    for b in range(blocks):
        at = slice(b * wide, (b + 1) * wide)
        act, slope = gelu_pair(nn(u, w1[0, :, at]))
        act = act.astype(bf16)
        act_ref[:, at] = act
        slope_ref[:, at] = slope.astype(bf16)
        out_ref[...] += nn(act, w2[0, at, :])


def router_probs(u, router, experts):
    lane = lax.broadcasted_iota(jnp.int32, (1, LANES), 1)
    logits = jnp.where(lane < experts, nn(u, router), NEG)
    e = jnp.exp(logits - jnp.max(logits, axis=-1, keepdims=True))
    return e * (1.0 / jnp.sum(e, axis=-1, keepdims=True))


def block2_body(split, images, seq, experts, x_ref, gain_ref, router_ref, disp_ref, live_ref, load_ref, *refs):
    n = split.count(2)
    pieces, (hidden_ref, qkv_ref, mix_ref, u_ref, probs_ref, sum_ref, ud_ref, w, sems) = refs[:n], refs[n:]
    copies = split.copies(pieces, w, sems)
    start(copies)
    finish(copies)
    step = hidden_ref.shape[0] // images
    hidden = attend_forward(
        step, seq, images, x_ref[...], gain_ref[2:3, :], [w.at[c] for c in range(3)], w.at[3], qkv_ref, mix_ref
    )
    hidden_ref[...] = hidden
    xn, _ = norm(hidden)
    u = (xn * gain_ref[3:4, :]).astype(bf16)
    u_ref[...] = u
    ud_ref[...] = nn(disp_ref[...], u).astype(bf16)
    probs = router_probs(u, router_ref[...], experts)
    probs_ref[...] = probs
    sums = jnp.sum(probs * live_ref[...], axis=0, keepdims=True)
    sum_ref[...] = jnp.concatenate([load_ref[...], sums, jnp.zeros((6, LANES), f32)], axis=0)


def split_rows(block, local):
    n, r, w = block.shape
    v = block.astype(f32)
    if r != local * CAP:
        v = v[:, :local * CAP]
    v = v.reshape(n, local, CAP, w)
    return [v[:, i].reshape(n * CAP, w) for i in range(local)]


def join_rows(parts, sources, block):
    local = len(parts)
    w = parts[0].shape[1]
    v = jnp.concatenate([p.reshape(sources, 1, CAP, w) for p in parts], axis=1).reshape(sources, local * CAP, w)
    if block != local * CAP:
        v = jnp.concatenate([v, jnp.zeros((sources, block - local * CAP, w), f32)], axis=1)
    return v


def gate_of(u, router, experts, e):
    lane = lax.broadcasted_iota(jnp.int32, (1, LANES), 1)
    return jnp.sum(jnp.where(lane == e, router_probs(u, router, experts), 0.0), axis=-1, keepdims=True)


def xor(a, b, bits):
    out = 0
    for i in range(bits):
        out = out + ((a // (1 << i) + b // (1 << i)) % 2) * (1 << i)
    return out


def expert_body(owners, shards, local, experts, group, uout_ref, dy_ref, router_ref, stat_ref, w1_hbm, w2_hbm,
                uin_ref, served_ref, duback_ref, dgback_ref, total_ref, dyx_ref,
                w1, w2, dusend, dgsend, statx, state, wsem, lsem, us, ur, ds_, dr, gs, gr, xs, xr, ss, sr, ys, yr):
    me, x = lax.axis_index("expert"), lax.axis_index("shard")
    bits = owners.bit_length() - 1
    barrier = pltpu.get_barrier_semaphore()

    def at(e, s):
        return dict(device_id=(e, s), device_id_type=pl.DeviceIdType.MESH)

    def each(lo, hi, f):
        lax.fori_loop(lo, hi, lambda k, c: (f(k), c)[1], 0)

    def peer(k):
        return xor(me, k, bits)

    each(1, owners, lambda k: pl.semaphore_signal(barrier, inc=1, **at(peer(k), x)))
    each(1, shards, lambda k: pl.semaphore_signal(barrier, inc=1, **at(me, (x + k) % shards)))
    weights = [pltpu.make_async_copy(w1_hbm, w1, wsem.at[0]), pltpu.make_async_copy(w2_hbm, w2, wsem.at[1])]
    start(weights)
    own = pltpu.make_async_copy(uout_ref.at[me], uin_ref.at[me], lsem.at[0])
    own.start()
    pl.semaphore_wait(barrier, owners - 1 + shards - 1)

    def send_u(k):
        return pltpu.make_async_remote_copy(uout_ref.at[peer(k)], uin_ref.at[me], us.at[k], ur.at[k], **at(peer(k), x))

    def send_du(k):
        return pltpu.make_async_remote_copy(dusend.at[peer(k)], duback_ref.at[me], ds_.at[k], dr.at[k], **at(peer(k), x))

    def send_dg(k):
        return pltpu.make_async_remote_copy(dgsend.at[peer(k)], dgback_ref.at[me], gs.at[k], gr.at[k], **at(peer(k), x))

    def send_statx(k):
        return pltpu.make_async_remote_copy(stat_ref, statx.at[k], xs.at[k], xr.at[k], **at(me, (x + k) % shards))

    def send_dyx(k):
        return pltpu.make_async_remote_copy(dy_ref, dyx_ref.at[k - 1], ys.at[k], yr.at[k], **at(me, (x + k) % shards))

    def send_state(k):
        return pltpu.make_async_remote_copy(state.at[0], state.at[k], ss.at[k], sr.at[k], **at(peer(k), x))

    each(1, shards, lambda k: send_statx(k).start())
    each(1, owners, lambda k: send_u(owners - k).start())
    each(1, shards, lambda k: send_dyx(k).start())
    each(1, shards, lambda k: send_statx(k).wait())
    sums = stat_ref[...]
    for k in range(1, shards):
        sums = sums + statx[k]
    state[0] = sums
    each(1, owners, lambda k: send_state(k).start())
    finish(weights)

    def work(g):
        base = xor(me // group, g, bits) * group
        rows = pl.ds(base, group)
        us_, dys = split_rows(uin_ref[rows], local), split_rows(dy_ref[rows], local)
        served, dus, prods = [], [], []
        for i in range(local):
            u, dy = us_[i].astype(bf16), dys[i]
            gate = gate_of(u, router_ref[...], experts, me * local + i)
            dsv = (gate * dy).astype(bf16)
            act, slope = gelu_pair(nn(u, w1[i]))
            out = nn(act.astype(bf16), w2[i])
            dz = (slope * nt(dsv, w2[i])).astype(bf16)
            dus.append(nt(dz, w1[i]))
            served.append(gate * out)
            prods.append(dy * out)
        block = uin_ref.shape[1]
        served_ref[rows] = join_rows(served, group, block).astype(bf16)
        dusend[rows] = join_rows(dus, group, block).astype(bf16)
        prod = join_rows(prods, group, block)
        ones = jnp.ones((8, prod.shape[2]), bf16)
        for j in range(group):
            hi = prod[j].astype(bf16)
            lo = (prod[j] - hi.astype(f32)).astype(bf16)
            dgsend[base + j, :, 0:block] = nt(ones, hi) + nt(ones, lo)

    def step(g):
        @pl.when(g == 0)
        def _():
            own.wait()

        for j in range(group):
            k = g * group + j
            if j == 0:
                pl.when(g > 0)(lambda k=k: send_u(k).wait_recv())
            else:
                send_u(k).wait_recv()
        work(g)
        for j in range(group):
            k = g * group + j
            if j == 0:
                @pl.when(g > 0)
                def _(k=k):
                    send_du(k).start()
                    send_dg(k).start()
            else:
                send_du(k).start()
                send_dg(k).start()

    each(0, owners // group, step)
    backs = [pltpu.make_async_copy(dusend.at[me], duback_ref.at[me], lsem.at[0]),
             pltpu.make_async_copy(dgsend.at[me], dgback_ref.at[me], lsem.at[1])]
    start(backs)
    each(1, owners, lambda k: send_state(k).wait())
    total = state[0]
    for k in range(1, owners):
        total = total + state[k]
    total_ref[...] = total
    each(1, owners, lambda k: send_u(k).wait_send())
    finish(backs)
    each(1, shards, lambda k: send_dyx(k).wait())
    each(1, owners, lambda k: send_du(k).wait())
    each(1, owners, lambda k: send_dg(k).wait())


def expert_grad_body(pieces, experts, *refs):
    us, dys = refs[:pieces], refs[pieces:2 * pieces]
    router_ref, w1_ref, w2_ref, g1_ref, g2_ref, urow, drow, stage, sems = refs[2 * pieces:]
    local = pl.num_programs(0)
    e = lax.axis_index("expert") * local + pl.program_id(0)

    @pl.when((pl.program_id(0) == 0) & (pl.program_id(1) == 0))
    def _():
        todo = [(us[i], urow, i) for i in range(pieces)] + [(dys[i], drow, i) for i in range(pieces)]
        copies = [pltpu.make_async_copy(r, stage.at[n % 2], sems.at[n % 2]) for n, (r, _, _) in enumerate(todo)]
        copies[0].start()
        for n, (_, to, i) in enumerate(todo):
            if n + 1 < len(todo):
                copies[n + 1].start()
            copies[n].wait()
            for j, v in enumerate(split_rows(stage[n % 2], urow.shape[1])):
                to[i, j] = v.astype(bf16)

    at = pl.program_id(0)
    for i in range(pieces):
        u = urow[i, at]
        dy = drow[i, at]
        gate = gate_of(u, router_ref[...], experts, e)
        ds = (gate * dy.astype(f32)).astype(bf16)
        act, slope = gelu_pair(nn(u, w1_ref[0]))
        dz = (slope * nt(ds, w2_ref[0])).astype(bf16)
        g1 = tn(u, dz)
        g2 = tn(act.astype(bf16), ds)
        if i == 0:
            g1_ref[0] = g1
            g2_ref[0] = g2
        else:
            g1_ref[0] += g1
            g2_ref[0] += g2


def split3(v):
    hi = v.astype(bf16)
    r = v - hi.astype(f32)
    mid = r.astype(bf16)
    lo = (r - mid.astype(f32)).astype(bf16)
    return hi, mid, lo


def back2_body(split, images, seq, experts, dy_ref, u_ref, probs_ref, hidden_ref, x_ref, gain_ref, router_ref, aux_ref,
               stat_ref, live_ref, back_ref, ret_ref, dgate_ref, qkv_ref, mix_ref, *refs):
    n = split.count(2)
    pieces, (grad_ref, pack_ref, small_ref, w, sems, dmix_ref, dqkv_ref) = refs[:n], refs[n:]
    copies = split.copies(pieces, w, sems)
    start(copies)
    slots = back_ref.shape[1]
    owners = dgate_ref.shape[0]
    local = experts // owners
    block = slots // owners
    off = lax.broadcasted_iota(jnp.int32, (slots, LANES), 0).astype(f32) - slot_start(
        lax.broadcasted_iota(jnp.int32, (slots, LANES), 1), local, block)
    oe = lax.broadcasted_iota(jnp.int32, (owners, LANES), 0).astype(f32)
    ee = lax.broadcasted_iota(jnp.int32, (owners, LANES), 1).astype(f32)
    pick = ((ee >= oe * local) & (ee < oe * local + local)).astype(f32).astype(bf16)
    column = 0.0
    for part in split3(dgate_ref[:, 0, :]):
        column = column + tn(part, pick)
    table = jnp.where((off >= 0) & (off < CAP), jnp.concatenate([column[0:block]] * owners, axis=0), 0.0)
    lane = lax.broadcasted_iota(jnp.int32, (1, LANES), 1)
    stat = stat_ref[0:1, :]
    total = jnp.sum(jnp.where(lane == LANES - 1, stat, 0.0), axis=-1, keepdims=True)
    fraction = jnp.where(lane < experts, stat, 0.0) / (2.0 * total)
    loss = experts * jnp.sum(fraction * stat_ref[1:2, :] / total, axis=-1, keepdims=True)
    small_ref[LANES + 2:LANES + 3, :] = jnp.broadcast_to(loss, (1, small_ref.shape[1]))
    dprobs = (aux_ref[0, 0] * experts * fraction / total) * live_ref[...]
    for part in split3(table):
        dprobs = dprobs + nn(back_ref[...], part)
    probs = probs_ref[...]
    dlog = (probs * (dprobs - jnp.sum(probs * dprobs, axis=-1, keepdims=True))).astype(bf16)
    small_ref[0:LANES, :] = tn(dlog, u_ref[...])
    du = nn(back_ref[...], ret_ref[...]) + nt(dlog, router_ref[...])
    xn, rs = norm(hidden_ref[...])
    dv, dg = norm_back(du, xn, rs, gain_ref[3:4, :])
    small_ref[LANES:LANES + 1, :] = dg
    grad = dy_ref[...].astype(f32) + dv
    grad_ref[...] = grad
    finish(copies)
    step = hidden_ref.shape[0] // images
    dv, dg = attend_backward(
        step, seq, images, grad, x_ref[...], gain_ref[2:3, :], [w.at[c] for c in range(3)], w.at[3],
        qkv_ref, mix_ref, dmix_ref, dqkv_ref, pack_ref, 0,
    )
    small_ref[LANES + 1:LANES + 2, :] = dg
    grad_ref[...] += dv


def mlp_back_body(split, blocks, grad_ref, hidden_ref, gain_ref, act_ref, slope_ref, *refs):
    n = 2 * split.count(1)
    pieces, (out_ref, pack_ref, dgain_ref, w1, w2, sems, du_ref) = refs[:n], refs[n:]
    half = n // 2
    copies = split.copies(pieces[:half], w1, sems.at[0]) + split.copies(pieces[half:], w2, sems.at[1])
    start(copies)
    xn, rs = norm(hidden_ref[...])
    gain = gain_ref[1:2, :]
    u = (xn * gain).astype(bf16)
    grad = grad_ref[...]
    low = grad.astype(bf16)
    finish(copies)
    width = grad.shape[1]
    ff = act_ref.shape[1]
    shards = pack_ref.shape[0]
    part, fpart = width // shards, ff // shards
    blocks = ff // width
    base = part * blocks
    for b in range(blocks):
        at = slice(b * width, (b + 1) * width)
        dz = (slope_ref[:, at].astype(f32) * nt(low, w2[0, at, :])).astype(bf16)
        d = nt(dz, w1[0, :, at])
        if b == 0:
            du_ref[...] = d
        else:
            du_ref[...] += d
        gin = tn(u, dz).astype(bf16)
        for s in range(shards):
            pack_ref[s, b * part:(b + 1) * part, :] = gin[s * part:(s + 1) * part]
        gout = tn(act_ref[:, at], low).astype(bf16)
        per = min(width, fpart)
        for j in range(width // per):
            row = b * width + j * per
            s, off = row // fpart, row % fpart
            pack_ref[s, base + off:base + off + per, :] = gout[j * per:(j + 1) * per]
    dv, dg = norm_back(du_ref[...], xn, rs, gain)
    dgain_ref[...] = dg
    out_ref[...] = grad + dv


def back1_body(split, images, seq, experts, grad_ref, tok_ref, gain_ref, qkv_ref, mix_ref, small_ref, dg2_ref, *refs):
    n = split.count(2)
    pieces, (out_ref, pack_ref, w, sems, x_ref, dmix_ref, dqkv_ref) = refs[:n], refs[n:]
    copies = split.copies(pieces, w, sems)
    start(copies)
    step = x_ref.shape[0] // images
    pad_store(x_ref, lambda i: tok_ref[i], images, seq, step)
    finish(copies)
    width = x_ref.shape[1]
    dv, dg1 = attend_backward(
        step, seq, images, grad_ref[...], x_ref[...], gain_ref[0:1, :], [w.at[c] for c in range(3)], w.at[3],
        qkv_ref, mix_ref, dmix_ref, dqkv_ref, pack_ref, 0,
    )
    x_ref[...] = grad_ref[...] + dv
    for i in range(images):
        out_ref[i] = x_ref[i * step:i * step + seq, :]
    shards = pack_ref.shape[0]
    part = width // shards
    base = 4 * part
    gains = jnp.concatenate(
        [dg1, dg2_ref[...], small_ref[LANES + 1:LANES + 2, :], small_ref[LANES:LANES + 1, :], jnp.zeros((28, width), f32)], axis=0
    )
    both = jnp.concatenate([small_ref[0:32, :], gains], axis=0).astype(bf16)
    for s in range(shards):
        one = both[:, s * part:(s + 1) * part]
        pack_ref[s, base:base + 64, :] = jnp.concatenate([one, jnp.zeros((64, width - part), bf16)], axis=1)


def output_body(images, seq, hidden_ref, back_ref, ret_ref, live_ref, out_ref, tmp_ref):
    step = hidden_ref.shape[0] // images
    tmp_ref[...] = (hidden_ref[...] + nn(back_ref[...], ret_ref[...])) * live_ref[...]
    for i in range(images):
        out_ref[i] = tmp_ref[i * step:i * step + seq, :].astype(bf16)


def swap(owners, bit):
    return [(i, i ^ (1 << bit)) for i in range(owners)]


def reduce_all(g, owners, shards):
    me = lax.axis_index("expert")
    bits = owners.bit_length() - 1

    def add(a, b):
        return (a.astype(f32) + b.astype(f32)).astype(bf16)

    def fold(v, bit, axis):
        own = (me >> bit) & 1
        half = v.shape[axis] // 2
        keep = lax.dynamic_slice_in_dim(v, own * half, half, axis)
        send = lax.dynamic_slice_in_dim(v, (1 - own) * half, half, axis)
        return add(keep, lax.ppermute(send, "expert", swap(owners, bit)))

    v = fold(g, 0, 1)
    if shards == 2:
        x = lax.axis_index("shard")
        keep = lax.dynamic_index_in_dim(v, x, 0, keepdims=False)
        send = lax.dynamic_index_in_dim(v, 1 - x, 0, keepdims=False)
        v = add(keep, lax.ppermute(send, "shard", [(0, 1), (1, 0)]))
    else:
        v = lax.psum_scatter(v, "shard", scatter_dimension=0, tiled=True)[0]
    for bit in range(1, bits):
        v = fold(v, bit, 0)
    for bit in reversed(range(bits)):
        own = (me >> bit) & 1
        other = lax.ppermute(v, "expert", swap(owners, bit))
        v = jnp.where(own == 0, jnp.concatenate([v, other]), jnp.concatenate([other, v]))
    return v


def per_device(
    owners, shards, tokens, cotangent, routes, counts, aux_weight, attn_qkv1, attn_out1, mlp_in, mlp_out, gains1,
    attn_qkv2, attn_out2, router, gains2, expert_in, expert_out,
):
    images, seq, width = tokens.shape
    step = padded(seq)
    rows = images * step
    experts = router.shape[1]
    local = expert_in.shape[0]
    ff = mlp_in.shape[1]
    block_rows = -(-local * CAP // 16) * 16
    slots = owners * block_rows
    split = Split(shards)
    expert_swap = functools.partial(lax.all_to_all, axis_name="expert", split_axis=0, concat_axis=0, tiled=True)

    within = jnp.arange(step, dtype=jnp.int32) < seq
    live = ((jnp.arange(images, dtype=jnp.int32)[:, None] < counts[0]) & within[None, :]).reshape(rows)
    live = live.astype(f32)
    routes_pad = jnp.pad(routes, ((0, 0), (0, step - seq), (0, 0)), constant_values=-1).reshape(rows, 2)
    lanes = jnp.arange(LANES, dtype=jnp.int32)
    loads = jnp.sum(((routes_pad[:, :, None] == lanes) & (live[:, None, None] > 0)).astype(f32), axis=(0, 1))
    loads = jnp.where(lanes == LANES - 1, jnp.sum(live), loads)
    live_col = live[:, None]

    w_one = split.gather([attn_qkv1, attn_out1[None]])
    w_up = split.gather([mlp_in[None]])
    w_down = split.gather([mlp_out[None]])
    w_two = split.gather([attn_qkv2, attn_out2[None]])
    gains = jnp.concatenate([gains1, gains2])
    if shards == 2:
        x = lax.axis_index("shard")
        other = lax.ppermute(gains, "shard", [(0, 1), (1, 0)])
        gains = jnp.where(x == 0, jnp.concatenate([gains, other], 1), jnp.concatenate([other, gains], 1))
        other = lax.ppermute(router, "shard", [(0, 1), (1, 0)])
        router_full = jnp.where(x == 0, jnp.concatenate([router, other]), jnp.concatenate([other, router]))
    else:
        gains = lax.all_gather(gains, "shard", axis=1, tiled=True)
        router_full = lax.all_gather(router, "shard", axis=0, tiled=True)
    gains = gains.astype(f32)
    router_full = jnp.pad(router_full, ((0, 0), (0, LANES - experts)))

    dy, dy_out, disp, back = call(
        functools.partial(route_body, images, seq, local, block_rows),
        [sds((rows, width), bf16), sds((slots, width), bf16), sds((slots, rows), bf16), sds((rows, slots), bf16)],
        [routes_pad, routes_pad.T, live_col, cotangent], flops=2e9, nbytes=6e6,
    )
    block = (owners, block_rows, width)
    dy_in = expert_swap(dy_out.reshape(block))

    sem = pltpu.SemaphoreType.DMA
    attn_scratch = [pltpu.VMEM((4, width, width), bf16), sem((4,))]
    mlp_scratch = [pltpu.VMEM((1, width, ff), bf16), pltpu.VMEM((1, ff, width), bf16), sem((2, 4))]

    def specs(n, ins):
        return [VM] * n + [ANY] * (len(ins) - n)

    ins = [tokens, gains] + w_one
    hidden, qkv_one, mix_one = call(
        functools.partial(block1_body, split, images, seq),
        [sds((rows, width), f32), sds((rows, 3 * width), bf16), sds((rows, width), bf16)],
        ins, attn_scratch, specs(2, ins), flops=4e9, nbytes=8e6,
    )
    ins = [hidden, gains] + w_up + w_down
    block_out, act, slope = call(
        functools.partial(mlp_body, split, 4),
        [sds((rows, width), f32), sds((rows, ff), bf16), sds((rows, ff), bf16)],
        ins, mlp_scratch, specs(2, ins), flops=6e9, nbytes=12e6,
    )
    ins = [block_out, gains, router_full, disp, live_col, loads[None, :]] + w_two
    hidden_two, qkv_two, mix_two, u_two, probs, stat, u_out = call(
        functools.partial(block2_body, split, images, seq, experts),
        [sds((rows, width), f32), sds((rows, 3 * width), bf16), sds((rows, width), bf16), sds((rows, width), bf16),
         sds((rows, LANES), f32), sds((8, LANES), f32), sds((slots, width), bf16)],
        ins, attn_scratch, specs(6, ins), flops=5e9, nbytes=10e6,
    )

    group = min(4, owners)
    u_in, served, du_back, dgate_back, stat, dy_far = pl.pallas_call(
        functools.partial(expert_body, owners, shards, local, experts, group),
        out_shape=[sds(block, bf16), sds(block, bf16), sds(block, bf16), sds((owners, 8, LANES), f32), sds((8, LANES), f32),
                   sds((shards - 1,) + block, bf16)],
        in_specs=[VM] * 4 + [ANY] * 2,
        out_specs=[VM] * 6,
        scratch_shapes=[
            pltpu.VMEM((local, width, ff), bf16), pltpu.VMEM((local, ff, width), bf16), pltpu.VMEM(block, bf16),
            pltpu.VMEM((owners, 8, LANES), f32), pltpu.VMEM((shards, 8, LANES), f32), pltpu.VMEM((owners, 8, LANES), f32),
            sem((2,)), sem((2,)),
        ] + [sem((owners,))] * 6 + [sem((shards,))] * 2 + [sem((owners,))] * 2 + [sem((shards,))] * 2,
        compiler_params=pltpu.CompilerParams(vmem_limit_bytes=VMEM_BYTES, collective_id=0, has_side_effects=True),
        cost_estimate=pl.CostEstimate(flops=int(11e9), bytes_accessed=int(15e6), transcendentals=0),
    )(u_out.reshape(block), dy_in, router_full, stat, expert_in, expert_out)
    served_back = expert_swap(served).reshape(slots, width)

    if shards == 2:
        us = [u_in, lax.ppermute(u_in, "shard", [(0, 1), (1, 0)])]
    else:
        far = lax.all_gather(u_in, "shard")
        us = [u_in] + [lax.dynamic_index_in_dim(far, (lax.axis_index("shard") + shards - k) % shards, 0, False) for k in range(1, shards)]
    dys = [dy_in] + [dy_far[k] for k in range(shards - 1)]
    parts = 4
    wide = ff // parts
    up_spec = pl.BlockSpec((1, width, wide), lambda e, f: (e, 0, f))
    down_spec = pl.BlockSpec((1, wide, width), lambda e, f: (e, f, 0))
    grad_e_in, grad_e_out = pl.pallas_call(
        functools.partial(expert_grad_body, shards, experts),
        grid=(local, parts),
        out_shape=[sds((local, width, ff), f32), sds((local, ff, width), f32)],
        in_specs=[ANY] * (2 * shards) + [VM, up_spec, down_spec],
        out_specs=[up_spec, down_spec],
        scratch_shapes=[pltpu.VMEM((shards, local, owners * CAP, width), bf16)] * 2 + [pltpu.VMEM((2,) + block, bf16), sem((2,))],
        compiler_params=pltpu.CompilerParams(vmem_limit_bytes=VMEM_BYTES),
        cost_estimate=pl.CostEstimate(flops=int(27e9), bytes_accessed=int(40e6), transcendentals=0),
    )(*us, *dys, router_full, expert_in, expert_out)

    part = width // shards
    back_scratch = [pltpu.VMEM((rows, width), bf16), pltpu.VMEM((rows, 3 * width), bf16)]
    ins = [dy, u_two, probs, hidden_two, block_out, gains, router_full, aux_weight.reshape(1, 1), stat, live_col, back,
           du_back.reshape(slots, width), dgate_back,
           qkv_two, mix_two]
    n = len(ins)
    ins = ins + w_two
    grad_block, pack_two, small = call(
        functools.partial(back2_body, split, images, seq, experts),
        [sds((rows, width), f32), sds((shards, 4 * part, width), bf16), sds((LANES + 8, width), f32)],
        ins, attn_scratch + back_scratch, specs(n, ins), flops=9e9, nbytes=16e6,
    )
    balance_loss = small[LANES + 2, 0]
    late = reduce_all(pack_two, owners, shards)
    ins = [grad_block, hidden, gains, act, slope] + w_up + w_down
    grad_hidden, pack_mlp, dg_two = call(
        functools.partial(mlp_back_body, split, 4),
        [sds((rows, width), f32), sds((shards, part * (ff // width) + ff // shards, width), bf16), sds((1, width), f32)],
        ins, mlp_scratch + [pltpu.VMEM((rows, width), f32)], specs(5, ins), flops=11e9, nbytes=16e6,
    )
    middle = reduce_all(pack_mlp, owners, shards)
    ins = [grad_hidden, tokens, gains, qkv_one, mix_one, small, dg_two] + w_one
    grad_tokens, pack_one = call(
        functools.partial(back1_body, split, images, seq, experts),
        [sds((images, seq, width), f32), sds((shards, 4 * part + 64, width), bf16)],
        ins, attn_scratch + [pltpu.VMEM((rows, width), f32)] + back_scratch, specs(7, ins), flops=9e9, nbytes=14e6,
    )
    early = reduce_all(pack_one, owners, shards)
    (output,) = call(
        functools.partial(output_body, images, seq), [sds((images, seq, width), bf16)],
        [hidden_two, back, served_back, live_col], [pltpu.VMEM((rows, width), f32)], flops=1e9, nbytes=5e6,
    )

    late, middle, early = late.astype(f32), middle.astype(f32), early.astype(f32)
    up = middle[:part * (ff // width)].reshape(ff // width, part, width).transpose(1, 0, 2).reshape(part, ff)
    tail = early[4 * part:, :part]
    return (
        output,
        balance_loss,
        grad_tokens,
        early[:3 * part].reshape(3, part, width),
        early[3 * part:4 * part],
        up,
        middle[part * (ff // width):],
        tail[32:34],
        late[:3 * part].reshape(3, part, width),
        late[3 * part:],
        tail[:experts].T,
        tail[34:36],
        grad_e_in,
        grad_e_out,
    )


def solution(mesh):
    owners, shards = mesh.shape["expert"], mesh.shape["shard"]
    both = ("expert", "shard")
    return jax.shard_map(
        functools.partial(per_device, owners, shards),
        mesh=mesh,
        in_specs=(
            P(both, None, None), P(both, None, None), P(both, None, None), P(both), P(),
            P(None, "shard", None), P("shard", None), P("shard", None), P("shard", None), P(None, "shard"),
            P(None, "shard", None), P("shard", None), P("shard", None), P(None, "shard"),
            P("expert", None, None), P("expert", None, None),
        ),
        out_specs=(
            P(both, None, None), P(), P(both, None, None),
            P(None, "shard", None), P("shard", None), P("shard", None), P("shard", None), P(None, "shard"),
            P(None, "shard", None), P("shard", None), P("shard", None), P(None, "shard"),
            P("expert", None, None), P("expert", None, None),
        ),
        check_vma=False,
    )
```

time: 1030 us -> 436 us (0.42)
  waiting for transfers between devices: 382 us -> 95.9 us
  blocking collectives: 267 us -> 0 us
  Pallas kernels: 0 us -> 211 us
  matrix products: 157 us -> 0 us
  local copies, waits for them, and re-layouts: 117 us -> 29.6 us
  starting transfers between devices: 8.75 us -> 69.6 us
  other arithmetic: 68.4 us -> 22.7 us
  between operations: 20.1 us -> 2.84 us
    psum x2 -> x0, waiting for transfers between devices: 236 us -> none  [the longest x1 130 us: per_device(): lax.psum(grad_ein.astype(jnp.bfloat16), 'shard').astype(jnp.float32)]
    pallas_call x0 -> x10, Pallas kernels: none -> 211 us  [the longest x8 97.5 us: call(): pl.pallas_call(body, out_shape=outs, in_specs=specs or [VM] * len(ins), o...]
    dot_general x39 -> x0, matrix products: 157 us -> none  [the longest x1 28.4 us: serve_rows(): jnp.einsum('slcd,ldf->slcf', received, expert_in, preferred_element_type=...]
    psum x3 -> x0, blocking collectives: 150 us -> none  [the longest x2 90.1 us: per_device(): lax.psum((load_local, prob_local, token_local), ('expert', 'shard'))]
    ppermute x0 -> x38, waiting for transfers between devices: none -> 95.9 us  [the longest x3 36.6 us: reduce_all(): v = add(keep, lax.ppermute(send, 'shard', [(0, 1), (1, 0)]))]
    reduce_scatter x7 -> x0, waiting for transfers between devices: 83.6 us -> none  [the longest x1 34.7 us: per_device(): lax.psum_scatter(grad_w_up.astype(jnp.bfloat16), 'shard', scatter_dimensi...]
    all_to_all x2 -> x0, blocking collectives: 76.5 us -> none  [the longest x1 39.5 us: per_device(): lax.all_to_all(grad_send, 'expert', split_axis=0, concat_axis=0, tiled=True)]
    ppermute x0 -> x38, starting transfers between devices: none -> 58.6 us  [the longest x12 36.5 us: fold(): return add(keep, lax.ppermute(send, 'expert', swap(owners, bit)))]
  transfers between devices with their start and end apart: 17 -> 40, of which waited for: 9 -> 13; matrix products, arithmetic and copies ran while one was open for 17% -> 9% of each run, Pallas kernels for 0% -> 28%
where the time goes in v1:
time: 436 us; the launch traced here: 432 us
  Pallas kernels  211 us (48%)
  waiting for transfers between devices  95.9 us (22%)
  starting transfers between devices  69.6 us (16%)
  local copies, waits for them, and re-layouts  29.6 us (7%)
  other arithmetic  22.7 us (5%)
    pallas_call x8, Pallas kernels, call(): pl.pallas_call(body, out_shape=outs, in_specs=specs or [VM] * len(ins), o...  97.5 us
    pallas_call x1, Pallas kernels, per_device(): pl.pallas_call(functools.partial(expert_body, owners, shards, local, expe...  67.7 us
    pallas_call x1, Pallas kernels, per_device(): pl.pallas_call(functools.partial(expert_grad_body, shards, experts), grid...  45.8 us
    ppermute x3, waiting for transfers between devices, reduce_all(): v = add(keep, lax.ppermute(send, 'shard', [(0, 1), (1, 0)]))  36.6 us
    ppermute x12, starting transfers between devices, fold(): return add(keep, lax.ppermute(send, 'expert', swap(owners, bit)))  36.5 us
    ppermute x12, waiting for transfers between devices, reduce_all(): other = lax.ppermute(v, 'expert', swap(owners, bit))  23.2 us
    ppermute x4, waiting for transfers between devices, gather(): far = lax.ppermute(send, 'shard', [(0, 1), (1, 0)])  14.5 us
    ppermute x12, waiting for transfers between devices, fold(): return add(keep, lax.ppermute(send, 'expert', swap(owners, bit)))  14.1 us
  transfers between devices with their start and end apart: 40, of which 13 were waited for; matrix products, arithmetic and copies ran while one was open for 9% of the time, Pallas kernels for 28%

profile of v1, /device:TPU:0, one launch (start us, length us, event | category | flops | bytes accessed | tf_op | source)
XLA Modules:
  0.0 431.8 jit_solution(1726782612402994021)
XLA Ops:
  1.5 2.9 collective-permute-start
  12.4 6.1 %shard_map.265 = (bf16[624,512]{1,0:T(8,128)(2,1)}, bf16[1280,512]{1,0:T(8,128)(2,1)}, bf16[1280,624]{1,0:T(8,128)(2,1)}, bf16[624,1280]{1,0:T(8,128)(2,1)}) custom-call(s32[624,2]{1,0:T(8,128)} %copy.61.r_ref, s32[2,624]{1,0:T(2,128)} %bitcast.65, f32[624,1]{1,0:T(8,128)} %reshape.148.live_ref, bf16[3,197,512]{2,1,0:T(8,128)(2,1)} %cot_ref.1), custom_call_target="tpu_custom_call" | custom-call | flops 2000000000 | bytes 6000000 | tf_op jit(solution)/shard_map/pallas_call | solution.py:122
  18.5 7.1 %all-to-all-start = ((bf16[16,80,512]{2,1,0:T(8,128)(2,1)}), bf16[16,80,512]{2,1,0:T(8,128)(2,1)S(1)}, u32[]{:S(2)}, u32[]{:S(2)}) async-start(bf16[16,80,512]{2,1,0:T(8,128)(2,1)} %bitcast.56), calls=%async_computation | async-start | bytes 2621440 | tf_op jit(solution)/shard_map/all_to_all | solution.py:724
  28.4 14.5 %collective-permute-done.1.refs_2_ = bf16[4,128,512]{2,1,0:T(8,128)(2,1)} collective-permute-done((bf16[4,128,512]{2,1,0:T(8,128)(2,1)S(1)}, bf16[4,128,512]{2,1,0:T(8,128)(2,1)}, u32[]{:S(2)}, u32[]{:S(2)}) %collective-permute-start.1) | collective-permute-done | bytes 524320 | tf_op jit(solution)/shard_map/ppermute | solution.py:79
  45.5 7.5 %collective-permute-done.7 = bf16[256,32]{0,1:T(8,128)(2,1)S(1)} collective-permute-done((bf16[256,32]{0,1:T(8,128)(2,1)S(1)}, bf16[256,32]{0,1:T(8,128)(2,1)S(1)}, u32[]{:S(2)}, u32[]{:S(2)}) %collective-permute-start.7) | collective-permute-done | bytes 16416 | tf_op jit(solution)/shard_map/ppermute | solution.py:710
  54.7 9.8 %shard_map.263 = (f32[624,512]{1,0:T(8,128)}, bf16[624,1536]{1,0:T(8,128)(2,1)}, bf16[624,512]{1,0:T(8,128)(2,1)}) custom-call(bf16[3,197,512]{2,1,0:T(8,128)(2,1)} %tok_ref.1, f32[4,512]{1,0:T(4,128)} %fusion.7.gain_ref, bf16[3,256,512]{2,1,0:T(8,128)(2,1)} %refs_0_.7, bf16[1,256,512]{2,1,0:T(8,128)(2,1)} %bitcast.63, ...), custom_call_target="tpu_custom_call" | custom-call | flops 4000000000 | bytes 8000000 | tf_op jit(solution)/shard_map/pallas_call | solution.py:122
  65.4 12.1 %shard_map.264 = (f32[624,512]{1,0:T(8,128)}, bf16[624,2048]{1,0:T(8,128)(2,1)}, bf16[624,2048]{1,0:T(8,128)(2,1)}) custom-call(f32[624,512]{1,0:T(8,128)} %get-tuple-element.47.hidden_ref, f32[4,512]{1,0:T(4,128)} %fusion.7.gain_ref, bf16[1,256,2048]{2,1,0:T(8,128)(2,1)} %bitcast.57, bf16[1,128,2048]{2,1,0:T(8,128)(2,1)} %collective-permute-done.3.refs_1_, ...), custom_call_target="tpu_custom_call" | custom-call | flops 6000000000 | bytes 12000000 | tf_op jit(solution)/shard_map/pallas_call | solution.py:122
  78.3 12.8 %shard_map.266 = (f32[624,512]{1,0:T(8,128)}, bf16[624,1536]{1,0:T(8,128)(2,1)}, bf16[624,512]{1,0:T(8,128)(2,1)}, bf16[624,512]{1,0:T(8,128)(2,1)}, f32[624,128...) custom-call(f32[624,512]{1,0:T(8,128)} %get-tuple-element.48.x_ref, f32[4,512]{1,0:T(4,128)} %fusion.7.gain_ref, ...), custom_call_target="tpu_custom_call" | custom-call | flops 5000000000 | bytes 10000000 | tf_op jit(solution)/shard_map/pallas_call | solution.py:122
  92.2 67.7 %shard_map.267 = (bf16[16,80,512]{2,1,0:T(8,128)(2,1)}, bf16[16,80,512]{2,1,0:T(8,128)(2,1)}, bf16[16,80,512]{2,1,0:T(8,128)(2,1)}, f32[16,8,128]{2,1,0:T(8,128)...) custom-call(bf16[16,80,512]{2,1,0:T(8,128)(2,1)} %bitcast.68, bf16[16,80,512]{2,1,0:T(8,128)(2,1)} %copy-done.5, ...), custom_call_target="tpu_custom_call" | custom-call | flops 11000000512 | bytes 15000000 | tf_op jit(solution)/shard_map/pallas_call | solution.py:754
  160.0 21.9 %shard_map.269 = (f32[624,512]{1,0:T(8,128)}, bf16[2,1024,512]{2,1,0:T(8,128)(2,1)}, f32[136,512]{1,0:T(8,128)}) custom-call(bf16[624,512]{1,0:T(8,128)(2,1)} %get-tuple-element.56.dy_ref, bf16[624,512]{1,0:T(8,128)(2,1)} %get-tuple-element.57.u_ref, f32[624,128]{1,0:T(8,128)} %get-tuple-element.58.probs_ref, f32[624,512]{1,0:T(8,128)} %get-tuple-element.50.hidden_ref, ...), custom_call_target="tpu_custom_call" | custom-call | flops 8999999488 | bytes 16000000 | tf_op jit(solution)/shard_map/pallas_call | solution.py:122
  181.9 2.3 constant_dynamic-slice_fusion.3
  185.8 13.8 %shard_map.270 = (f32[624,512]{1,0:T(8,128)}, bf16[2,2048,512]{2,1,0:T(8,128)(2,1)}, f32[1,512]{1,0:T(1,128)}) custom-call(f32[624,512]{1,0:T(8,128)} %get-tuple-element.65.grad_ref, f32[624,512]{1,0:T(8,128)} %get-tuple-element.47.hidden_ref, f32[4,512]{1,0:T(4,128)} %fusion.7.gain_ref, bf16[624,2048]{1,0:T(8,128)(2,1)} %get-tuple-element.66.act_ref, ...), custom_call_target="tpu_custom_call" | custom-call | flops 11000000512 | bytes 16000000 | tf_op jit(solution)/shard_map/pallas_call | solution.py:122
  199.6 3.1 constant_dynamic-slice_fusion.7
  202.6 17.0 %shard_map.271 = (f32[3,197,512]{2,1,0:T(8,128)}, bf16[2,1088,512]{2,1,0:T(8,128)(2,1)}) custom-call(f32[624,512]{1,0:T(8,128)} %get-tuple-element.68.grad_ref, bf16[3,197,512]{2,1,0:T(8,128)(2,1)} %tok_ref.1, f32[4,512]{1,0:T(4,128)} %fusion.7.gain_ref, bf16[624,1536]{1,0:T(8,128)(2,1)} %get-tuple-element.69.qkv_ref, ...), custom_call_target="tpu_custom_call" | custom-call | flops 8999999488 | bytes 14000000 | tf_op jit(solution)/shard_map/pallas_call | solution.py:122
  224.2 2.3 collective-permute-start.29
  235.0 4.6 %collective-permute-done.29 = bf16[512,512]{1,0:T(8,128)(2,1)} collective-permute-done((bf16[512,512]{1,0:T(8,128)(2,1)}, bf16[512,512]{1,0:T(8,128)(2,1)}, u32[]{:S(2)}, u32[]{:S(2)}) %collective-permute-start.29) | collective-permute-done | bytes 524320 | tf_op jit(solution)/shard_map/ppermute | solution.py:665
  242.1 31.9 %collective-permute-done.11 = bf16[544,512]{1,0:T(8,128)(2,1)} collective-permute-done((bf16[544,512]{1,0:T(8,128)(2,1)}, bf16[544,512]{1,0:T(8,128)(2,1)}, u32[]{:S(2)}, u32[]{:S(2)}) %collective-permute-start.11) | collective-permute-done | bytes 557088 | tf_op jit(solution)/shard_map/ppermute | solution.py:665
  279.1 8.0 %collective-permute-start.31 = (bf16[128,512]{1,0:T(8,128)(2,1)S(1)}, bf16[128,512]{1,0:T(8,128)(2,1)S(1)}, u32[]{:S(2)}, u32[]{:S(2)}) collective-permute-start(bf16[128,512]{1,0:T(8,128)(2,1)S(1)} %constant_dynamic-slice_fusion.1), channel_id=1, source_target_pairs={{0,8},{2,10},{4,12},{6,14},{8,0},{10,2},{12,4},{14,6},{16,24},{18,... | collective-permute-start | bytes 393224 | tf_op jit(solution)/shard_map/ppermute | solution.py:658
  287.3 5.8 %collective-permute-start.13 = (bf16[136,512]{1,0:T(8,128)(2,1)S(1)}, bf16[136,512]{1,0:T(8,128)(2,1)S(1)}, u32[]{:S(2)}, u32[]{:S(2)}) collective-permute-start(bf16[136,512]{1,0:T(8,128)(2,1)S(1)} %constant_dynamic-slice_fusion.9), channel_id=1, source_target_pairs={{0,8},{2,10},{4,12},{6,14},{8,0},{10,2},{12,4},{14,6},{16,24},{18,... | collective-permute-start | bytes 417800 | tf_op jit(solution)/shard_map/ppermute | solution.py:658
  294.8 7.0 %collective-permute-start.22 = (bf16[256,512]{1,0:T(8,128)(2,1)S(1)}, bf16[256,512]{1,0:T(8,128)(2,1)S(1)}, u32[]{:S(2)}, u32[]{:S(2)}) collective-permute-start(bf16[256,512]{1,0:T(8,128)(2,1)S(1)} %constant_dynamic-slice_fusion.5), channel_id=1, source_target_pairs={{0,8},{2,10},{4,12},{6,14},{8,0},{10,2},{12,4},{14,6},{16,24},{18,... | collective-permute-start | bytes 786440 | tf_op jit(solution)/shard_map/ppermute | solution.py:658
  303.8 3.3 collective-permute-done.22
  307.2 5.2 %collective-permute-start.23 = (bf16[128,512]{1,0:T(8,128)(2,1)S(1)}, bf16[128,512]{1,0:T(8,128)(2,1)S(1)}, u32[]{:S(2)}, u32[]{:S(2)}) collective-permute-start(bf16[128,512]{1,0:T(8,128)(2,1)S(1)} %constant_dynamic-slice_fusion.4), channel_id=1, source_target_pairs={{0,16},{2,18},{4,20},{6,22},{8,24},{10,26},{12,28},{14,30},{16,0},... | collective-permute-start | bytes 393224 | tf_op jit(solution)/shard_map/ppermute | solution.py:658
  312.6 7.6 %collective-permute-done.23 = bf16[128,512]{1,0:T(8,128)(2,1)S(1)} collective-permute-done((bf16[128,512]{1,0:T(8,128)(2,1)S(1)}, bf16[128,512]{1,0:T(8,128)(2,1)S(1)}, u32[]{:S(2)}, u32[]{:S(2)}) %collective-permute-start.23) | collective-permute-done | bytes 131104 | tf_op jit(solution)/shard_map/ppermute | solution.py:658
  320.4 3.0 collective-permute-start.14
  323.4 4.3 collective-permute-done.24
  330.3 2.4 collective-permute-start.34
  332.7 2.3 collective-permute-done.15
  343.0 4.0 all-to-all-start.1
  346.9 9.8 %collective-permute-done.35 = bf16[256,512]{1,0:T(8,128)(2,1)S(1)} collective-permute-done((bf16[256,512]{1,0:T(8,128)(2,1)S(1)}, bf16[256,512]{1,0:T(8,128)(2,1)S(1)}, u32[]{:S(2)}, u32[]{:S(2)}) %collective-permute-start.35) | collective-permute-done | bytes 262176 | tf_op jit(solution)/shard_map/ppermute | solution.py:672
  357.7 6.0 %collective-permute-done.17 = bf16[272,512]{1,0:T(8,128)(2,1)S(1)} collective-permute-done((bf16[272,512]{1,0:T(8,128)(2,1)S(1)}, bf16[272,512]{1,0:T(8,128)(2,1)S(1)}, u32[]{:S(2)}, u32[]{:S(2)}) %collective-permute-start.17) | collective-permute-done | bytes 278560 | tf_op jit(solution)/shard_map/ppermute | solution.py:672
  366.2 45.8 %shard_map.272 = (f32[2,512,2048]{2,1,0:T(8,128)}, f32[2,2048,512]{2,1,0:T(8,128)}) custom-call(bf16[16,80,512]{2,1,0:T(8,128)(2,1)} %get-tuple-element.76.refs_0_, bf16[16,80,512]{2,1,0:T(8,128)(2,1)} %collective-permute-done.37.refs_1_, bf16[16,80,512]{2,1,0:T(8,128)(2,1)} %copy-done.5, bf16[16,80,512]{2,1,0:T(8,128)(2,1)} %bitcast.66, ...), custom_call_target="tpu_custom_call" | custom-call | flops 27000000512 | bytes 40000000 | tf_op jit(solution)/shard_map/pallas_call | solution.py:780
  413.1 4.1 shard_map.268
  (174 shorter events, 73.0 us)
Async XLA Ops:
  1.5 43.3 %collective-permute-start = (bf16[4,256]{1,0:T(4,128)(2,1)S(1)}, bf16[4,256]{1,0:T(4,128)(2,1)S(1)}, u32[]{:S(2)}, u32[]{:S(2)}) collective-permute-start(bf16[4,256]{1,0:T(4,128)(2,1)S(1)} %pad_maximum_fusion.4), channel_id=1, source_target_pairs={{0,1},{1,0},{2,3},{3,2},{4,5},{5,4},{6,7},{7,6},{8,9},{9,8},{10,11... | collective-permute-start | bytes 6152 | tf_op jit(solution)/shard_map/ppermute | solution.py:708
  5.5 47.8 %collective-permute-start.5 = (bf16[1,512,512]{2,1,0:T(8,128)(2,1)S(1)}, bf16[1,512,512]{2,1,0:T(8,128)(2,1)}, u32[]{:S(2)}, u32[]{:S(2)}) collective-permute-start(bf16[1,512,512]{2,1,0:T(8,128)(2,1)S(1)} %dynamic-slice_bitcast_fusion.3), channel_id=1, source_target_pairs={{0,1},{1,0},{2,3},{3,2},{4,5},{5,4},{6,7},{7,6},{8,9},{9,8},{10,11... | collective-permute-start | bytes 1572872 | tf_op jit(solution)/shard_map/ppermute | solution.py:79
  7.5 45.9 %collective-permute-start.3 = (bf16[1,128,2048]{2,1,0:T(8,128)(2,1)}, bf16[1,128,2048]{2,1,0:T(8,128)(2,1)}, u32[]{:S(2)}, u32[]{:S(2)}) collective-permute-start(bf16[1,128,2048]{2,1,0:T(8,128)(2,1)} %dynamic-slice_bitcast_fusion.4), channel_id=1, source_target_pairs={{0,1},{1,0},{2,3},{3,2},{4,5},{5,4},{6,7},{7,6},{8,9},{9,8},{10,11... | collective-permute-start | bytes 1572872 | tf_op jit(solution)/shard_map/ppermute | solution.py:79
  9.6 33.4 %collective-permute-start.1 = (bf16[4,128,512]{2,1,0:T(8,128)(2,1)S(1)}, bf16[4,128,512]{2,1,0:T(8,128)(2,1)}, u32[]{:S(2)}, u32[]{:S(2)}) collective-permute-start(bf16[4,128,512]{2,1,0:T(8,128)(2,1)S(1)} %pad_maximum_fusion), channel_id=1, source_target_pairs={{0,1},{1,0},{2,3},{3,2},{4,5},{5,4},{6,7},{7,6},{8,9},{9,8},{10,11... | collective-permute-start | bytes 1572872 | tf_op jit(solution)/shard_map/ppermute | solution.py:79
  18.5 72.6 %all-to-all-start = ((bf16[16,80,512]{2,1,0:T(8,128)(2,1)}), bf16[16,80,512]{2,1,0:T(8,128)(2,1)S(1)}, u32[]{:S(2)}, u32[]{:S(2)}) async-start(bf16[16,80,512]{2,1,0:T(8,128)(2,1)} %bitcast.56), calls=%async_computation | async-start | bytes 2621440 | tf_op jit(solution)/shard_map/all_to_all | solution.py:724
  25.8 28.8 %collective-permute-start.8 = (bf16[4,128,512]{2,1,0:T(8,128)(2,1)S(1)}, bf16[4,128,512]{2,1,0:T(8,128)(2,1)}, u32[]{:S(2)}, u32[]{:S(2)}) collective-permute-start(bf16[4,128,512]{2,1,0:T(8,128)(2,1)S(1)} %pad_maximum_fusion.1), channel_id=1, source_target_pairs={{0,1},{1,0},{2,3},{3,2},{4,5},{5,4},{6,7},{7,6},{8,9},{9,8},{10,11... | collective-permute-start | bytes 1572872 | tf_op jit(solution)/shard_map/ppermute | solution.py:79
  43.0 11.7 %collective-permute-start.2 = (bf16[4,128,512]{2,1,0:T(8,128)(2,1)}, bf16[4,128,512]{2,1,0:T(8,128)(2,1)}, u32[]{:S(2)}, u32[]{:S(2)}) collective-permute-start(bf16[4,128,512]{2,1,0:T(8,128)(2,1)} %collective-permute-done.1.refs_2_), channel_id=1, source_target_pairs={{0,2},{2,0},{4,6},{6,4},{8,10},{10,8},{12,14},{14,12},{16,18},{18,... | collective-permute-start | bytes 1572872 | tf_op jit(solution)/shard_map/ppermute | solution.py:80
  53.3 11.2 %collective-permute-start.6 = (bf16[1,512,512]{2,1,0:T(8,128)(2,1)}, bf16[1,512,512]{2,1,0:T(8,128)(2,1)S(1)}, u32[]{:S(2)}, u32[]{:S(2)}) collective-permute-start(bf16[1,512,512]{2,1,0:T(8,128)(2,1)} %collective-permute-done.5.refs_4_), channel_id=1, source_target_pairs={{0,2},{2,0},{4,6},{6,4},{8,10},{10,8},{12,14},{14,12},{16,18},{18,... | collective-permute-start | bytes 1572872 | tf_op jit(solution)/shard_map/ppermute | solution.py:80
  53.4 11.1 %collective-permute-start.4 = (bf16[1,128,2048]{2,1,0:T(8,128)(2,1)}, bf16[1,128,2048]{2,1,0:T(8,128)(2,1)S(1)}, u32[]{:S(2)}, u32[]{:S(2)}) collective-permute-start(bf16[1,128,2048]{2,1,0:T(8,128)(2,1)} %collective-permute-done.3.refs_1_), channel_id=1, source_target_pairs={{0,2},{2,0},{4,6},{6,4},{8,10},{10,8},{12,14},{14,12},{16,18},{18,... | collective-permute-start | bytes 1572872 | tf_op jit(solution)/shard_map/ppermute | solution.py:80
  54.6 23.0 %collective-permute-start.9 = (bf16[4,128,512]{2,1,0:T(8,128)(2,1)}, bf16[4,128,512]{2,1,0:T(8,128)(2,1)S(1)}, u32[]{:S(2)}, u32[]{:S(2)}) collective-permute-start(bf16[4,128,512]{2,1,0:T(8,128)(2,1)} %collective-permute-done.8.refs_2_), channel_id=1, source_target_pairs={{0,2},{2,0},{4,6},{6,4},{8,10},{10,8},{12,14},{14,12},{16,18},{18,... | collective-permute-start | bytes 1572872 | tf_op jit(solution)/shard_map/ppermute | solution.py:80
  184.2 37.6 %collective-permute-start.28 = (bf16[2,512,512]{2,1,0:T(8,128)(2,1)}, bf16[2,512,512]{2,1,0:T(8,128)(2,1)}, u32[]{:S(2)}, u32[]{:S(2)}) collective-permute-start(bf16[2,512,512]{2,1,0:T(8,128)(2,1)} %constant_dynamic-slice_fusion.3), channel_id=1, source_target_pairs={{0,2},{2,0},{4,6},{6,4},{8,10},{10,8},{12,14},{14,12},{16,18},{18,... | collective-permute-start | bytes 3145736 | tf_op jit(solution)/shard_map/ppermute | solution.py:658
  202.6 25.5 %collective-permute-start.19 = (bf16[2,1024,512]{2,1,0:T(8,128)(2,1)}, bf16[2,1024,512]{2,1,0:T(8,128)(2,1)}, u32[]{:S(2)}, u32[]{:S(2)}) collective-permute-start(bf16[2,1024,512]{2,1,0:T(8,128)(2,1)} %constant_dynamic-slice_fusion.7), channel_id=1, source_target_pairs={{0,2},{2,0},{4,6},{6,4},{8,10},{10,8},{12,14},{14,12},{16,18},{18,... | collective-permute-start | bytes 6291464 | tf_op jit(solution)/shard_map/ppermute | solution.py:658
  224.2 15.4 %collective-permute-start.29 = (bf16[512,512]{1,0:T(8,128)(2,1)}, bf16[512,512]{1,0:T(8,128)(2,1)}, u32[]{:S(2)}, u32[]{:S(2)}) collective-permute-start(bf16[512,512]{1,0:T(8,128)(2,1)} %dynamic-slice_bitcast_fusion.2), channel_id=1, source_target_pairs={{0,1},{1,0},{2,3},{3,2},{4,5},{5,4},{6,7},{7,6},{8,9},{9,8},{10,11... | collective-permute-start | bytes 1572872 | tf_op jit(solution)/shard_map/ppermute | solution.py:665
  231.4 45.0 %collective-permute-start.20 = (bf16[1024,512]{1,0:T(8,128)(2,1)}, bf16[1024,512]{1,0:T(8,128)(2,1)}, u32[]{:S(2)}, u32[]{:S(2)}) collective-permute-start(bf16[1024,512]{1,0:T(8,128)(2,1)} %dynamic-slice_bitcast_fusion), channel_id=1, source_target_pairs={{0,1},{1,0},{2,3},{3,2},{4,5},{5,4},{6,7},{7,6},{8,9},{9,8},{10,11... | collective-permute-start | bytes 3145736 | tf_op jit(solution)/shard_map/ppermute | solution.py:665
  233.0 41.0 %collective-permute-start.11 = (bf16[544,512]{1,0:T(8,128)(2,1)}, bf16[544,512]{1,0:T(8,128)(2,1)}, u32[]{:S(2)}, u32[]{:S(2)}) collective-permute-start(bf16[544,512]{1,0:T(8,128)(2,1)} %dynamic-slice_bitcast_fusion.1), channel_id=1, source_target_pairs={{0,1},{1,0},{2,3},{3,2},{4,5},{5,4},{6,7},{7,6},{8,9},{9,8},{10,11... | collective-permute-start | bytes 1671176 | tf_op jit(solution)/shard_map/ppermute | solution.py:665
  234.3 131.9 %collective-permute-start.37 = (bf16[16,80,512]{2,1,0:T(8,128)(2,1)}, bf16[16,80,512]{2,1,0:T(8,128)(2,1)}, u32[]{:S(2)}, u32[]{:S(2)}) collective-permute-start(bf16[16,80,512]{2,1,0:T(8,128)(2,1)} %get-tuple-element.76.refs_0_), channel_id=1, source_target_pairs={{0,1},{1,0},{2,3},{3,2},{4,5},{5,4},{6,7},{7,6},{8,9},{9,8},{10,11... | collective-permute-start | bytes 3932168 | tf_op jit(solution)/shard_map/ppermute | solution.py:771
  241.0 38.0 %collective-permute-start.30 = (bf16[256,512]{1,0:T(8,128)(2,1)S(1)}, bf16[256,512]{1,0:T(8,128)(2,1)S(1)}, u32[]{:S(2)}, u32[]{:S(2)}) collective-permute-start(bf16[256,512]{1,0:T(8,128)(2,1)S(1)} %constant_dynamic-slice_fusion.2), channel_id=1, source_target_pairs={{0,4},{2,6},{4,0},{6,2},{8,12},{10,14},{12,8},{14,10},{16,20},{18,... | collective-permute-start | bytes 786440 | tf_op jit(solution)/shard_map/ppermute | solution.py:658
  275.3 11.9 %collective-permute-start.12 = (bf16[272,512]{1,0:T(8,128)(2,1)S(1)}, bf16[272,512]{1,0:T(8,128)(2,1)S(1)}, u32[]{:S(2)}, u32[]{:S(2)}) collective-permute-start(bf16[272,512]{1,0:T(8,128)(2,1)S(1)} %constant_dynamic-slice_fusion.10), channel_id=1, source_target_pairs={{0,4},{2,6},{4,0},{6,2},{8,12},{10,14},{12,8},{14,10},{16,20},{18,... | collective-permute-start | bytes 835592 | tf_op jit(solution)/shard_map/ppermute | solution.py:658
  278.0 16.7 %collective-permute-start.21 = (bf16[512,512]{1,0:T(8,128)(2,1)S(1)}, bf16[512,512]{1,0:T(8,128)(2,1)S(1)}, u32[]{:S(2)}, u32[]{:S(2)}) collective-permute-start(bf16[512,512]{1,0:T(8,128)(2,1)S(1)} %constant_dynamic-slice_fusion.6), channel_id=1, source_target_pairs={{0,4},{2,6},{4,0},{6,2},{8,12},{10,14},{12,8},{14,10},{16,20},{18,... | collective-permute-start | bytes 1572872 | tf_op jit(solution)/shard_map/ppermute | solution.py:658
  279.1 22.7 %collective-permute-start.31 = (bf16[128,512]{1,0:T(8,128)(2,1)S(1)}, bf16[128,512]{1,0:T(8,128)(2,1)S(1)}, u32[]{:S(2)}, u32[]{:S(2)}) collective-permute-start(bf16[128,512]{1,0:T(8,128)(2,1)S(1)} %constant_dynamic-slice_fusion.1), channel_id=1, source_target_pairs={{0,8},{2,10},{4,12},{6,14},{8,0},{10,2},{12,4},{14,6},{16,24},{18,... | collective-permute-start | bytes 393224 | tf_op jit(solution)/shard_map/ppermute | solution.py:658
  287.3 33.1 %collective-permute-start.13 = (bf16[136,512]{1,0:T(8,128)(2,1)S(1)}, bf16[136,512]{1,0:T(8,128)(2,1)S(1)}, u32[]{:S(2)}, u32[]{:S(2)}) collective-permute-start(bf16[136,512]{1,0:T(8,128)(2,1)S(1)} %constant_dynamic-slice_fusion.9), channel_id=1, source_target_pairs={{0,8},{2,10},{4,12},{6,14},{8,0},{10,2},{12,4},{14,6},{16,24},{18,... | collective-permute-start | bytes 417800 | tf_op jit(solution)/shard_map/ppermute | solution.py:658
  294.8 12.3 %collective-permute-start.22 = (bf16[256,512]{1,0:T(8,128)(2,1)S(1)}, bf16[256,512]{1,0:T(8,128)(2,1)S(1)}, u32[]{:S(2)}, u32[]{:S(2)}) collective-permute-start(bf16[256,512]{1,0:T(8,128)(2,1)S(1)} %constant_dynamic-slice_fusion.5), channel_id=1, source_target_pairs={{0,8},{2,10},{4,12},{6,14},{8,0},{10,2},{12,4},{14,6},{16,24},{18,... | collective-permute-start | bytes 786440 | tf_op jit(solution)/shard_map/ppermute | solution.py:658
  301.9 10.6 %collective-permute-start.32 = (bf16[64,512]{1,0:T(8,128)(2,1)S(1)}, bf16[64,512]{1,0:T(8,128)(2,1)S(1)}, u32[]{:S(2)}, u32[]{:S(2)}) collective-permute-start(bf16[64,512]{1,0:T(8,128)(2,1)S(1)} %constant_dynamic-slice_fusion), channel_id=1, source_target_pairs={{0,16},{2,18},{4,20},{6,22},{8,24},{10,26},{12,28},{14,30},{16,0},... | collective-permute-start | bytes 196616 | tf_op jit(solution)/shard_map/ppermute | solution.py:658
  307.2 13.0 %collective-permute-start.23 = (bf16[128,512]{1,0:T(8,128)(2,1)S(1)}, bf16[128,512]{1,0:T(8,128)(2,1)S(1)}, u32[]{:S(2)}, u32[]{:S(2)}) collective-permute-start(bf16[128,512]{1,0:T(8,128)(2,1)S(1)} %constant_dynamic-slice_fusion.4), channel_id=1, source_target_pairs={{0,16},{2,18},{4,20},{6,22},{8,24},{10,26},{12,28},{14,30},{16,0},... | collective-permute-start | bytes 393224 | tf_op jit(solution)/shard_map/ppermute | solution.py:658
  312.5 17.8 %collective-permute-start.33 = (bf16[64,512]{1,0:T(8,128)(2,1)S(1)}, bf16[64,512]{1,0:T(8,128)(2,1)S(1)}, u32[]{:S(2)}, u32[]{:S(2)}) collective-permute-start(bf16[64,512]{1,0:T(8,128)(2,1)S(1)} %add_convert_fusion.11), channel_id=1, source_target_pairs={{0,16},{2,18},{4,20},{6,22},{8,24},{10,26},{12,28},{14,30},{16,0},... | collective-permute-start | bytes 196616 | tf_op jit(solution)/shard_map/ppermute | solution.py:672
  337.2 26.9 %collective-permute-start.26 = (bf16[512,512]{1,0:T(8,128)(2,1)S(1)}, bf16[512,512]{1,0:T(8,128)(2,1)}, u32[]{:S(2)}, u32[]{:S(2)}) collective-permute-start(bf16[512,512]{1,0:T(8,128)(2,1)S(1)} %maximum_select_fusion.5), channel_id=1, source_target_pairs={{0,4},{2,6},{4,0},{6,2},{8,12},{10,14},{12,8},{14,10},{16,20},{18,... | collective-permute-start | bytes 1572872 | tf_op jit(solution)/shard_map/ppermute | solution.py:672
  338.6 18.1 %collective-permute-start.35 = (bf16[256,512]{1,0:T(8,128)(2,1)S(1)}, bf16[256,512]{1,0:T(8,128)(2,1)S(1)}, u32[]{:S(2)}, u32[]{:S(2)}) collective-permute-start(bf16[256,512]{1,0:T(8,128)(2,1)S(1)} %maximum_select_fusion.9), channel_id=1, source_target_pairs={{0,4},{2,6},{4,0},{6,2},{8,12},{10,14},{12,8},{14,10},{16,20},{18,... | collective-permute-start | bytes 786440 | tf_op jit(solution)/shard_map/ppermute | solution.py:672
  340.2 23.5 %collective-permute-start.17 = (bf16[272,512]{1,0:T(8,128)(2,1)S(1)}, bf16[272,512]{1,0:T(8,128)(2,1)S(1)}, u32[]{:S(2)}, u32[]{:S(2)}) collective-permute-start(bf16[272,512]{1,0:T(8,128)(2,1)S(1)} %maximum_select_fusion.7), channel_id=1, source_target_pairs={{0,4},{2,6},{4,0},{6,2},{8,12},{10,14},{12,8},{14,10},{16,20},{18,... | collective-permute-start | bytes 835592 | tf_op jit(solution)/shard_map/ppermute | solution.py:672
  343.0 69.1 %all-to-all-start.1 = ((bf16[16,80,512]{2,1,0:T(8,128)(2,1)}), bf16[16,80,512]{2,1,0:T(8,128)(2,1)S(1)}, u32[]{:S(2)}, u32[]{:S(2)}) async-start(bf16[16,80,512]{2,1,0:T(8,128)(2,1)} %get-tuple-element.55), calls=%async_computation.1 | async-start | bytes 2621440 | tf_op jit(solution)/shard_map/all_to_all | solution.py:768
  357.7 59.4 %collective-permute-start.36 = (bf16[512,512]{1,0:T(8,128)(2,1)}, bf16[512,512]{1,0:T(8,128)(2,1)}, u32[]{:S(2)}, u32[]{:S(2)}) collective-permute-start(bf16[512,512]{1,0:T(8,128)(2,1)} %maximum_select_fusion.6), channel_id=1, source_target_pairs={{0,2},{2,0},{4,6},{6,4},{8,10},{10,8},{12,14},{14,12},{16,18},{18,... | collective-permute-start | bytes 1572872 | tf_op jit(solution)/shard_map/ppermute | solution.py:672
  364.0 57.3 %collective-permute-start.18 = (bf16[544,512]{1,0:T(8,128)(2,1)S(1)}, bf16[544,512]{1,0:T(8,128)(2,1)}, u32[]{:S(2)}, u32[]{:S(2)}) collective-permute-start(bf16[544,512]{1,0:T(8,128)(2,1)S(1)} %maximum_select_fusion.4), channel_id=1, source_target_pairs={{0,2},{2,0},{4,6},{6,4},{8,10},{10,8},{12,14},{14,12},{16,18},{18,... | collective-permute-start | bytes 1671176 | tf_op jit(solution)/shard_map/ppermute | solution.py:672
  365.6 60.5 %collective-permute-start.27 = (bf16[1024,512]{1,0:T(8,128)(2,1)S(1)}, bf16[1024,512]{1,0:T(8,128)(2,1)}, u32[]{:S(2)}, u32[]{:S(2)}) collective-permute-start(bf16[1024,512]{1,0:T(8,128)(2,1)S(1)} %maximum_select_fusion.2), channel_id=1, source_target_pairs={{0,2},{2,0},{4,6},{6,4},{8,10},{10,8},{12,14},{14,12},{16,18},{18,... | collective-permute-start | bytes 3145736 | tf_op jit(solution)/shard_map/ppermute | solution.py:672
  (27 other events, 207.2 us)

commit v2 on v1

--- a/solution.py
+++ b/solution.py
@@ -207,7 +207,8 @@
     return x + nn(mix_ref[...], wo[...])
 
 
-def attend_backward(step, seq, images, grad, x, gain, wq, wo, qkv_ref, mix_ref, dmix_ref, dqkv_ref, pack_ref, base):
+def attend_backward(step, seq, images, grad, x, gain, wq, wo, qkv_ref, mix_ref, dmix_ref, dqkv_ref, pack_ref, base,
+                    tick=None):
     width = x.shape[1]
     head = width // HEADS
     scale = head ** -0.5
@@ -247,6 +248,8 @@
             dqkv_ref[at, hp * LANES:(hp + 1) * LANES] = dq.astype(bf16)
             dqkv_ref[at, width + hp * LANES:width + (hp + 1) * LANES] = dk.astype(bf16)
             dqkv_ref[at, 2 * width + hp * LANES:2 * width + (hp + 1) * LANES] = dv.astype(bf16)
+        if tick is not None:
+            tick(i)
         return 0
 
     lax.fori_loop(0, images, image, 0)
@@ -276,7 +279,7 @@
     )
 
 
-def mlp_body(split, blocks, hidden_ref, gain_ref, *refs):
+def mlp_body(split, hidden_ref, gain_ref, *refs):
     n = 2 * split.count(1)
     pieces, (out_ref, act_ref, slope_ref, w1, w2, sems) = refs[:n], refs[n:]
     half = n // 2
@@ -287,14 +290,13 @@
     u = (xn * gain_ref[1:2, :]).astype(bf16)
     out_ref[...] = hidden
     finish(copies)
-    ff = act_ref.shape[1]
-    wide = ff // blocks
-    for b in range(blocks):
+    wide = act_ref.shape[2]
+    for b in range(act_ref.shape[0]):
         at = slice(b * wide, (b + 1) * wide)
         act, slope = gelu_pair(nn(u, w1[0, :, at]))
         act = act.astype(bf16)
-        act_ref[:, at] = act
-        slope_ref[:, at] = slope.astype(bf16)
+        act_ref[b] = act
+        slope_ref[b] = slope.astype(bf16)
         out_ref[...] += nn(act, w2[0, at, :])
 
 
@@ -517,12 +519,8 @@
     return hi, mid, lo
 
 
-def back2_body(split, images, seq, experts, dy_ref, u_ref, probs_ref, hidden_ref, x_ref, gain_ref, router_ref, aux_ref,
-               stat_ref, live_ref, back_ref, ret_ref, dgate_ref, qkv_ref, mix_ref, *refs):
-    n = split.count(2)
-    pieces, (grad_ref, pack_ref, small_ref, w, sems, dmix_ref, dqkv_ref) = refs[:n], refs[n:]
-    copies = split.copies(pieces, w, sems)
-    start(copies)
+def router_backward(experts, dy_ref, u_ref, probs_ref, hidden_ref, gain_ref, router_ref, aux_ref, stat_ref, live_ref,
+                    back_ref, ret_ref, dgate_ref, small_ref):
     slots = back_ref.shape[1]
     owners = dgate_ref.shape[0]
     local = experts // owners
@@ -548,11 +546,22 @@
     probs = probs_ref[...]
     dlog = (probs * (dprobs - jnp.sum(probs * dprobs, axis=-1, keepdims=True))).astype(bf16)
     small_ref[0:LANES, :] = tn(dlog, u_ref[...])
-    du = nn(back_ref[...], ret_ref[...]) + nt(dlog, router_ref[...])
+    du = nn(back_ref[...], ret_ref[...].reshape(slots, dy_ref.shape[1])) + nt(dlog, router_ref[...])
     xn, rs = norm(hidden_ref[...])
     dv, dg = norm_back(du, xn, rs, gain_ref[3:4, :])
     small_ref[LANES:LANES + 1, :] = dg
     grad = dy_ref[...].astype(f32) + dv
+    return grad
+
+
+def back2_body(split, images, seq, experts, dy_ref, u_ref, probs_ref, hidden_ref, x_ref, gain_ref, router_ref, aux_ref,
+               stat_ref, live_ref, back_ref, ret_ref, dgate_ref, qkv_ref, mix_ref, *refs):
+    n = split.count(2)
+    pieces, (grad_ref, pack_ref, small_ref, w, sems, dmix_ref, dqkv_ref) = refs[:n], refs[n:]
+    copies = split.copies(pieces, w, sems)
+    start(copies)
+    grad = router_backward(experts, dy_ref, u_ref, probs_ref, hidden_ref, gain_ref, router_ref, aux_ref, stat_ref, live_ref,
+                           back_ref, ret_ref, dgate_ref, small_ref)
     grad_ref[...] = grad
     finish(copies)
     step = hidden_ref.shape[0] // images
@@ -564,7 +573,7 @@
     grad_ref[...] += dv
 
 
-def mlp_back_body(split, blocks, grad_ref, hidden_ref, gain_ref, act_ref, slope_ref, *refs):
+def mlp_back_body(split, grad_ref, hidden_ref, gain_ref, act_ref, slope_ref, *refs):
     n = 2 * split.count(1)
     pieces, (out_ref, pack_ref, dgain_ref, w1, w2, sems, du_ref) = refs[:n], refs[n:]
     half = n // 2
@@ -577,14 +586,14 @@
     low = grad.astype(bf16)
     finish(copies)
     width = grad.shape[1]
-    ff = act_ref.shape[1]
+    blocks = act_ref.shape[0]
+    ff = blocks * width
     shards = pack_ref.shape[0]
     part, fpart = width // shards, ff // shards
-    blocks = ff // width
     base = part * blocks
     for b in range(blocks):
         at = slice(b * width, (b + 1) * width)
-        dz = (slope_ref[:, at].astype(f32) * nt(low, w2[0, at, :])).astype(bf16)
+        dz = (slope_ref[b].astype(f32) * nt(low, w2[0, at, :])).astype(bf16)
         d = nt(dz, w1[0, :, at])
         if b == 0:
             du_ref[...] = d
@@ -593,7 +602,7 @@
         gin = tn(u, dz).astype(bf16)
         for s in range(shards):
             pack_ref[s, b * part:(b + 1) * part, :] = gin[s * part:(s + 1) * part]
-        gout = tn(act_ref[:, at], low).astype(bf16)
+        gout = tn(act_ref[b], low).astype(bf16)
         per = min(width, fpart)
         for j in range(width // per):
             row = b * width + j * per
@@ -637,6 +646,317 @@
     tmp_ref[...] = (hidden_ref[...] + nn(back_ref[...], ret_ref[...])) * live_ref[...]
     for i in range(images):
         out_ref[i] = tmp_ref[i * step:i * step + seq, :].astype(bf16)
+
+
+def backward_body(split, images, seq, experts, local, owners, plan, *refs):
+    (gain_ref, router_ref, aux_ref, stat_ref, live_ref, back_ref, dgate_ref, tok_ref, dy_h, u_h, probs_h, du_h,
+     hid2_h, x2_h, hid1_h, qkv2_h, mix2_h, qkv1_h, mix1_h, act_h, slope_h, served_h, uin_h, dyin_h, dyx_h, we1_h, we2_h,
+     *refs) = refs
+    na, nm = split.count(2), split.count(1)
+    two, refs = refs[:na], refs[na:]
+    up, refs = refs[:nm], refs[nm:]
+    down, refs = refs[:nm], refs[nm:]
+    one, refs = refs[:na], refs[na:]
+    (out_ref, gtok_ref, fin, smout_ref, small_ref, ge1_h, ge2_h, sback_h, ux_h,
+     hid2, xbuf, grad_ref, dubuf, qkv, mix, dmix, dqkv, watt, w1, w2, big, stage, pack, crecv, xa, yb, ya, xb, zr,
+     sm, smr,
+     lsem, wsem, vs, vr, xs, xr, gs, gr, ms, mr, esem, osem, tsem) = refs
+    me, x = lax.axis_index("expert"), lax.axis_index("shard")
+    bits = owners.bit_length() - 1
+    bit = [(me // (1 << i)) % 2 for i in range(bits)]
+    hop = [me + (1 - 2 * bit[i]) * (1 << i) for i in range(bits)]
+    rows, width = grad_ref.shape
+    step = rows // images
+    blocks = act_h.shape[0]
+    whole = pack.shape[2]
+    part = width // 2
+
+    def to(e, s):
+        return dict(device_id=(e, s), device_id_type=pl.DeviceIdType.MESH)
+
+    def each(lo, hi, f):
+        lax.fori_loop(lo, hi, lambda k, c: (f(k), c)[1], 0)
+
+    barrier = pltpu.get_barrier_semaphore()
+    each(1, owners, lambda k: pl.semaphore_signal(barrier, inc=1, **to(xor(me, k, bits), x)))
+    pl.semaphore_signal(barrier, inc=1, **to(me, 1 - x))
+
+    def load(src, dst, i):
+        return pltpu.make_async_copy(src, dst, lsem.at[i])
+
+    count = 4 + 2 * blocks
+    dy_ref, u_ref, probs_ref, du_ref = dmix, dqkv.at[:, 0:width], dubuf.at[:, 0:LANES], stage.at[0]
+    start_in = [load(hid2_h, hid2, 0), load(du_h, du_ref, count), load(dy_h, dy_ref, count + 1), load(u_h, u_ref, count + 2),
+                load(probs_h, probs_ref, count + 3)]
+    start(start_in)
+    first = [load(x2_h, xbuf, 1), load(qkv2_h, qkv, 2), load(mix2_h, mix, 3)]
+    w_two = split.copies(two, watt, wsem.at[0])
+    w_mlp = split.copies(up, w1, wsem.at[1]) + split.copies(down, w2, wsem.at[2])
+    gelus = [load(act_h.at[b], big.at[b, 0:rows], 4 + b) for b in range(blocks)]
+    gelus += [load(slope_h.at[b], big.at[b, big.shape[1] // 2:big.shape[1] // 2 + rows], 4 + blocks + b) for b in range(blocks)]
+    start(first + w_two + w_mlp + gelus)
+    own = pltpu.make_async_copy(served_h.at[me], sback_h.at[me], tsem.at[0])
+    own.start()
+    pl.semaphore_wait(barrier, owners)
+
+    def send_served(k):
+        p = xor(me, k, bits)
+        return pltpu.make_async_remote_copy(served_h.at[p], sback_h.at[me], vs.at[k], vr.at[k], **to(p, x))
+
+    def send_rows():
+        return pltpu.make_async_remote_copy(uin_h, ux_h, xs.at[0], xr.at[0], **to(me, 1 - x))
+
+    send_rows().start()
+    each(1, owners, lambda k: send_served(owners - k).start())
+
+    def add(ref, at, other):
+        ref[at] = (ref[at].astype(f32) + other.astype(f32)).astype(bf16)
+
+    def stages(n):
+        def copy(src, dst, i, peer):
+            return pltpu.make_async_remote_copy(src, dst, gs.at[n, i], gr.at[n, i], **peer)
+
+        q = whole // 4
+        o = bit[0] * (whole // 2)
+        out = []
+        out.append((
+            lambda: [copy(pack.at[n, :, pl.ds((1 - bit[0]) * (whole // 2), whole // 2)], crecv.at[n], 0, to(hop[0], x))],
+            lambda: add(pack, (n, slice(None), pl.ds(o, whole // 2)), crecv[n])))
+        e = q // 2
+        b1 = bit[1] * e
+
+        def after1():
+            add(pack, (n, x, pl.ds(o, q)), xa[n])
+            add(pack, (n, slice(None), pl.ds(o + q + b1, e)), yb[n])
+
+        out.append((
+            lambda: [copy(pack.at[n, 1 - x, pl.ds(o, q)], xa.at[n], 1, to(me, 1 - x)),
+                     copy(pack.at[n, :, pl.ds(o + q + e - b1, e)], yb.at[n], 2, to(hop[1], x))],
+            after1))
+
+        def after2():
+            add(pack, (n, x, pl.ds(o + b1, e)), ya[n])
+            add(pack, (n, x, pl.ds(o + q + b1, e)), xb[n])
+
+        out.append((
+            lambda: [copy(pack.at[n, x, pl.ds(o + e - b1, e)], ya.at[n], 3, to(hop[1], x)),
+                     copy(pack.at[n, 1 - x, pl.ds(o + q + b1, e)], xb.at[n], 4, to(me, 1 - x))],
+            after2))
+        at, size, sem, starts = o + b1, e, 5, [(o, q), (o + b1, e)]
+        zoff = 0
+        for i in range(2, bits):
+            size //= 2
+            keep, give = at + bit[i] * size, at + (1 - bit[i]) * size
+
+            def go(give=give, size=size, sem=sem, i=i, zoff=zoff):
+                return [copy(pack.at[n, x, pl.ds(give + j * q, size)], zr.at[n, j, pl.ds(zoff, size)], sem + j, to(hop[i], x))
+                        for j in range(2)]
+
+            def after(keep=keep, size=size, zoff=zoff):
+                for j in range(2):
+                    add(pack, (n, x, pl.ds(keep + j * q, size)), zr[n, j, zoff:zoff + size])
+
+            out.append((go, after))
+            at, sem, zoff = keep, sem + 2, zoff + size
+            starts.append((at, size))
+        last_go, last_after = out[-1]
+
+        def after_last(at=at, size=size):
+            last_after()
+            for j in range(2):
+                fin[n, pl.ds(at + j * q, size)] = pack[n, x, pl.ds(at + j * q, size)]
+
+        out[-1] = (last_go, after_last)
+        for i in reversed(range(1, bits)):
+            at, size = starts[i]
+
+            def go(at=at, size=size, sem=sem, i=i):
+                return [copy(fin.at[n, pl.ds(at + j * q, size)], fin.at[n, pl.ds(at + j * q, size)], sem + j, to(hop[i], x))
+                        for j in range(2)]
+
+            out.append((go, lambda: None))
+            sem += 2
+        out.append((lambda sem=sem: [copy(fin.at[n, pl.ds(o, whole // 2)], fin.at[n, pl.ds(o, whole // 2)], sem, to(hop[0], x))],
+                    lambda: None))
+        return out
+
+    groups = [stages(n) for n in range(4)]
+
+    def small_stage(i):
+        if i == 0:
+            src, dst, peer = sm, smr.at[0], to(hop[0], x)
+        elif i == 1:
+            src, dst, peer = sm.at[1 - x], smr.at[1, 0], to(me, 1 - x)
+        else:
+            src, dst, peer = sm.at[x], smr.at[i, 0], to(hop[i - 1], x)
+        return pltpu.make_async_remote_copy(src, dst, ms.at[i], mr.at[i], **peer)
+
+    def small_after(i):
+        if i == 0:
+            sm[...] += smr[0]
+        else:
+            sm[x] += smr[i, 0]
+
+    def tick(n, k):
+        table = groups[n]
+        if k > 0:
+            finish(table[k - 1][0]())
+            table[k - 1][1]()
+            if n == 3 and k - 1 < bits + 1:
+                small_stage(k - 1).wait()
+                small_after(k - 1)
+        if k < len(table):
+            start(table[k][0]())
+            if n == 3 and k < bits + 1:
+                small_stage(k).start()
+
+    done = [0] * 4
+
+    def at_point(name, index=None):
+        for i, n in plan.get(name, ()):
+            if index is None:
+                tick(n, done[n])
+            else:
+                pl.when(index == i)(functools.partial(tick, n, done[n]))
+            done[n] += 1
+
+    finish(start_in)
+    grad_ref[...] = router_backward(experts, dy_ref, u_ref, probs_ref, hid2, gain_ref, router_ref, aux_ref, stat_ref, live_ref,
+                                    back_ref, du_ref, dgate_ref, small_ref)
+    finish(first + w_two)
+    dv, dg = attend_backward(
+        step, seq, images, grad_ref[...], xbuf[...], gain_ref[2:3, :], [watt.at[c] for c in range(3)], watt.at[3],
+        qkv, mix, dmix, dqkv, pack.at[0], 0,
+    )
+    small_ref[LANES + 1:LANES + 2, :] = dg
+    grad_ref[...] += dv
+    at_point("two")
+    second = [load(hid1_h, xbuf, 1), load(qkv1_h, qkv, 2), load(mix1_h, mix, 3)]
+    w_one = split.copies(one, watt, wsem.at[0])
+    start(second + w_one)
+
+    finish(gelus + w_mlp)
+    low = grad_ref[...].astype(bf16)
+    fpart = blocks * width // 2
+    for b in range(blocks):
+        s, off = b * width // fpart, b * width % fpart
+        pack[1, s, off:off + width, :] = tn(big[b, 0:rows], low).astype(bf16)
+    at_point("out")
+    finish(second[:1])
+    xn, rs = norm(xbuf[...])
+    gain = gain_ref[1:2, :]
+    u = (xn * gain).astype(bf16)
+    half = big.shape[1] // 2
+    for b in range(blocks):
+        cols = slice(b * width, (b + 1) * width)
+        dz = (big[b, half:half + rows].astype(f32) * nt(low, w2[0, cols, :])).astype(bf16)
+        d = nt(dz, w1[0, :, cols])
+        if b == 0:
+            dubuf[...] = d
+        else:
+            dubuf[...] += d
+        gin = tn(u, dz).astype(bf16)
+        for s in range(2):
+            pack[2, s, b * part:(b + 1) * part, :] = gin[s * part:(s + 1) * part]
+        at_point("in%d" % b)
+    dv, dg = norm_back(dubuf[...], xn, rs, gain)
+    small_ref[LANES + 3:LANES + 4, :] = dg
+    grad_ref[...] += dv
+    at_point("mlp")
+
+    pad_store(xbuf, lambda i: tok_ref[i], images, seq, step)
+    finish(second[1:] + w_one)
+    dv, dg = attend_backward(
+        step, seq, images, grad_ref[...], xbuf[...], gain_ref[0:1, :], [watt.at[c] for c in range(3)], watt.at[3],
+        qkv, mix, dmix, dqkv, pack.at[3], 0, tick=lambda i: at_point("image", i),
+    )
+    sm[...] = jnp.zeros(sm.shape, f32)
+    for s in range(2):
+        cols = slice(s * part, (s + 1) * part)
+        sm[s, 0:experts] = small_ref[0:experts, cols]
+        sm[s, experts:experts + 1] = dg[:, cols]
+        sm[s, experts + 1:experts + 2] = small_ref[LANES + 3:LANES + 4, cols]
+        sm[s, experts + 2:experts + 3] = small_ref[LANES + 1:LANES + 2, cols]
+        sm[s, experts + 3:experts + 4] = small_ref[LANES:LANES + 1, cols]
+    at_point("one")
+    grad_ref[...] += dv
+    for i in range(images):
+        gtok_ref[i] = grad_ref[i * step:i * step + seq, :]
+
+    own.wait()
+    each(1, owners, lambda k: send_served(k).wait())
+    send_rows().wait()
+    at_point("rows")
+
+    todo = [(uin_h, 0, 0), (ux_h, 0, 1), (dyin_h, 1, 0), (dyx_h.at[0], 1, 1)]
+    moves = [pltpu.make_async_copy(r, stage.at[i % 2], esem.at[i % 2]) for i, (r, _, _) in enumerate(todo)]
+
+    def lane(i):
+        return pl.ds(pl.multiple_of(i * width, width), width)
+
+    def chunk(i):
+        e, f = i // blocks, i % blocks
+        slot = i % 2
+        col = pl.ds(pl.multiple_of(f * width, width), width)
+        return [pltpu.make_async_copy(we1_h.at[e, :, col], w1.at[0, :, lane(slot)], esem.at[2 + slot]),
+                pltpu.make_async_copy(we2_h.at[e, col, :], w2.at[0, lane(slot), :], esem.at[4 + slot])]
+
+    def result(i):
+        e, f = i // blocks, i % blocks
+        slot = i % 2
+        col = pl.ds(pl.multiple_of(f * width, width), width)
+        return [pltpu.make_async_copy(w1.at[0, :, lane(2 + slot)], ge1_h.at[e, :, col], osem.at[slot]),
+                pltpu.make_async_copy(w2.at[0, lane(2 + slot), :], ge2_h.at[e, col, :], osem.at[2 + slot])]
+
+    moves[0].start()
+    start(chunk(0))
+    for i, (_, kind, piece) in enumerate(todo):
+        if i + 1 < len(todo):
+            moves[i + 1].start()
+        moves[i].wait()
+        for e, v in enumerate(split_rows(stage[i % 2], local)):
+            if kind == 1:
+                u = big[e, piece * half:(piece + 1) * half]
+                v = v * gate_of(u, router_ref[...], experts, me * local + e)
+            big[kind * local + e, piece * half:(piece + 1) * half] = v.astype(bf16)
+    back = pltpu.make_async_copy(sback_h, stage.at[0], tsem.at[0])
+    back.start()
+    back.wait()
+    grad_ref[...] = (hid2[...] + nn(back_ref[...], stage[0].reshape(back_ref.shape[1], width))) * live_ref[...]
+    for i in range(images):
+        out_ref[i] = grad_ref[i * step:i * step + seq, :].astype(bf16)
+    at_point("output")
+    count = local * blocks
+    acc1, acc2 = xbuf.at[0:width], dubuf.at[0:width]
+
+    def expert(i, c):
+        slot = i % 2
+        pl.when(i + 1 < count)(lambda: start(chunk(i + 1)))
+        finish(chunk(i))
+        e = i // blocks
+        for p in range(2):
+            u = big[e, p * half:(p + 1) * half]
+            dsv = big[local + e, p * half:(p + 1) * half]
+            act, slope = gelu_pair(nn(u, w1[0, :, lane(slot)]))
+            dz = (slope * nt(dsv, w2[0, lane(slot), :])).astype(bf16)
+            g1, g2 = tn(u, dz), tn(act.astype(bf16), dsv)
+            if p == 0:
+                acc1[...] = g1
+                acc2[...] = g2
+                at_point("early", i)
+            else:
+                pl.when(i >= 2)(lambda: finish(result(i - 2)))
+                w1[0, :, lane(2 + slot)] = (acc1[...] + g1).astype(bf16)
+                w2[0, lane(2 + slot), :] = (acc2[...] + g2).astype(bf16)
+        start(result(i))
+        at_point("late", i)
+        return c
+
+    lax.fori_loop(0, count, expert, 0)
+    at_point("end")
+    for i in range(max(0, count - 2), count):
+        finish(result(i))
+    smout_ref[...] = sm[x]
 
 
 def swap(owners, bit):
@@ -738,8 +1058,8 @@
     )
     ins = [hidden, gains] + w_up + w_down
     block_out, act, slope = call(
-        functools.partial(mlp_body, split, 4),
-        [sds((rows, width), f32), sds((rows, ff), bf16), sds((rows, ff), bf16)],
+        functools.partial(mlp_body, split),
+        [sds((rows, width), f32)] + [sds((ff // width, rows, width), bf16)] * 2,
         ins, mlp_scratch, specs(2, ins), flops=6e9, nbytes=12e6,
     )
     ins = [block_out, gains, router_full, disp, live_col, loads[None, :]] + w_two
@@ -765,6 +1085,10 @@
         compiler_params=pltpu.CompilerParams(vmem_limit_bytes=VMEM_BYTES, collective_id=0, has_side_effects=True),
         cost_estimate=pl.CostEstimate(flops=int(11e9), bytes_accessed=int(15e6), transcendentals=0),
     )(u_out.reshape(block), dy_in, router_full, stat, expert_in, expert_out)
+    parts_of = (gains, router_full, aux_weight.reshape(1, 1), stat, live_col, back, dgate_back, tokens, dy, u_two, probs, du_back)
+    if shards == 2:
+        return fused_backward(split, experts, tokens, parts_of, hidden_two, block_out, hidden, qkv_two, mix_two, qkv_one, mix_one,
+                              act, slope, served, u_in, dy_in, dy_far, expert_in, expert_out, w_two, w_up, w_down, w_one)
     served_back = expert_swap(served).reshape(slots, width)
 
     if shards == 2:
@@ -804,7 +1128,7 @@
     late = reduce_all(pack_two, owners, shards)
     ins = [grad_block, hidden, gains, act, slope] + w_up + w_down
     grad_hidden, pack_mlp, dg_two = call(
-        functools.partial(mlp_back_body, split, 4),
+        functools.partial(mlp_back_body, split),
         [sds((rows, width), f32), sds((shards, part * (ff // width) + ff // shards, width), bf16), sds((1, width), f32)],
         ins, mlp_scratch + [pltpu.VMEM((rows, width), f32)], specs(5, ins), flops=11e9, nbytes=16e6,
     )
@@ -839,6 +1163,94 @@
         tail[34:36],
         grad_e_in,
         grad_e_out,
+    )
+
+
+PLAN = {
+    "two": [(0, 0)],
+    "out": [(0, 0), (0, 1)],
+    "in0": [(0, 1)],
+    "in2": [(0, 0)],
+    "mlp": [(0, 2), (0, 1)],
+    "image": [(0, 2), (0, 0), (1, 1), (1, 2), (2, 0), (2, 1)],
+    "one": [(0, 3), (0, 0)],
+    "rows": [(0, 3), (0, 2), (0, 1)],
+    "output": [(0, 3), (0, 2), (0, 0)],
+    "early": [(0, 1), (1, 3), (1, 1), (2, 3), (2, 1), (3, 3), (4, 3), (5, 3)],
+    "late": [(0, 2), (0, 0), (1, 2), (1, 0), (2, 2), (2, 0), (3, 1), (3, 2), (4, 2)],
+    "end": [],
+}
+
+
+def fused_backward(split, experts, tokens, parts_of, hidden_two, block_out, hidden, qkv_two, mix_two, qkv_one, mix_one,
+                   act, slope, served, u_in, dy_in, dy_far, expert_in, expert_out, w_two, w_up, w_down, w_one):
+    images, seq, width = tokens.shape
+    rows = hidden.shape[0]
+    local, _, ff = expert_in.shape
+    block = served.shape
+    owners = block[0]
+    bits = owners.bit_length() - 1
+    whole = 2 * width
+    part = width // 2
+    blocks = ff // width
+    stages = 3 + (bits - 2) + (bits - 1) + 1
+    plan = {k: list(v) for k, v in PLAN.items()}
+    left = [stages + 1] * 4
+    for k in plan:
+        for item in list(plan[k]):
+            if left[item[1]] > 0:
+                left[item[1]] -= 1
+            else:
+                plan[k].remove(item)
+    plan["end"] = plan["end"] + [(0, n) for i in range(max(left)) for n in range(4) if left[n] > i]
+    small_rows = -(-(experts + 4) // 8) * 8
+    sem = pltpu.SemaphoreType.DMA
+    ins = list(parts_of) + [hidden_two, block_out, hidden, qkv_two, mix_two, qkv_one, mix_one, act, slope, served, u_in, dy_in,
+                            dy_far, expert_in, expert_out] + w_two + w_up + w_down + w_one
+    vmem = 8
+    big_rows = 2 * owners * CAP
+    nsem = 5 + 4 * (bits - 2) + 3
+    V = pltpu.VMEM
+    outs = pl.pallas_call(
+        functools.partial(backward_body, split, images, seq, experts, local, owners, plan),
+        out_shape=[
+            sds((images, seq, width), bf16), sds((images, seq, width), f32), sds((4, whole, width), bf16),
+            sds((small_rows, part), f32), sds((LANES + 8, width), f32), sds(expert_in.shape, bf16), sds(expert_out.shape, bf16),
+            sds(block, bf16), sds(block, bf16),
+        ],
+        in_specs=[VM] * vmem + [ANY] * (len(ins) - vmem),
+        out_specs=[VM] * 5 + [ANY] * 4,
+        scratch_shapes=[
+            V((rows, width), f32), V((rows, width), f32), V((rows, width), f32), V((rows, width), f32),
+            V((rows, 3 * width), bf16), V((rows, width), bf16), V((rows, width), bf16), V((rows, 3 * width), bf16),
+            V((4, width, width), bf16), V((1, width, ff), bf16), V((1, ff, width), bf16), V((blocks, big_rows, width), bf16),
+            V((2,) + block, bf16),
+            V((4, 2, whole, width), bf16), V((4, 2, whole // 2, width), bf16), V((4, whole // 4, width), bf16),
+            V((4, 2, whole // 8, width), bf16), V((4, whole // 8, width), bf16), V((4, whole // 8, width), bf16),
+            V((4, 2, whole // 8 - whole // (1 << (bits + 1)), width), bf16),
+            V((2, small_rows, part), f32), V((bits + 1, 2, small_rows, part), f32),
+            sem((8 + 2 * blocks,)), sem((3, 4)), sem((owners,)), sem((owners,)), sem((1,)), sem((1,)),
+            sem((4, nsem)), sem((4, nsem)), sem((bits + 1,)), sem((bits + 1,)), sem((6,)), sem((4,)), sem((1,)),
+        ],
+        compiler_params=pltpu.CompilerParams(vmem_limit_bytes=63 << 20, collective_id=1, has_side_effects=True),
+        cost_estimate=pl.CostEstimate(flops=int(60e9), bytes_accessed=int(80e6), transcendentals=0),
+    )(*ins)
+    output, grad_tokens, fin, tail, small, grad_e_in, grad_e_out = outs[:7]
+    return (
+        output,
+        small[LANES + 2, 0],
+        grad_tokens,
+        fin[3, :3 * part].astype(f32).reshape(3, part, width),
+        fin[3, 3 * part:].astype(f32),
+        fin[2].astype(f32).reshape(blocks, part, width).transpose(1, 0, 2).reshape(part, ff),
+        fin[1].astype(f32),
+        tail[experts:experts + 2],
+        fin[0, :3 * part].astype(f32).reshape(3, part, width),
+        fin[0, 3 * part:].astype(f32),
+        tail[:experts].T,
+        tail[experts + 2:experts + 4],
+        grad_e_in.astype(f32),
+        grad_e_out.astype(f32),
     )
 
 

time: 436 us -> 329 us (0.75)
  waiting for transfers between devices: 95.9 us -> 22 us
  starting transfers between devices: 69.6 us -> 14.5 us
  Pallas kernels: 211 us -> 246 us
  local copies, waits for them, and re-layouts: 29.6 us -> 19.7 us
    pallas_call x1, Pallas kernels: 45.8 us -> 138 us  [fused_backward(): pl.pallas_call(functools.partial(backward_body, split, images, seq, exper...]
    ppermute x28 -> x0, waiting for transfers between devices: 73.9 us -> none  [the longest x3 36.6 us: reduce_all(): v = add(keep, lax.ppermute(send, 'shard', [(0, 1), (1, 0)]))]
    pallas_call x8 -> x4, Pallas kernels: 97.5 us -> 40.9 us  [call(): pl.pallas_call(body, out_shape=outs, in_specs=specs or [VM] * len(ins), o...]
    ppermute x28 -> x0, starting transfers between devices: 51.2 us -> none  [the longest x12 36.5 us: fold(): return add(keep, lax.ppermute(send, 'expert', swap(owners, bit)))]
    dynamic_slice x12 -> x0, local copies, waits for them, and re-layouts: 7.07 us -> none  [fold(): send = lax.dynamic_slice_in_dim(v, (1 - own) * half, half, axis)]
    convert_element_type x18 -> x6, other arithmetic: 15.7 us -> 15.7 us  [the longest x1 4.6 us: fused_backward(): grad_e_out.astype(f32)]
  transfers between devices with their start and end apart: 40 -> 11, of which waited for: 13 -> 2; matrix products, arithmetic and copies ran while one was open for 9% -> 3% of each run, Pallas kernels for 28% -> 13%
where the time goes in v2:
time: 329 us; the launch traced here: 325 us
  Pallas kernels  246 us (75%)
  waiting for transfers between devices  22 us (7%)
  other arithmetic  19.8 us (6%)
  local copies, waits for them, and re-layouts  19.7 us (6%)
  starting transfers between devices  14.5 us (4%)
    pallas_call x1, Pallas kernels, fused_backward(): pl.pallas_call(functools.partial(backward_body, split, images, seq, exper...  138 us
    pallas_call x1, Pallas kernels, per_device(): pl.pallas_call(functools.partial(expert_body, owners, shards, local, expe...  67.7 us
    pallas_call x4, Pallas kernels, call(): pl.pallas_call(body, out_shape=outs, in_specs=specs or [VM] * len(ins), o...  40.9 us
    ppermute x4, waiting for transfers between devices, gather(): far = lax.ppermute(send, 'shard', [(0, 1), (1, 0)])  14.5 us
    ppermute x1, waiting for transfers between devices, per_device(): other = lax.ppermute(router, 'shard', [(0, 1), (1, 0)])  7.47 us
    all_to_all x1, starting transfers between devices, per_device(): dy_in = expert_swap(dy_out.reshape(block))  7.12 us
    unnamed x41, local copies, waits for them, and re-layouts  6.83 us
  transfers between devices with their start and end apart: 11, of which 2 were waited for; matrix products, arithmetic and copies ran while one was open for 3% of the time, Pallas kernels for 13%

profile of v2, /device:TPU:0, one launch (start us, length us, event | category | flops | bytes accessed | tf_op | source)
XLA Modules:
  0.0 324.6 jit_solution(7064568755337900931)
XLA Ops:
  1.5 2.9 collective-permute-start
  4.4 1.1 dynamic-slice_bitcast_fusion
  5.6 1.9 dynamic-slice_bitcast_fusion.1
  7.5 2.0 collective-permute-start.4
  10.6 0.9 reshape.151.live_ref.refs_4_
  11.5 0.9 copy.59.r_ref
  12.4 6.1 %shard_map.265 = (bf16[624,512]{1,0:T(8,128)(2,1)}, bf16[1280,512]{1,0:T(8,128)(2,1)}, bf16[1280,624]{1,0:T(8,128)(2,1)}, bf16[624,1280]{1,0:T(8,128)(2,1)}) custom-call(s32[624,2]{1,0:T(8,128)} %copy.59.r_ref, s32[2,624]{1,0:T(2,128)} %bitcast.58, f32[624,1]{1,0:T(8,128)} %reshape.151.live_ref.refs_4_, bf16[3,197,512]{2,1,0:T(8,128)(2,1)} %cot_ref.1), custom_call_target="tpu_custom_call" | custom-call | flops 2000000000 | bytes 6000000 | tf_op jit(solution)/shard_map/pallas_call | solution.py:122
  18.6 7.1 %all-to-all-start = ((bf16[16,80,512]{2,1,0:T(8,128)(2,1)}), bf16[16,80,512]{2,1,0:T(8,128)(2,1)S(1)}, u32[]{:S(2)}, u32[]{:S(2)}) async-start(bf16[16,80,512]{2,1,0:T(8,128)(2,1)} %bitcast.49), calls=%async_computation | async-start | bytes 2621440 | tf_op jit(solution)/shard_map/all_to_all | solution.py:1044
  25.8 1.6 collective-permute-start.8
  28.5 14.5 %collective-permute-done.2.refs_2_.refs_39_ = bf16[4,128,512]{2,1,0:T(8,128)(2,1)} collective-permute-done((bf16[4,128,512]{2,1,0:T(8,128)(2,1)S(1)}, bf16[4,128,512]{2,1,0:T(8,128)(2,1)}, u32[]{:S(2)}, u32[]{:S(2)}) %collective-permute-start.2) | collective-permute-done | bytes 524320 | tf_op jit(solution)/shard_map/ppermute | solution.py:79
  43.0 1.2 compare_select_fusion.load_ref
  45.5 7.5 %collective-permute-done.1 = bf16[256,32]{0,1:T(8,128)(2,1)S(1)} collective-permute-done((bf16[256,32]{0,1:T(8,128)(2,1)S(1)}, bf16[256,32]{0,1:T(8,128)(2,1)S(1)}, u32[]{:S(2)}, u32[]{:S(2)}) %collective-permute-start.1) | collective-permute-done | bytes 16416 | tf_op jit(solution)/shard_map/ppermute | solution.py:1030
  54.6 9.8 %shard_map.263 = (f32[624,512]{1,0:T(8,128)}, bf16[624,1536]{1,0:T(8,128)(2,1)}, bf16[624,512]{1,0:T(8,128)(2,1)}) custom-call(bf16[3,197,512]{2,1,0:T(8,128)(2,1)} %refs_7_.1, f32[4,512]{1,0:T(4,128)} %fusion.1.gain_ref.refs_0_, bf16[3,256,512]{2,1,0:T(8,128)(2,1)} %refs_37_.1, bf16[1,256,512]{2,1,0:T(8,128)(2,1)} %bitcast.54, ...), custom_call_target="tpu_custom_call" | custom-call | flops 4000000000 | bytes 8000000 | tf_op jit(solution)/shard_map/pallas_call | solution.py:122
  65.5 12.1 %shard_map.264 = (f32[624,512]{1,0:T(8,128)}, bf16[4,624,512]{2,1,0:T(8,128)(2,1)}, bf16[4,624,512]{2,1,0:T(8,128)(2,1)}) custom-call(f32[624,512]{1,0:T(8,128)} %get-tuple-element.44.hidden_ref.refs_14_, f32[4,512]{1,0:T(4,128)} %fusion.1.gain_ref.refs_0_, bf16[1,256,2048]{2,1,0:T(8,128)(2,1)} %bitcast.50, ...), custom_call_target="tpu_custom_call" | custom-call | flops 6000000000 | bytes 12000000 | tf_op jit(solution)/shard_map/pallas_call | solution.py:122
  78.4 12.8 %shard_map.266 = (f32[624,512]{1,0:T(8,128)}, bf16[624,1536]{1,0:T(8,128)(2,1)}, bf16[624,512]{1,0:T(8,128)(2,1)}, bf16[624,512]{1,0:T(8,128)(2,1)}, f32[624,128...) custom-call(f32[624,512]{1,0:T(8,128)} %get-tuple-element.45.x_ref.refs_13_, ...), custom_call_target="tpu_custom_call" | custom-call | flops 5000000000 | bytes 10000000 | tf_op jit(solution)/shard_map/pallas_call | solution.py:122
  91.2 1.0 copy-done.3
  92.3 67.7 %shard_map.267 = (bf16[16,80,512]{2,1,0:T(8,128)(2,1)}, bf16[16,80,512]{2,1,0:T(8,128)(2,1)}, bf16[16,80,512]{2,1,0:T(8,128)(2,1)}, f32[16,8,128]{2,1,0:T(8,128)...) custom-call(bf16[16,80,512]{2,1,0:T(8,128)(2,1)} %bitcast.59, bf16[16,80,512]{2,1,0:T(8,128)(2,1)} %copy-done.3, ...), custom_call_target="tpu_custom_call" | custom-call | flops 11000000512 | bytes 15000000 | tf_op jit(solution)/shard_map/pallas_call | solution.py:1074
  160.0 137.6 %shard_map.268 = (bf16[3,197,512]{2,1,0:T(8,128)(2,1)}, f32[3,197,512]{2,1,0:T(8,128)}, bf16[4,1024,512]{2,1,0:T(8,128)(2,1)}, f32[40,256]{1,0:T(8,128)}, f32[13...) custom-call(f32[4,512]{1,0:T(4,128)} %fusion.1.gain_ref.refs_0_, ...), custom_call_target="tpu_custom_call" | custom-call | flops 60000002048 | bytes 80000000 | tf_op jit(solution)/shard_map/pallas_call | solution.py:1214
  297.5 1.4 fusion.5
  298.9 1.4 slice_bitcast_fusion
  300.3 2.3 bitcast_convert_fusion.1
  302.5 1.5 fusion.4
  304.0 1.7 bitcast_convert_fusion
  305.7 1.2 slice.30
  306.9 1.4 convert.9
  308.2 1.4 convert.13
  309.9 1.5 copy.65
  311.4 1.5 copy-done.1
  312.8 4.4 %convert_element_type.88 = f32[2,512,2048]{2,1,0:T(8,128)} convert(bf16[2,512,2048]{2,1,0:T(8,128)(2,1)S(1)} %copy-done.1) | non-fusion elementwise | flops 2097152 | bytes 12582912 | tf_op jit(solution)/shard_map/convert_element_type | solution.py:1252
  317.3 4.6 %convert_element_type.89 = f32[2,2048,512]{2,1,0:T(8,128)} convert(bf16[2,2048,512]{2,1,0:T(8,128)(2,1)S(1)} %copy-done) | non-fusion elementwise | flops 2097152 | bytes 12582912 | tf_op jit(solution)/shard_map/convert_element_type | solution.py:1253
  321.9 0.8 copy.70
  323.4 1.0 copy.71
  (75 shorter events, 7.5 us)
Async XLA Ops:
  0.6 8.8 %copy-start.8 = (bf16[256,512]{1,0:T(8,128)(2,1)S(1)}, bf16[256,512]{1,0:T(8,128)(2,1)}, u32[]{:S(2)}) copy-start(bf16[256,512]{1,0:T(8,128)(2,1)} %param.22) | copy-start | bytes 786436
  0.7 8.8 %copy-start.6 = (bf16[3,256,512]{2,1,0:T(8,128)(2,1)S(1)}, bf16[3,256,512]{2,1,0:T(8,128)(2,1)}, u32[]{:S(2)}) copy-start(bf16[3,256,512]{2,1,0:T(8,128)(2,1)} %refs_37_.1) | copy-start | bytes 2359300
  1.5 43.3 %collective-permute-start = (bf16[4,256]{1,0:T(4,128)(2,1)S(1)}, bf16[4,256]{1,0:T(4,128)(2,1)S(1)}, u32[]{:S(2)}, u32[]{:S(2)}) collective-permute-start(bf16[4,256]{1,0:T(4,128)(2,1)S(1)} %pad_maximum_fusion.4), channel_id=1, source_target_pairs={{0,1},{1,0},{2,3},{3,2},{4,5},{5,4},{6,7},{7,6},{8,9},{9,8},{10,11... | collective-permute-start | bytes 6152 | tf_op jit(solution)/shard_map/ppermute | solution.py:1028
  4.4 6.0 %copy-start.13 = (s32[3,197,2]{1,2,0:T(2,128)S(1)}, s32[3,197,2]{1,2,0:T(2,128)}, u32[]{:S(2)}) copy-start(s32[3,197,2]{1,2,0:T(2,128)} %param.18) | copy-start | bytes 14188
  5.5 47.8 %collective-permute-start.6 = (bf16[1,512,512]{2,1,0:T(8,128)(2,1)S(1)}, bf16[1,512,512]{2,1,0:T(8,128)(2,1)}, u32[]{:S(2)}, u32[]{:S(2)}) collective-permute-start(bf16[1,512,512]{2,1,0:T(8,128)(2,1)S(1)} %dynamic-slice_bitcast_fusion), channel_id=1, source_target_pairs={{0,1},{1,0},{2,3},{3,2},{4,5},{5,4},{6,7},{7,6},{8,9},{9,8},{10,11... | collective-permute-start | bytes 1572872 | tf_op jit(solution)/shard_map/ppermute | solution.py:79
  7.5 45.9 %collective-permute-start.4 = (bf16[1,128,2048]{2,1,0:T(8,128)(2,1)}, bf16[1,128,2048]{2,1,0:T(8,128)(2,1)}, u32[]{:S(2)}, u32[]{:S(2)}) collective-permute-start(bf16[1,128,2048]{2,1,0:T(8,128)(2,1)} %dynamic-slice_bitcast_fusion.1), channel_id=1, source_target_pairs={{0,1},{1,0},{2,3},{3,2},{4,5},{5,4},{6,7},{7,6},{8,9},{9,8},{10,11... | collective-permute-start | bytes 1572872 | tf_op jit(solution)/shard_map/ppermute | solution.py:79
  9.6 33.4 %collective-permute-start.2 = (bf16[4,128,512]{2,1,0:T(8,128)(2,1)S(1)}, bf16[4,128,512]{2,1,0:T(8,128)(2,1)}, u32[]{:S(2)}, u32[]{:S(2)}) collective-permute-start(bf16[4,128,512]{2,1,0:T(8,128)(2,1)S(1)} %pad_maximum_fusion), channel_id=1, source_target_pairs={{0,1},{1,0},{2,3},{3,2},{4,5},{5,4},{6,7},{7,6},{8,9},{9,8},{10,11... | collective-permute-start | bytes 1572872 | tf_op jit(solution)/shard_map/ppermute | solution.py:79
  10.5 1.9 copy-start.10
  18.5 7.2 %copy-start.7 = (bf16[3,256,512]{2,1,0:T(8,128)(2,1)S(1)}, bf16[3,256,512]{2,1,0:T(8,128)(2,1)}, u32[]{:S(2)}) copy-start(bf16[3,256,512]{2,1,0:T(8,128)(2,1)} %refs_27_.1) | copy-start | bytes 2359300
  18.5 7.2 %copy-start.9 = (bf16[256,512]{1,0:T(8,128)(2,1)S(1)}, bf16[256,512]{1,0:T(8,128)(2,1)}, u32[]{:S(2)}) copy-start(bf16[256,512]{1,0:T(8,128)(2,1)} %param.27) | copy-start | bytes 786436
  18.5 9.0 %copy-start.11 = (s32[624,2]{0,1:T(2,128)S(1)}, s32[624,2]{0,1:T(2,128)}, u32[]{:S(2)}) copy-start(s32[624,2]{0,1:T(2,128)} %copy-done.10) | copy-start | bytes 14980
  18.5 26.3 %copy-start.12 = (bf16[256,32]{0,1:T(8,128)(2,1)S(1)}, bf16[256,32]{0,1:T(8,128)(2,1)}, u32[]{:S(2)}) copy-start(bf16[256,32]{0,1:T(8,128)(2,1)} %param.28) | copy-start | bytes 49156
  18.5 26.4 %copy-start.14 = (bf16[2,256]{1,0:T(2,128)(2,1)S(1)}, bf16[2,256]{1,0:T(2,128)(2,1)}, u32[]{:S(2)}) copy-start(bf16[2,256]{1,0:T(2,128)(2,1)} %param.29) | copy-start | bytes 3076
  18.6 26.4 %copy-start.15 = (bf16[2,256]{1,0:T(2,128)(2,1)S(1)}, bf16[2,256]{1,0:T(2,128)(2,1)}, u32[]{:S(2)}) copy-start(bf16[2,256]{1,0:T(2,128)(2,1)} %param.25) | copy-start | bytes 3076
  18.6 72.6 %all-to-all-start = ((bf16[16,80,512]{2,1,0:T(8,128)(2,1)}), bf16[16,80,512]{2,1,0:T(8,128)(2,1)S(1)}, u32[]{:S(2)}, u32[]{:S(2)}) async-start(bf16[16,80,512]{2,1,0:T(8,128)(2,1)} %bitcast.49), calls=%async_computation | async-start | bytes 2621440 | tf_op jit(solution)/shard_map/all_to_all | solution.py:1044
  25.8 28.7 %collective-permute-start.8 = (bf16[4,128,512]{2,1,0:T(8,128)(2,1)S(1)}, bf16[4,128,512]{2,1,0:T(8,128)(2,1)}, u32[]{:S(2)}, u32[]{:S(2)}) collective-permute-start(bf16[4,128,512]{2,1,0:T(8,128)(2,1)S(1)} %pad_maximum_fusion.1), channel_id=1, source_target_pairs={{0,1},{1,0},{2,3},{3,2},{4,5},{5,4},{6,7},{7,6},{8,9},{9,8},{10,11... | collective-permute-start | bytes 1572872 | tf_op jit(solution)/shard_map/ppermute | solution.py:79
  43.0 11.7 %collective-permute-start.3 = (bf16[4,128,512]{2,1,0:T(8,128)(2,1)}, bf16[4,128,512]{2,1,0:T(8,128)(2,1)}, u32[]{:S(2)}, u32[]{:S(2)}) collective-permute-start(bf16[4,128,512]{2,1,0:T(8,128)(2,1)} %collective-permute-done.2.refs_2_.refs_39_), channel_id=1, source_target_pairs={{0,2},{2,0},{4,6},{6,4},{8,10},{10,8},{12,14},{14,12},{16,18},{18,... | collective-permute-start | bytes 1572872 | tf_op jit(solution)/shard_map/ppermute | solution.py:80
  44.8 8.2 %collective-permute-start.1 = (bf16[256,32]{0,1:T(8,128)(2,1)S(1)}, bf16[256,32]{0,1:T(8,128)(2,1)S(1)}, u32[]{:S(2)}, u32[]{:S(2)}) collective-permute-start(bf16[256,32]{0,1:T(8,128)(2,1)S(1)} %copy-done.12), channel_id=1, source_target_pairs={{0,1},{1,0},{2,3},{3,2},{4,5},{5,4},{6,7},{7,6},{8,9},{9,8},{10,11... | collective-permute-start | bytes 49160 | tf_op jit(solution)/shard_map/ppermute | solution.py:1030
  53.3 11.2 %collective-permute-start.7 = (bf16[1,512,512]{2,1,0:T(8,128)(2,1)}, bf16[1,512,512]{2,1,0:T(8,128)(2,1)S(1)}, u32[]{:S(2)}, u32[]{:S(2)}) collective-permute-start(bf16[1,512,512]{2,1,0:T(8,128)(2,1)} %collective-permute-done.6.refs_4_.refs_35_), channel_id=1, source_target_pairs={{0,2},{2,0},{4,6},{6,4},{8,10},{10,8},{12,14},{14,12},{16,18},{18,... | collective-permute-start | bytes 1572872 | tf_op jit(solution)/shard_map/ppermute | solution.py:80
  53.4 11.2 %collective-permute-start.5 = (bf16[1,128,2048]{2,1,0:T(8,128)(2,1)}, bf16[1,128,2048]{2,1,0:T(8,128)(2,1)S(1)}, u32[]{:S(2)}, u32[]{:S(2)}) collective-permute-start(bf16[1,128,2048]{2,1,0:T(8,128)(2,1)} %collective-permute-done.4.refs_1_.refs_32_), channel_id=1, source_target_pairs={{0,2},{2,0},{4,6},{6,4},{8,10},{10,8},{12,14},{14,12},{16,18},{18,... | collective-permute-start | bytes 1572872 | tf_op jit(solution)/shard_map/ppermute | solution.py:80
  54.5 23.0 %collective-permute-start.9 = (bf16[4,128,512]{2,1,0:T(8,128)(2,1)}, bf16[4,128,512]{2,1,0:T(8,128)(2,1)S(1)}, u32[]{:S(2)}, u32[]{:S(2)}) collective-permute-start(bf16[4,128,512]{2,1,0:T(8,128)(2,1)} %collective-permute-done.8.refs_2_.refs_29_), channel_id=1, source_target_pairs={{0,2},{2,0},{4,6},{6,4},{8,10},{10,8},{12,14},{14,12},{16,18},{18,... | collective-permute-start | bytes 1572872 | tf_op jit(solution)/shard_map/ppermute | solution.py:80
  64.5 0.8 copy-start.16
  64.5 0.9 copy-start.17
  77.6 0.8 copy-start.18
  91.2 1.1 copy-start.3
  300.3 3.8 %copy-start.2 = (bf16[4,1024,512]{2,1,0:T(8,128)(2,1)S(1)}, bf16[4,1024,512]{2,1,0:T(8,128)(2,1)}, u32[]{:S(2)}) copy-start(bf16[4,1024,512]{2,1,0:T(8,128)(2,1)} %get-tuple-element.70) | copy-start | bytes 12582916
  309.9 3.0 copy-start.1
  312.8 4.5 %copy-start = (bf16[2,2048,512]{2,1,0:T(8,128)(2,1)S(1)}, bf16[2,2048,512]{2,1,0:T(8,128)(2,1)}, u32[]{:S(2)}) copy-start(bf16[2,2048,512]{2,1,0:T(8,128)(2,1)} %get-tuple-element.73) | copy-start | bytes 12582916
  317.3 4.6 %copy-start.5 = (bf16[3,197,512]{2,1,0:T(8,128)(2,1)S(1)}, bf16[3,197,512]{2,1,0:T(8,128)(2,1)}, u32[]{:S(2)}) copy-start(bf16[3,197,512]{2,1,0:T(8,128)(2,1)} %get-tuple-element.100) | copy-start | bytes 1815556
  321.9 1.5 copy-start.4

commit v3 on v2

--- a/solution.py
+++ b/solution.py
@@ -143,11 +143,16 @@
 
 
 def route_body(images, seq, local, block, r_ref, rt_ref, live_ref, cot_ref, dy_ref, dyd_ref, disp_ref, back_ref):
+    step = r_ref.shape[0] // images
+    pad_store(dy_ref, lambda i: cot_ref[i], images, seq, step)
+    dy_ref[...] = (dy_ref[...].astype(f32) * live_ref[...]).astype(bf16)
+    route_tables(local, block, r_ref, rt_ref, disp_ref, back_ref)
+    dyd_ref[...] = nn(disp_ref[...], dy_ref[...]).astype(bf16)
+
+
+def route_tables(local, block, r_ref, rt_ref, disp_ref, back_ref):
     rows = r_ref.shape[0]
     slots = disp_ref.shape[0]
-    step = rows // images
-    pad_store(dy_ref, lambda i: cot_ref[i], images, seq, step)
-    dy_ref[...] = (dy_ref[...].astype(f32) * live_ref[...]).astype(bf16)
     lane = lax.broadcasted_iota(jnp.int32, (rows, LANES), 1)
     hit = (r_ref[:, 0:1] == lane) | (r_ref[:, 1:2] == lane)
     ti = lax.broadcasted_iota(jnp.int32, (rows, rows), 0)
@@ -170,10 +175,10 @@
     within_t = jnp.sum(spread_t * off, axis=1, keepdims=True)
     within_t = jnp.where(jnp.sum(spread_t, axis=1, keepdims=True) > 0, within_t, -2.0)
     disp_ref[...] = (nn(spread_t.astype(bf16), place_t) == within_t).astype(f32).astype(bf16)
-    dyd_ref[...] = nn(disp_ref[...], dy_ref[...]).astype(bf16)
-
-
-def attend_forward(step, seq, images, x, gain, wq, wo, qkv_ref, mix_ref):
+    return hit.astype(f32)
+
+
+def attend_forward(step, seq, images, x, gain, wq, wo, qkv_ref, mix_ref, tick=None, image_tick=None):
     width = x.shape[1]
     head = width // HEADS
     scale = head ** -0.5
@@ -181,6 +186,8 @@
     a = (xn * gain).astype(bf16)
     for c in range(3):
         qkv_ref[:, c * width:(c + 1) * width] = nn(a, wq[c][...]).astype(bf16)
+    if tick is not None:
+        tick()
     lane = lax.broadcasted_iota(jnp.int32, (1, LANES), 1)
     col = lax.broadcasted_iota(jnp.int32, (1, step), 1)
     per = LANES // head
@@ -201,6 +208,8 @@
                 o = nn(p, v)
                 got = o if got is None else jnp.where(mine, o, got)
             mix_ref[at, hp * LANES:(hp + 1) * LANES] = got.astype(bf16)
+        if image_tick is not None:
+            image_tick(i)
         return 0
 
     lax.fori_loop(0, images, image, 0)
@@ -328,6 +337,225 @@
     sum_ref[...] = jnp.concatenate([load_ref[...], sums, jnp.zeros((6, LANES), f32)], axis=0)
 
 
+def forward_body(images, seq, experts, local, owners, *refs):
+    (r_ref, rt_ref, counts_ref, tok_ref, cot_ref, gain_ref, router_ref, q1_h, o1_h, up_h, down_h, q2_h, o2_h,
+     gains_out, router_out, stat_out, live_out,
+     dy_o, uout_o, hid1_o, x2_o, hid2_o, qkv1_o, mix1_o, qkv2_o, mix2_o, act_o, slope_o, u_o, probs_o, back_o,
+     wa_o, wu_o, wd_o, wb_o, dyin_o,
+     wa, wu, wd, wb, dy, slot_rows, disp, back, hid1, x2, hid2, qkv1, mix1, qkv2, mix2, act, slope, u, probs, gx,
+     lsem, osem, ks, kr, vs, vr) = refs
+    me, x = lax.axis_index("expert"), lax.axis_index("shard")
+    bits = owners.bit_length() - 1
+    b0, b1 = me % 2, (me // 2) % 2
+    core, side = me + 1 - 2 * b0, me + (1 - 2 * b1) * 2
+    rows, width = dy.shape
+    step = rows // images
+    part = width // 2
+    ff = wd.shape[1]
+    fpart = ff // 2
+
+    def to(e, s):
+        return dict(device_id=(e, s), device_id_type=pl.DeviceIdType.MESH)
+
+    def each(lo, hi, f):
+        lax.fori_loop(lo, hi, lambda k, c: (f(k), c)[1], 0)
+
+    barrier = pltpu.get_barrier_semaphore()
+    each(1, owners, lambda k: pl.semaphore_signal(barrier, inc=1, **to(xor(me, k, bits), x)))
+    pl.semaphore_signal(barrier, inc=1, **to(me, 1 - x))
+
+    def at(first, size):
+        return pl.ds(pl.multiple_of(first, 64), size)
+
+    mine, theirs = x * part, (1 - x) * part
+    loads = [
+        pltpu.make_async_copy(q1_h, wa.at[0:3, at(mine, part)], lsem.at[0]),
+        pltpu.make_async_copy(o1_h, wa.at[3, at(mine, part)], lsem.at[1]),
+        pltpu.make_async_copy(up_h, wu.at[0, at(mine, part)], lsem.at[2]),
+        pltpu.make_async_copy(down_h, wd.at[0, at(x * fpart, fpart)], lsem.at[3]),
+        pltpu.make_async_copy(q2_h, wb.at[0:3, at(mine, part)], lsem.at[4]),
+        pltpu.make_async_copy(o2_h, wb.at[3, at(mine, part)], lsem.at[5]),
+    ]
+    start(loads)
+    router_out[at(mine, part), :] = router_ref[...]
+    pl.semaphore_wait(barrier, owners)
+
+    def remote(src, dst, i, peer):
+        return pltpu.make_async_remote_copy(src, dst, ks.at[i], kr.at[i], **peer)
+
+    far, near, over = to(me, 1 - x), to(core, x), to(side, x)
+    half, quarter, fquarter = part // 2, part // 4, fpart // 4
+    p = b0 * 2 + b1
+    h = b0 * half
+    here = at(theirs + h, half)
+    moves = {
+        "small": [lambda: remote(gain_ref, gx, 0, far), lambda: remote(router_ref, router_out.at[at(mine, part), :], 1, far)],
+        "ax": [lambda: remote(q1_h.at[:, at(h, half)], wa.at[0:3, at(mine + h, half)], 2, far),
+               lambda: remote(o1_h.at[at(h, half)], wa.at[3, at(mine + h, half)], 3, far)],
+        "ac": [lambda: remote(wa.at[:, here], wa.at[:, here], 4, near)],
+        "ux": [lambda: remote(up_h.at[at(p * quarter, quarter)], wu.at[0, at(mine + p * quarter, quarter)], 5, far)],
+        "uy": [lambda: remote(wu.at[0, at(theirs + p * quarter, quarter)], wu.at[0, at(theirs + p * quarter, quarter)], 6, over)],
+        "uc": [lambda: remote(wu.at[0, here], wu.at[0, here], 7, near)],
+        "dx": [lambda: remote(down_h.at[at(p * fquarter, fquarter)], wd.at[0, at(x * fpart + p * fquarter, fquarter)], 8, far)],
+        "dy": [lambda: remote(wd.at[0, at((1 - x) * fpart + p * fquarter, fquarter)],
+                              wd.at[0, at((1 - x) * fpart + p * fquarter, fquarter)], 9, over)],
+        "dc": [lambda: remote(wd.at[0, at((1 - x) * fpart + b0 * 2 * fquarter, 2 * fquarter)],
+                              wd.at[0, at((1 - x) * fpart + b0 * 2 * fquarter, 2 * fquarter)], 10, near)],
+        "bx": [lambda: remote(q2_h.at[:, at(p * quarter, quarter)], wb.at[0:3, at(mine + p * quarter, quarter)], 11, far),
+               lambda: remote(o2_h.at[at(p * quarter, quarter)], wb.at[3, at(mine + p * quarter, quarter)], 12, far)],
+        "by": [lambda: remote(wb.at[:, at(theirs + p * quarter, quarter)], wb.at[:, at(theirs + p * quarter, quarter)], 13, over)],
+        "bc": [lambda: remote(wb.at[:, here], wb.at[:, here], 14, near)],
+    }
+
+    def go(*names):
+        for n in names:
+            for m in moves[n]:
+                m().start()
+
+    def done(*names):
+        for n in names:
+            for m in moves[n]:
+                m().wait()
+
+    def send_dy(k):
+        q = xor(me, k, bits)
+        return pltpu.make_async_remote_copy(slot_rows.at[0, q], dyin_o.at[me], vs.at[k], vr.at[k], **to(q, x))
+
+    out = []
+
+    def keep(src, dst):
+        c = pltpu.make_async_copy(src, dst, osem.at[len(out)])
+        c.start()
+        out.append(c)
+
+    go("ax", "small")
+    row = lax.broadcasted_iota(jnp.int32, (rows, 1), 0)
+    live = ((row < counts_ref[0] * step) & (r_ref[:, 0:1] >= 0)).astype(f32)
+    live_out[...] = live
+    pad_store(dy, lambda i: cot_ref[i], images, seq, step)
+    dy[...] = (dy[...].astype(f32) * live).astype(bf16)
+    keep(dy, dy_o)
+    hit = route_tables(local, slot_rows.shape[2], r_ref, rt_ref, disp, back)
+    keep(back, back_o)
+    slot_rows[0] = nn(disp[...], dy[...]).astype(bf16).reshape(slot_rows.shape[1:])
+    keep(slot_rows.at[0, me], dyin_o.at[me])
+    lane = lax.broadcasted_iota(jnp.int32, (1, LANES), 1)
+    load = jnp.where(lane == LANES - 1, jnp.sum(live, axis=0, keepdims=True), jnp.sum(hit * live, axis=0, keepdims=True))
+    done("ax")
+    go("ac", "ux", "dx")
+    each(1, owners, lambda k: send_dy(owners - k).start())
+    pad_store(hid1, lambda i: tok_ref[i], images, seq, step)
+    done("small")
+    own_gain, far_gain = gain_ref[...], gx[...]
+    gains = jnp.where(x == 0, jnp.concatenate([own_gain, far_gain], axis=1), jnp.concatenate([far_gain, own_gain], axis=1))
+    gains_out[...] = gains
+    finish(loads)
+    done("ac")
+    keep(wa, wa_o)
+
+    def first_tick():
+        go("bx")
+
+    def first_image(i):
+        @pl.when(i == 0)
+        def _():
+            done("ux")
+            go("uy")
+
+        @pl.when(i == 1)
+        def _():
+            done("dx", "uy")
+            go("dy", "uc")
+
+        @pl.when(i == 2)
+        def _():
+            done("bx")
+            go("by")
+
+    hid1[...] = attend_forward(step, seq, images, hid1[...], gains[0:1], [wa.at[c] for c in range(3)], wa.at[3], qkv1, mix1,
+                               first_tick, first_image)
+    keep(hid1, hid1_o)
+    keep(qkv1, qkv1_o)
+    keep(mix1, mix1_o)
+
+    done("uc")
+    keep(wu, wu_o)
+    xn, _ = norm(hid1[...])
+    a = (xn * gains[1:2]).astype(bf16)
+    for b in range(act.shape[0]):
+        one, two = gelu_pair(nn(a, wu[0, :, b * width:(b + 1) * width]))
+        act[b] = one.astype(bf16)
+        slope[b] = two.astype(bf16)
+        if b == 0:
+            done("dy", "by")
+            go("dc", "bc")
+    keep(slope, slope_o)
+    keep(act, act_o)
+    done("dc", "bc")
+    keep(wd, wd_o)
+    keep(wb, wb_o)
+    total = hid1[...]
+    for b in range(act.shape[0]):
+        total = total + nn(act[b], wd[0, b * width:(b + 1) * width, :])
+    x2[...] = total
+    keep(x2, x2_o)
+
+    hid2[...] = attend_forward(step, seq, images, x2[...], gains[2:3], [wb.at[c] for c in range(3)], wb.at[3], qkv2, mix2)
+    keep(qkv2, qkv2_o)
+    keep(mix2, mix2_o)
+    keep(hid2, hid2_o)
+    xn, _ = norm(hid2[...])
+    u[...] = (xn * gains[3:4]).astype(bf16)
+    keep(u, u_o)
+    slot_rows[1] = nn(disp[...], u[...]).astype(bf16).reshape(slot_rows.shape[1:])
+    keep(slot_rows.at[1], uout_o)
+    probs[...] = router_probs(u[...], router_out[...], experts)
+    keep(probs, probs_o)
+    sums = jnp.sum(probs[...] * live, axis=0, keepdims=True)
+    stat_out[...] = jnp.concatenate([load, sums, jnp.zeros((6, LANES), f32)], axis=0)
+    each(1, owners, lambda k: send_dy(k).wait())
+    finish(out)
+
+
+def fused_forward(owners, experts, local, block, tokens, cotangent, routes, counts, gains, router, attn_qkv1, attn_out1, mlp_in, mlp_out,
+                  attn_qkv2, attn_out2):
+    images, seq, width = tokens.shape
+    step = padded(seq)
+    rows = images * step
+    ff = mlp_in.shape[1]
+    slots = owners * block[1]
+    blocks = ff // width
+    part = width // 2
+    routes_pad = jnp.pad(routes, ((0, 0), (0, step - seq), (0, 0)), constant_values=-1).reshape(rows, 2)
+    gains = jnp.pad(gains, ((0, 4), (0, 0))).astype(f32)
+    router = jnp.pad(router, ((0, 0), (0, LANES - experts)))
+    V, sem = pltpu.VMEM, pltpu.SemaphoreType.DMA
+    kept = [
+        ((rows, width), bf16), (block, bf16), ((rows, width), f32), ((rows, width), f32), ((rows, width), f32),
+        ((rows, 3 * width), bf16), ((rows, width), bf16), ((rows, 3 * width), bf16), ((rows, width), bf16),
+        ((blocks, rows, width), bf16), ((blocks, rows, width), bf16), ((rows, width), bf16), ((rows, LANES), f32), ((rows, slots), bf16),
+        ((4, width, width), bf16), ((1, width, ff), bf16), ((1, ff, width), bf16), ((4, width, width), bf16), (block, bf16),
+    ]
+    return pl.pallas_call(
+        functools.partial(forward_body, images, seq, experts, local, owners),
+        out_shape=[sds((8, width), f32), sds((width, LANES), bf16), sds((8, LANES), f32), sds((rows, 1), f32)]
+        + [sds(shape, dtype) for shape, dtype in kept],
+        in_specs=[VM, VM, pl.BlockSpec(memory_space=pltpu.SMEM)] + [VM] * 4 + [ANY] * 6,
+        out_specs=[VM] * 4 + [ANY] * len(kept),
+        scratch_shapes=[
+            V((4, width, width), bf16), V((1, width, ff), bf16), V((1, ff, width), bf16), V((4, width, width), bf16),
+            V((rows, width), bf16), V((2,) + block, bf16), V((slots, rows), bf16), V((rows, slots), bf16),
+            V((rows, width), f32), V((rows, width), f32), V((rows, width), f32),
+            V((rows, 3 * width), bf16), V((rows, width), bf16), V((rows, 3 * width), bf16), V((rows, width), bf16),
+            V((blocks, rows, width), bf16), V((blocks, rows, width), bf16), V((rows, width), bf16), V((rows, LANES), f32),
+            V((8, part), f32),
+            sem((6,)), sem((len(kept),)), sem((15,)), sem((15,)), sem((owners,)), sem((owners,)),
+        ],
+        compiler_params=pltpu.CompilerParams(vmem_limit_bytes=VMEM_BYTES, collective_id=2, has_side_effects=True),
+        cost_estimate=pl.CostEstimate(flops=int(18e9), bytes_accessed=int(60e6), transcendentals=0),
+    )(routes_pad, routes_pad.T, counts, tokens, cotangent, gains, router, attn_qkv1, attn_out1, mlp_in, mlp_out, attn_qkv2, attn_out2)
+
+
 def split_rows(block, local):
     n, r, w = block.shape
     v = block.astype(f32)
@@ -359,8 +587,8 @@
 
 
 def expert_body(owners, shards, local, experts, group, uout_ref, dy_ref, router_ref, stat_ref, w1_hbm, w2_hbm,
-                uin_ref, served_ref, duback_ref, dgback_ref, total_ref, dyx_ref,
-                w1, w2, dusend, dgsend, statx, state, wsem, lsem, us, ur, ds_, dr, gs, gr, xs, xr, ss, sr, ys, yr):
+                uin_ref, served_ref, duback_ref, dgback_ref, total_ref, dyx_ref, ux_ref,
+                w1, w2, dusend, dgsend, statx, state, wsem, lsem, us, ur, ds_, dr, gs, gr, ss, sr, fs, fr, xs, xr, ys, yr):
     me, x = lax.axis_index("expert"), lax.axis_index("shard")
     bits = owners.bit_length() - 1
     barrier = pltpu.get_barrier_semaphore()
@@ -396,6 +624,10 @@
 
     def send_dyx(k):
         return pltpu.make_async_remote_copy(dy_ref, dyx_ref.at[k - 1], ys.at[k], yr.at[k], **at(me, (x + k) % shards))
+
+    def send_far(g):
+        rows = pl.ds(xor(me // group, g, bits) * group, group)
+        return pltpu.make_async_remote_copy(uin_ref.at[rows], ux_ref.at[rows], fs.at[g], fr.at[g], **at(me, (x + 1) % shards))
 
     def send_state(k):
         return pltpu.make_async_remote_copy(state.at[0], state.at[k], ss.at[k], sr.at[k], **at(peer(k), x))
@@ -447,6 +679,8 @@
                 pl.when(g > 0)(lambda k=k: send_u(k).wait_recv())
             else:
                 send_u(k).wait_recv()
+        if shards == 2:
+            send_far(g).start()
         work(g)
         for j in range(group):
             k = g * group + j
@@ -471,6 +705,8 @@
     each(1, owners, lambda k: send_u(k).wait_send())
     finish(backs)
     each(1, shards, lambda k: send_dyx(k).wait())
+    if shards == 2:
+        each(0, owners // group, lambda g: send_far(g).wait())
     each(1, owners, lambda k: send_du(k).wait())
     each(1, owners, lambda k: send_dg(k).wait())
 
@@ -650,17 +886,17 @@
 
 def backward_body(split, images, seq, experts, local, owners, plan, *refs):
     (gain_ref, router_ref, aux_ref, stat_ref, live_ref, back_ref, dgate_ref, tok_ref, dy_h, u_h, probs_h, du_h,
-     hid2_h, x2_h, hid1_h, qkv2_h, mix2_h, qkv1_h, mix1_h, act_h, slope_h, served_h, uin_h, dyin_h, dyx_h, we1_h, we2_h,
+     hid2_h, x2_h, hid1_h, qkv2_h, mix2_h, qkv1_h, mix1_h, act_h, slope_h, served_h, uin_h, ux_h, dyin_h, dyx_h, we1_h, we2_h,
      *refs) = refs
-    na, nm = split.count(2), split.count(1)
+    na = nm = 1
     two, refs = refs[:na], refs[na:]
     up, refs = refs[:nm], refs[nm:]
     down, refs = refs[:nm], refs[nm:]
     one, refs = refs[:na], refs[na:]
-    (out_ref, gtok_ref, fin, smout_ref, small_ref, ge1_h, ge2_h, sback_h, ux_h,
+    (out_ref, gtok_ref, fin, smout_ref, small_ref, ge1_h, ge2_h, sback_h,
      hid2, xbuf, grad_ref, dubuf, qkv, mix, dmix, dqkv, watt, w1, w2, big, stage, pack, crecv, xa, yb, ya, xb, zr,
      sm, smr,
-     lsem, wsem, vs, vr, xs, xr, gs, gr, ms, mr, esem, osem, tsem) = refs
+     lsem, wsem, vs, vr, gs, gr, ms, mr, esem, osem, tsem) = refs
     me, x = lax.axis_index("expert"), lax.axis_index("shard")
     bits = owners.bit_length() - 1
     bit = [(me // (1 << i)) % 2 for i in range(bits)]
@@ -703,14 +939,15 @@
         p = xor(me, k, bits)
         return pltpu.make_async_remote_copy(served_h.at[p], sback_h.at[me], vs.at[k], vr.at[k], **to(p, x))
 
-    def send_rows():
-        return pltpu.make_async_remote_copy(uin_h, ux_h, xs.at[0], xr.at[0], **to(me, 1 - x))
-
-    send_rows().start()
     each(1, owners, lambda k: send_served(owners - k).start())
 
+    planes = owners // 4
+
     def add(ref, at, other):
-        ref[at] = (ref[at].astype(f32) + other.astype(f32)).astype(bf16)
+        ref[at] = ref[at] + other
+
+    def span(first, size):
+        return pl.ds(pl.multiple_of(first, 32), size)
 
     def stages(n):
         def copy(src, dst, i, peer):
@@ -720,64 +957,65 @@
         o = bit[0] * (whole // 2)
         out = []
         out.append((
-            lambda: [copy(pack.at[n, :, pl.ds((1 - bit[0]) * (whole // 2), whole // 2)], crecv.at[n], 0, to(hop[0], x))],
-            lambda: add(pack, (n, slice(None), pl.ds(o, whole // 2)), crecv[n])))
+            lambda: [copy(pack.at[n, :, span((1 - bit[0]) * (whole // 2), whole // 2)], crecv.at[n], 0, to(hop[0], x))],
+            lambda: add(pack, (n, slice(None), span(o, whole // 2)), crecv[n])))
         e = q // 2
         b1 = bit[1] * e
 
         def after1():
-            add(pack, (n, x, pl.ds(o, q)), xa[n])
-            add(pack, (n, slice(None), pl.ds(o + q + b1, e)), yb[n])
+            add(pack, (n, x, span(o, q)), xa[n])
+            add(pack, (n, slice(None), span(o + q + b1, e)), yb[n])
 
         out.append((
-            lambda: [copy(pack.at[n, 1 - x, pl.ds(o, q)], xa.at[n], 1, to(me, 1 - x)),
-                     copy(pack.at[n, :, pl.ds(o + q + e - b1, e)], yb.at[n], 2, to(hop[1], x))],
+            lambda: [copy(pack.at[n, 1 - x, span(o, q)], xa.at[n], 1, to(me, 1 - x)),
+                     copy(pack.at[n, :, span(o + q + e - b1, e)], yb.at[n], 2, to(hop[1], x))],
             after1))
 
         def after2():
-            add(pack, (n, x, pl.ds(o + b1, e)), ya[n])
-            add(pack, (n, x, pl.ds(o + q + b1, e)), xb[n])
+            add(pack, (n, x, span(o + b1, e)), ya[n])
+            add(pack, (n, x, span(o + q + b1, e)), xb[n])
 
         out.append((
-            lambda: [copy(pack.at[n, x, pl.ds(o + e - b1, e)], ya.at[n], 3, to(hop[1], x)),
-                     copy(pack.at[n, 1 - x, pl.ds(o + q + b1, e)], xb.at[n], 4, to(me, 1 - x))],
+            lambda: [copy(pack.at[n, x, span(o + e - b1, e)], ya.at[n], 3, to(hop[1], x)),
+                     copy(pack.at[n, 1 - x, span(o + q + b1, e)], xb.at[n], 4, to(me, 1 - x))],
             after2))
-        at, size, sem, starts = o + b1, e, 5, [(o, q), (o + b1, e)]
-        zoff = 0
-        for i in range(2, bits):
-            size //= 2
-            keep, give = at + bit[i] * size, at + (1 - bit[i]) * size
-
-            def go(give=give, size=size, sem=sem, i=i, zoff=zoff):
-                return [copy(pack.at[n, x, pl.ds(give + j * q, size)], zr.at[n, j, pl.ds(zoff, size)], sem + j, to(hop[i], x))
-                        for j in range(2)]
-
-            def after(keep=keep, size=size, zoff=zoff):
+        size = e // planes
+        base = o + b1
+
+        def rows_at(p):
+            return [span(base + p * size + j * q, size) for j in range(2)]
+
+        def over(make):
+            out = []
+            for k in range(1, planes):
+                p = xor(me // 4, k, bits)
                 for j in range(2):
-                    add(pack, (n, x, pl.ds(keep + j * q, size)), zr[n, j, zoff:zoff + size])
-
-            out.append((go, after))
-            at, sem, zoff = keep, sem + 2, zoff + size
-            starts.append((at, size))
-        last_go, last_after = out[-1]
-
-        def after_last(at=at, size=size):
-            last_after()
+                    out.append(make(k, p, j, 5 + 2 * (k - 1) + j, to(p * 4 + me % 4, x)))
+            return out
+
+        mine = me // 4
+
+        def after3():
             for j in range(2):
-                fin[n, pl.ds(at + j * q, size)] = pack[n, x, pl.ds(at + j * q, size)]
-
-        out[-1] = (last_go, after_last)
-        for i in reversed(range(1, bits)):
-            at, size = starts[i]
-
-            def go(at=at, size=size, sem=sem, i=i):
-                return [copy(fin.at[n, pl.ds(at + j * q, size)], fin.at[n, pl.ds(at + j * q, size)], sem + j, to(hop[i], x))
-                        for j in range(2)]
-
-            out.append((go, lambda: None))
-            sem += 2
-        out.append((lambda sem=sem: [copy(fin.at[n, pl.ds(o, whole // 2)], fin.at[n, pl.ds(o, whole // 2)], sem, to(hop[0], x))],
-                    lambda: None))
+                at = (n, x, rows_at(mine)[j])
+                total = pack[at].astype(f32)
+                for k in range(1, planes):
+                    total = total + zr[n, 2 * (k - 1) + j].astype(f32)
+                fin[(n, rows_at(mine)[j])] = total.astype(bf16)
+
+        out.append((
+            lambda: over(lambda k, p, j, i, peer: copy(pack.at[n, x, rows_at(p)[j]], zr.at[n, 2 * (k - 1) + j], i, peer)), after3))
+        more = 2 * (planes - 1)
+        out.append((
+            lambda: over(lambda k, p, j, i, peer: copy(fin.at[n, rows_at(mine)[j]], fin.at[n, rows_at(mine)[j]], i + more, peer)),
+            lambda: None))
+        out.append((
+            lambda: [copy(fin.at[n, span(base + j * q, e)], fin.at[n, span(base + j * q, e)], 5 + 2 * more + j, to(hop[1], x))
+                     for j in range(2)],
+            lambda: None))
+        out.append((
+            lambda: [copy(fin.at[n, span(o, whole // 2)], fin.at[n, span(o, whole // 2)], 7 + 2 * more, to(hop[0], x))],
+            lambda: None))
         return out
 
     groups = [stages(n) for n in range(4)]
@@ -810,15 +1048,12 @@
             if n == 3 and k < bits + 1:
                 small_stage(k).start()
 
-    done = [0] * 4
-
     def at_point(name, index=None):
-        for i, n in plan.get(name, ()):
+        for i, n, k in plan.get(name, ()):
             if index is None:
-                tick(n, done[n])
+                tick(n, k)
             else:
-                pl.when(index == i)(functools.partial(tick, n, done[n]))
-            done[n] += 1
+                pl.when(index == i)(functools.partial(tick, n, k))
 
     finish(start_in)
     grad_ref[...] = router_backward(experts, dy_ref, u_ref, probs_ref, hid2, gain_ref, router_ref, aux_ref, stat_ref, live_ref,
@@ -885,7 +1120,6 @@
 
     own.wait()
     each(1, owners, lambda k: send_served(k).wait())
-    send_rows().wait()
     at_point("rows")
 
     todo = [(uin_h, 0, 0), (ux_h, 0, 1), (dyin_h, 1, 0), (dyx_h.at[0], 1, 1)]
@@ -1009,86 +1243,95 @@
     split = Split(shards)
     expert_swap = functools.partial(lax.all_to_all, axis_name="expert", split_axis=0, concat_axis=0, tiled=True)
 
-    within = jnp.arange(step, dtype=jnp.int32) < seq
-    live = ((jnp.arange(images, dtype=jnp.int32)[:, None] < counts[0]) & within[None, :]).reshape(rows)
-    live = live.astype(f32)
-    routes_pad = jnp.pad(routes, ((0, 0), (0, step - seq), (0, 0)), constant_values=-1).reshape(rows, 2)
-    lanes = jnp.arange(LANES, dtype=jnp.int32)
-    loads = jnp.sum(((routes_pad[:, :, None] == lanes) & (live[:, None, None] > 0)).astype(f32), axis=(0, 1))
-    loads = jnp.where(lanes == LANES - 1, jnp.sum(live), loads)
-    live_col = live[:, None]
-
-    w_one = split.gather([attn_qkv1, attn_out1[None]])
-    w_up = split.gather([mlp_in[None]])
-    w_down = split.gather([mlp_out[None]])
-    w_two = split.gather([attn_qkv2, attn_out2[None]])
-    gains = jnp.concatenate([gains1, gains2])
+    block = (owners, block_rows, width)
+    sem = pltpu.SemaphoreType.DMA
     if shards == 2:
-        x = lax.axis_index("shard")
-        other = lax.ppermute(gains, "shard", [(0, 1), (1, 0)])
-        gains = jnp.where(x == 0, jnp.concatenate([gains, other], 1), jnp.concatenate([other, gains], 1))
-        other = lax.ppermute(router, "shard", [(0, 1), (1, 0)])
-        router_full = jnp.where(x == 0, jnp.concatenate([router, other]), jnp.concatenate([other, router]))
+        (gains, router_full, stat, live_col, dy, u_out, hidden, block_out, hidden_two, qkv_one, mix_one, qkv_two, mix_two, act, slope,
+         u_two, probs, back, w_one, w_up, w_down, w_two, dy_in) = fused_forward(
+            owners, experts, local, block, tokens, cotangent, routes, counts, jnp.concatenate([gains1, gains2]), router,
+            attn_qkv1, attn_out1, mlp_in, mlp_out, attn_qkv2, attn_out2)
+        w_one, w_up, w_down, w_two = [w_one], [w_up], [w_down], [w_two]
     else:
-        gains = lax.all_gather(gains, "shard", axis=1, tiled=True)
-        router_full = lax.all_gather(router, "shard", axis=0, tiled=True)
-    gains = gains.astype(f32)
-    router_full = jnp.pad(router_full, ((0, 0), (0, LANES - experts)))
-
-    dy, dy_out, disp, back = call(
-        functools.partial(route_body, images, seq, local, block_rows),
-        [sds((rows, width), bf16), sds((slots, width), bf16), sds((slots, rows), bf16), sds((rows, slots), bf16)],
-        [routes_pad, routes_pad.T, live_col, cotangent], flops=2e9, nbytes=6e6,
-    )
-    block = (owners, block_rows, width)
-    dy_in = expert_swap(dy_out.reshape(block))
-
-    sem = pltpu.SemaphoreType.DMA
-    attn_scratch = [pltpu.VMEM((4, width, width), bf16), sem((4,))]
-    mlp_scratch = [pltpu.VMEM((1, width, ff), bf16), pltpu.VMEM((1, ff, width), bf16), sem((2, 4))]
-
-    def specs(n, ins):
-        return [VM] * n + [ANY] * (len(ins) - n)
-
-    ins = [tokens, gains] + w_one
-    hidden, qkv_one, mix_one = call(
-        functools.partial(block1_body, split, images, seq),
-        [sds((rows, width), f32), sds((rows, 3 * width), bf16), sds((rows, width), bf16)],
-        ins, attn_scratch, specs(2, ins), flops=4e9, nbytes=8e6,
-    )
-    ins = [hidden, gains] + w_up + w_down
-    block_out, act, slope = call(
-        functools.partial(mlp_body, split),
-        [sds((rows, width), f32)] + [sds((ff // width, rows, width), bf16)] * 2,
-        ins, mlp_scratch, specs(2, ins), flops=6e9, nbytes=12e6,
-    )
-    ins = [block_out, gains, router_full, disp, live_col, loads[None, :]] + w_two
-    hidden_two, qkv_two, mix_two, u_two, probs, stat, u_out = call(
-        functools.partial(block2_body, split, images, seq, experts),
-        [sds((rows, width), f32), sds((rows, 3 * width), bf16), sds((rows, width), bf16), sds((rows, width), bf16),
-         sds((rows, LANES), f32), sds((8, LANES), f32), sds((slots, width), bf16)],
-        ins, attn_scratch, specs(6, ins), flops=5e9, nbytes=10e6,
-    )
+        within = jnp.arange(step, dtype=jnp.int32) < seq
+        live = ((jnp.arange(images, dtype=jnp.int32)[:, None] < counts[0]) & within[None, :]).reshape(rows)
+        live = live.astype(f32)
+        routes_pad = jnp.pad(routes, ((0, 0), (0, step - seq), (0, 0)), constant_values=-1).reshape(rows, 2)
+        lanes = jnp.arange(LANES, dtype=jnp.int32)
+        loads = jnp.sum(((routes_pad[:, :, None] == lanes) & (live[:, None, None] > 0)).astype(f32), axis=(0, 1))
+        loads = jnp.where(lanes == LANES - 1, jnp.sum(live), loads)
+        live_col = live[:, None]
+
+        w_one = split.gather([attn_qkv1, attn_out1[None]])
+        w_up = split.gather([mlp_in[None]])
+        w_down = split.gather([mlp_out[None]])
+        w_two = split.gather([attn_qkv2, attn_out2[None]])
+        gains = jnp.concatenate([gains1, gains2])
+        if shards == 2:
+            x = lax.axis_index("shard")
+            other = lax.ppermute(gains, "shard", [(0, 1), (1, 0)])
+            gains = jnp.where(x == 0, jnp.concatenate([gains, other], 1), jnp.concatenate([other, gains], 1))
+            other = lax.ppermute(router, "shard", [(0, 1), (1, 0)])
+            router_full = jnp.where(x == 0, jnp.concatenate([router, other]), jnp.concatenate([other, router]))
+        else:
+            gains = lax.all_gather(gains, "shard", axis=1, tiled=True)
+            router_full = lax.all_gather(router, "shard", axis=0, tiled=True)
+        gains = gains.astype(f32)
+        router_full = jnp.pad(router_full, ((0, 0), (0, LANES - experts)))
+
+        dy, dy_out, disp, back = call(
+            functools.partial(route_body, images, seq, local, block_rows),
+            [sds((rows, width), bf16), sds((slots, width), bf16), sds((slots, rows), bf16), sds((rows, slots), bf16)],
+            [routes_pad, routes_pad.T, live_col, cotangent], flops=2e9, nbytes=6e6,
+        )
+        block = (owners, block_rows, width)
+        dy_in = expert_swap(dy_out.reshape(block))
+
+        sem = pltpu.SemaphoreType.DMA
+        attn_scratch = [pltpu.VMEM((4, width, width), bf16), sem((4,))]
+        mlp_scratch = [pltpu.VMEM((1, width, ff), bf16), pltpu.VMEM((1, ff, width), bf16), sem((2, 4))]
+
+        def specs(n, ins):
+            return [VM] * n + [ANY] * (len(ins) - n)
+
+        ins = [tokens, gains] + w_one
+        hidden, qkv_one, mix_one = call(
+            functools.partial(block1_body, split, images, seq),
+            [sds((rows, width), f32), sds((rows, 3 * width), bf16), sds((rows, width), bf16)],
+            ins, attn_scratch, specs(2, ins), flops=4e9, nbytes=8e6,
+        )
+        ins = [hidden, gains] + w_up + w_down
+        block_out, act, slope = call(
+            functools.partial(mlp_body, split),
+            [sds((rows, width), f32)] + [sds((ff // width, rows, width), bf16)] * 2,
+            ins, mlp_scratch, specs(2, ins), flops=6e9, nbytes=12e6,
+        )
+        ins = [block_out, gains, router_full, disp, live_col, loads[None, :]] + w_two
+        hidden_two, qkv_two, mix_two, u_two, probs, stat, u_out = call(
+            functools.partial(block2_body, split, images, seq, experts),
+            [sds((rows, width), f32), sds((rows, 3 * width), bf16), sds((rows, width), bf16), sds((rows, width), bf16),
+             sds((rows, LANES), f32), sds((8, LANES), f32), sds((slots, width), bf16)],
+            ins, attn_scratch, specs(6, ins), flops=5e9, nbytes=10e6,
+        )
 
     group = min(4, owners)
-    u_in, served, du_back, dgate_back, stat, dy_far = pl.pallas_call(
+    u_in, served, du_back, dgate_back, stat, dy_far, u_far = pl.pallas_call(
         functools.partial(expert_body, owners, shards, local, experts, group),
         out_shape=[sds(block, bf16), sds(block, bf16), sds(block, bf16), sds((owners, 8, LANES), f32), sds((8, LANES), f32),
-                   sds((shards - 1,) + block, bf16)],
+                   sds((shards - 1,) + block, bf16), sds(block, bf16)],
         in_specs=[VM] * 4 + [ANY] * 2,
-        out_specs=[VM] * 6,
+        out_specs=[VM] * 5 + [ANY] * 2,
         scratch_shapes=[
             pltpu.VMEM((local, width, ff), bf16), pltpu.VMEM((local, ff, width), bf16), pltpu.VMEM(block, bf16),
             pltpu.VMEM((owners, 8, LANES), f32), pltpu.VMEM((shards, 8, LANES), f32), pltpu.VMEM((owners, 8, LANES), f32),
             sem((2,)), sem((2,)),
-        ] + [sem((owners,))] * 6 + [sem((shards,))] * 2 + [sem((owners,))] * 2 + [sem((shards,))] * 2,
+        ] + [sem((owners,))] * 10 + [sem((shards,))] * 4,
         compiler_params=pltpu.CompilerParams(vmem_limit_bytes=VMEM_BYTES, collective_id=0, has_side_effects=True),
         cost_estimate=pl.CostEstimate(flops=int(11e9), bytes_accessed=int(15e6), transcendentals=0),
     )(u_out.reshape(block), dy_in, router_full, stat, expert_in, expert_out)
     parts_of = (gains, router_full, aux_weight.reshape(1, 1), stat, live_col, back, dgate_back, tokens, dy, u_two, probs, du_back)
     if shards == 2:
-        return fused_backward(split, experts, tokens, parts_of, hidden_two, block_out, hidden, qkv_two, mix_two, qkv_one, mix_one,
-                              act, slope, served, u_in, dy_in, dy_far, expert_in, expert_out, w_two, w_up, w_down, w_one)
+        return fused_backward(Split(1), experts, tokens, parts_of, hidden_two, block_out, hidden, qkv_two, mix_two, qkv_one, mix_one,
+                              act, slope, served, u_in, u_far, dy_in, dy_far, expert_in, expert_out, w_two, w_up, w_down, w_one)
     served_back = expert_swap(served).reshape(slots, width)
 
     if shards == 2:
@@ -1166,24 +1409,25 @@
     )
 
 
-PLAN = {
-    "two": [(0, 0)],
-    "out": [(0, 0), (0, 1)],
-    "in0": [(0, 1)],
-    "in2": [(0, 0)],
-    "mlp": [(0, 2), (0, 1)],
-    "image": [(0, 2), (0, 0), (1, 1), (1, 2), (2, 0), (2, 1)],
-    "one": [(0, 3), (0, 0)],
-    "rows": [(0, 3), (0, 2), (0, 1)],
-    "output": [(0, 3), (0, 2), (0, 0)],
-    "early": [(0, 1), (1, 3), (1, 1), (2, 3), (2, 1), (3, 3), (4, 3), (5, 3)],
-    "late": [(0, 2), (0, 0), (1, 2), (1, 0), (2, 2), (2, 0), (3, 1), (3, 2), (4, 2)],
-    "end": [],
-}
+PLAN = [
+    ("two", None, 0),
+    ("out", None, 0), ("out", None, 1),
+    ("in1", None, 1),
+    ("mlp", None, 0), ("mlp", None, 2),
+    ("image", 0, 2), ("image", 0, 0), ("image", 0, 1), ("image", 1, 1), ("image", 2, 0),
+    ("one", None, 3), ("one", None, 2), ("one", None, 1),
+    ("rows", None, 3), ("rows", None, 0), ("rows", None, 2),
+    ("output", None, 1),
+    ("early", 0, 2), ("late", 0, 3), ("late", 0, 0),
+    ("early", 1, 1), ("late", 1, 3), ("late", 1, 2), ("late", 1, 0),
+    ("early", 2, 1), ("late", 2, 2),
+    ("early", 3, 3), ("early", 3, 2),
+    ("early", 4, 3), ("late", 5, 3), ("late", 6, 3),
+]
 
 
 def fused_backward(split, experts, tokens, parts_of, hidden_two, block_out, hidden, qkv_two, mix_two, qkv_one, mix_one,
-                   act, slope, served, u_in, dy_in, dy_far, expert_in, expert_out, w_two, w_up, w_down, w_one):
+                   act, slope, served, u_in, u_far, dy_in, dy_far, expert_in, expert_out, w_two, w_up, w_down, w_one):
     images, seq, width = tokens.shape
     rows = hidden.shape[0]
     local, _, ff = expert_in.shape
@@ -1193,33 +1437,31 @@
     whole = 2 * width
     part = width // 2
     blocks = ff // width
-    stages = 3 + (bits - 2) + (bits - 1) + 1
-    plan = {k: list(v) for k, v in PLAN.items()}
-    left = [stages + 1] * 4
-    for k in plan:
-        for item in list(plan[k]):
-            if left[item[1]] > 0:
-                left[item[1]] -= 1
-            else:
-                plan[k].remove(item)
-    plan["end"] = plan["end"] + [(0, n) for i in range(max(left)) for n in range(4) if left[n] > i]
+    stages = 7
+    left = [0] * 4
+    plan = {}
+    for name, index, n in PLAN:
+        if left[n] <= stages and (index is None or index < (images if name == "image" else local * blocks)):
+            plan.setdefault(name, []).append((index, n, left[n]))
+            left[n] += 1
+    plan["end"] = [(None, n, k) for k in range(stages + 1) for n in range(4) if k >= left[n]]
     small_rows = -(-(experts + 4) // 8) * 8
     sem = pltpu.SemaphoreType.DMA
-    ins = list(parts_of) + [hidden_two, block_out, hidden, qkv_two, mix_two, qkv_one, mix_one, act, slope, served, u_in, dy_in,
+    ins = list(parts_of) + [hidden_two, block_out, hidden, qkv_two, mix_two, qkv_one, mix_one, act, slope, served, u_in, u_far, dy_in,
                             dy_far, expert_in, expert_out] + w_two + w_up + w_down + w_one
     vmem = 8
     big_rows = 2 * owners * CAP
-    nsem = 5 + 4 * (bits - 2) + 3
+    nsem = 8 + 4 * (owners // 4 - 1)
     V = pltpu.VMEM
     outs = pl.pallas_call(
         functools.partial(backward_body, split, images, seq, experts, local, owners, plan),
         out_shape=[
             sds((images, seq, width), bf16), sds((images, seq, width), f32), sds((4, whole, width), bf16),
             sds((small_rows, part), f32), sds((LANES + 8, width), f32), sds(expert_in.shape, bf16), sds(expert_out.shape, bf16),
-            sds(block, bf16), sds(block, bf16),
+            sds(block, bf16),
         ],
         in_specs=[VM] * vmem + [ANY] * (len(ins) - vmem),
-        out_specs=[VM] * 5 + [ANY] * 4,
+        out_specs=[VM] * 5 + [ANY] * 3,
         scratch_shapes=[
             V((rows, width), f32), V((rows, width), f32), V((rows, width), f32), V((rows, width), f32),
             V((rows, 3 * width), bf16), V((rows, width), bf16), V((rows, width), bf16), V((rows, 3 * width), bf16),
@@ -1227,31 +1469,62 @@
             V((2,) + block, bf16),
             V((4, 2, whole, width), bf16), V((4, 2, whole // 2, width), bf16), V((4, whole // 4, width), bf16),
             V((4, 2, whole // 8, width), bf16), V((4, whole // 8, width), bf16), V((4, whole // 8, width), bf16),
-            V((4, 2, whole // 8 - whole // (1 << (bits + 1)), width), bf16),
+            V((4, 2 * (owners // 4 - 1), whole // (2 * owners), width), bf16),
             V((2, small_rows, part), f32), V((bits + 1, 2, small_rows, part), f32),
-            sem((8 + 2 * blocks,)), sem((3, 4)), sem((owners,)), sem((owners,)), sem((1,)), sem((1,)),
+            sem((8 + 2 * blocks,)), sem((3, 4)), sem((owners,)), sem((owners,)),
             sem((4, nsem)), sem((4, nsem)), sem((bits + 1,)), sem((bits + 1,)), sem((6,)), sem((4,)), sem((1,)),
         ],
         compiler_params=pltpu.CompilerParams(vmem_limit_bytes=63 << 20, collective_id=1, has_side_effects=True),
         cost_estimate=pl.CostEstimate(flops=int(60e9), bytes_accessed=int(80e6), transcendentals=0),
     )(*ins)
     output, grad_tokens, fin, tail, small, grad_e_in, grad_e_out = outs[:7]
+    qkv1, out1, up, down, qkv2, out2, grad_e_in, grad_e_out = widen(fin, grad_e_in, grad_e_out, part, width, blocks)
     return (
-        output,
-        small[LANES + 2, 0],
-        grad_tokens,
-        fin[3, :3 * part].astype(f32).reshape(3, part, width),
-        fin[3, 3 * part:].astype(f32),
-        fin[2].astype(f32).reshape(blocks, part, width).transpose(1, 0, 2).reshape(part, ff),
-        fin[1].astype(f32),
-        tail[experts:experts + 2],
-        fin[0, :3 * part].astype(f32).reshape(3, part, width),
-        fin[0, 3 * part:].astype(f32),
-        tail[:experts].T,
-        tail[experts + 2:experts + 4],
-        grad_e_in.astype(f32),
-        grad_e_out.astype(f32),
+        output, small[LANES + 2, 0], grad_tokens, qkv1, out1, up, down, tail[experts:experts + 2], qkv2, out2, tail[:experts].T,
+        tail[experts + 2:experts + 4], grad_e_in, grad_e_out,
     )
+
+
+def widen_body(sixth, fin_ref, e1_ref, e2_ref, qkv1_ref, out1_ref, up_ref, down_ref, qkv2_ref, out2_ref, g1_ref, g2_ref):
+    i = pl.program_id(0)
+    g1_ref[...] = e1_ref[...].astype(f32)
+    g2_ref[...] = e2_ref[...].astype(f32)
+    up_ref[...] = fin_ref[2].astype(f32)
+    down_ref[...] = fin_ref[1].astype(f32)
+
+    @pl.when(i < sixth)
+    def _():
+        qkv1_ref[0] = fin_ref[3].astype(f32)
+        qkv2_ref[0] = fin_ref[0].astype(f32)
+
+    @pl.when(i >= sixth)
+    def _():
+        out1_ref[...] = fin_ref[3].astype(f32)
+        out2_ref[...] = fin_ref[0].astype(f32)
+
+
+def widen(fin, e1, e2, part, width, blocks):
+    steps = 2 * blocks
+    some = fin.shape[1] // steps
+    per = part // some
+    sixth = 3 * per
+    local, _, ff = e1.shape
+    qkv = pl.BlockSpec((1, some, width), lambda i: (jnp.minimum(i, sixth - 1) // per, jnp.minimum(i, sixth - 1) % per, 0))
+    out = pl.BlockSpec((some, width), lambda i: (jnp.maximum(i - sixth, 0), 0))
+    return pl.pallas_call(
+        functools.partial(widen_body, sixth),
+        grid=(steps,),
+        out_shape=[sds((3, part, width), f32), sds((part, width), f32), sds((part, blocks * width), f32), sds((fin.shape[1], width), f32),
+                   sds((3, part, width), f32), sds((part, width), f32), sds(e1.shape, f32), sds(e2.shape, f32)],
+        in_specs=[pl.BlockSpec((4, some, width), lambda i: (0, i, 0)),
+                  pl.BlockSpec((local, width // steps, ff), lambda i: (0, i, 0)),
+                  pl.BlockSpec((local, ff // steps, width), lambda i: (0, i, 0))],
+        out_specs=[qkv, out, pl.BlockSpec((some, width), lambda i: (i % per, i // per)), pl.BlockSpec((some, width), lambda i: (i, 0)),
+                   qkv, out, pl.BlockSpec((local, width // steps, ff), lambda i: (0, i, 0)),
+                   pl.BlockSpec((local, ff // steps, width), lambda i: (0, i, 0))],
+        compiler_params=pltpu.CompilerParams(vmem_limit_bytes=VMEM_BYTES),
+        cost_estimate=pl.CostEstimate(flops=0, bytes_accessed=int(40e6), transcendentals=0),
+    )(fin, e1, e2)
 
 
 def solution(mesh):

time: 329 us -> 302 us (0.918)
  Pallas kernels: 246 us -> 283 us
  waiting for transfers between devices: 22 us -> 0 us
  other arithmetic: 19.8 us -> 1.31 us
  starting transfers between devices: 14.5 us -> 0 us
  local copies, waits for them, and re-layouts: 19.7 us -> 9.62 us
    pallas_call x4 -> x2, Pallas kernels: 40.9 us -> 85.1 us  [the longest x1 71.1 us: fused_forward(): pl.pallas_call(functools.partial(forward_body, images, seq, experts, loca...]
    ppermute x10 -> x0, waiting for transfers between devices: 22 us -> none  [the longest x4 14.5 us: gather(): far = lax.ppermute(send, 'shard', [(0, 1), (1, 0)])]
    convert_element_type x7 -> x1, other arithmetic: 16.3 us -> 1.31 us  [fused_forward(): gains = jnp.pad(gains, ((0, 4), (0, 0))).astype(f32)]
    pallas_call x1, Pallas kernels: 138 us -> 130 us  [fused_backward(): pl.pallas_call(functools.partial(backward_body, split, images, seq, exper...]
    ppermute x10 -> x0, starting transfers between devices: 7.4 us -> none  [the longest x4 3.74 us: gather(): far = lax.ppermute(send, 'shard', [(0, 1), (1, 0)])]
    all_to_all x1 -> x0, starting transfers between devices: 7.12 us -> none  [per_device(): dy_in = expert_swap(dy_out.reshape(block))]
    unnamed x41 -> x10, local copies, waits for them, and re-layouts: 6.83 us -> 4.06 us
  transfers between devices with their start and end apart: 11 -> 0, of which waited for: 2 -> 0; matrix products, arithmetic and copies ran while one was open for 3% -> 0% of each run, Pallas kernels for 13% -> 0%
where the time goes in v3:
time: 302 us; the launch traced here: 296 us
  Pallas kernels  283 us (94%)
  local copies, waits for them, and re-layouts  9.62 us (3%)
    pallas_call x1, Pallas kernels, fused_backward(): pl.pallas_call(functools.partial(backward_body, split, images, seq, exper...  130 us
    pallas_call x1, Pallas kernels, fused_forward(): pl.pallas_call(functools.partial(forward_body, images, seq, experts, loca...  71.1 us
    pallas_call x1, Pallas kernels, per_device(): pl.pallas_call(functools.partial(expert_body, owners, shards, local, expe...  68.3 us
    pallas_call x1, Pallas kernels, widen(): pl.pallas_call(functools.partial(widen_body, sixth), grid=(steps,), out_s...  14 us

profile of v3, /device:TPU:0, one launch (start us, length us, event | category | flops | bytes accessed | tf_op | source)
XLA Modules:
  0.0 296.3 jit_solution(3750825688336127805)
XLA Ops:
  1.9 0.7 copy.36
  2.6 0.1 reshape.34
  2.7 0.0 copy-start.2
  2.7 1.3 fusion.3.refs_5_
  4.0 0.8 copy.34
  4.9 0.7 pad.14.refs_6_
  5.5 0.9 copy.35.refs_0_
  6.4 0.0 copy-done.2
  6.4 71.1 %shard_map.263 = (f32[8,512]{1,0:T(8,128)}, bf16[512,128]{1,0:T(8,128)(2,1)}, f32[8,128]{1,0:T(8,128)}, f32[624,1]{1,0:T(8,128)}, bf16[624,512]{1,0:T(8,128)(2,1...) custom-call(s32[624,2]{1,0:T(8,128)} %copy.35.refs_0_, ...), custom_call_target="tpu_custom_call" | custom-call | flops 17999998976 | bytes 60000000 | tf_op jit(solution)/shard_map/pallas_call | solution.py:539
  77.6 68.3 %shard_map.264 = (bf16[16,80,512]{2,1,0:T(8,128)(2,1)}, bf16[16,80,512]{2,1,0:T(8,128)(2,1)}, bf16[16,80,512]{2,1,0:T(8,128)(2,1)}, f32[16,8,128]{2,1,0:T(8,128)...) custom-call(bf16[16,80,512]{2,1,0:T(8,128)(2,1)} %get-tuple-element.61.uout_ref, ...), custom_call_target="tpu_custom_call" | custom-call | flops 11000000512 | bytes 15000000 | tf_op jit(solution)/shard_map/pallas_call | solution.py:1317
  145.9 129.6 %shard_map.265 = (bf16[3,197,512]{2,1,0:T(8,128)(2,1)}, f32[3,197,512]{2,1,0:T(8,128)}, bf16[4,1024,512]{2,1,0:T(8,128)(2,1)}, f32[40,256]{1,0:T(8,128)}, f32[13...) custom-call(f32[8,512]{1,0:T(8,128)} %get-tuple-element.59.refs_0_, ...), custom_call_target="tpu_custom_call" | custom-call | flops 60000002048 | bytes 80000000 | tf_op jit(solution)/shard_map/pallas_call | solution.py:1456
  275.5 1.2 slice.12
  276.7 1.4 fusion.4
  278.0 1.4 slice_bitcast_fusion
  279.4 0.0 copy-start.1
  279.4 14.0 %shard_map.266 = (f32[3,256,512]{2,1,0:T(8,128)}, f32[256,512]{1,0:T(8,128)}, f32[256,2048]{1,0:T(8,128)}, f32[1024,512]{1,0:T(8,128)}, f32[3,256,512]{2,1,0:T(8...) custom-call(bf16[4,1024,512]{2,1,0:T(8,128)(2,1)} %get-tuple-element.92.fin_ref, ...), custom_call_target="tpu_custom_call" | custom-call | bytes 40000000 | tf_op jit(solution)/shard_map/pallas_call | solution.py:1514
  293.3 0.0 copy-start
  293.4 0.0 copy-done.1
  293.4 0.8 copy.41
  294.2 0.7 copy-done
  294.9 1.0 copy.42
  (1 shorter events, 0.0 us)
Async XLA Ops:
  2.7 3.7 %copy-start.2 = (s32[624,2]{0,1:T(2,128)}, s32[624,2]{0,1:T(2,128)S(1)}, u32[]{:S(2)}) copy-start(s32[624,2]{0,1:T(2,128)S(1)} %reshape.34) | copy-start | bytes 14980
  279.4 14.0 %copy-start.1 = (bf16[3,197,512]{2,1,0:T(8,128)(2,1)S(1)}, bf16[3,197,512]{2,1,0:T(8,128)(2,1)}, u32[]{:S(2)}) copy-start(bf16[3,197,512]{2,1,0:T(8,128)(2,1)} %get-tuple-element.120) | copy-start | bytes 1815556
  293.3 1.5 copy-start
